TPU v7x, 512 devices: a whole 4x8x8 slice. The times are simulated.
512 devices in a mesh: gx: 16 (over y, core), gy: 8 (over z), gz: 4 (over x).
Axes of the slice: x: 4, y: 8, z: 8, core: 2. Of those that a mesh axis runs over, the one named last changes fastest.
Arguments:
- parcel_vel: float32 [65536, 3, 128], P(('gx', 'gy', 'gz')), may hold values from -6 to 6
- parcel_props: float32 [65536, 2, 128], P(('gx', 'gy', 'gz')), may hold values from 0.05 to 2
- fill_count: int32 [65536], P(('gx', 'gy', 'gz')), may hold values from 64 to 128
- owner_peer: int32 [65536, 1], P(('gx', 'gy', 'gz')), may hold values from 0 to 127; in each aligned block of 128 rows (0 to 127, 128 to 255, ...) at most 2 rows name the same one
- cell_offset: int32 [65536], P(('gx', 'gy', 'gz')), may hold values from 0 to 36124
- shell_weight: float32 [128, 128], replicated, may hold values from 0 to 0.015625
- gas_state: float32 [4, 256, 128, 512], P(None, 'gx', 'gy', 'gz'), may hold values from -6 to 6
Outputs:
- parcels_next: float32 [131072, 5, 128], P(('gx', 'gy', 'gz'))
- gas_next: float32 [4, 256, 128, 512], P(None, 'gx', 'gy', 'gz')
Inputs may be any that keep to these rules, and one draw needn't show every extreme that they name: `owner_peer`: among the 128 blocks of one device no owner is named more than 2 times, a bound that some block reaches.
All inputs are finite; a program needn't handle non-finite values.
Results may differ from a plain program's by a relative error of at most 0.000068.
Values sent between devices are 32-bit elements; how exact they have to be, the bound alone decides.
No kernel may reach another device: no remote copies, remote signals or barrier semaphores. Data moves between devices by JAX's collectives and lax.ppermute only.
A program may use at most 128 MiB of HBM per device.

v0:
```python
import functools
import jax
import jax.numpy as jnp
from jax import lax
from jax.experimental import pallas as pl
from jax.experimental.pallas import tpu as pltpu
from jax.sharding import PartitionSpec as P

TIME_STEP = 0.05
SETTLING = 1.0
F32 = jnp.float32
BF16 = jnp.bfloat16
HI = lax.Precision.HIGHEST

LANES = 128
ROWS = 11
ZR = 144
ZO = 8
YS = 32


def iota(shape, dim):
    return lax.broadcasted_iota(jnp.int32, shape, dim)


def pack_kernel(tgt_ref, off_ref, cnt_ref, vel_ref, prop_ref, out_ref):
    n = LANES
    hot = (iota((n, n), 0) == tgt_ref[...]).astype(F32)
    earlier = (iota((n, n), 0) < iota((n, n), 1)).astype(BF16)
    rank = jnp.dot(hot.astype(BF16), earlier, preferred_element_type=F32)
    first = jnp.where(rank < 0.5, hot, 0.0)
    second = jnp.where(rank > 0.5, hot, 0.0)
    off = off_ref[...].astype(F32)
    cnt = cnt_ref[...].astype(F32)
    lane = iota((n, n), 1)
    head = jnp.zeros((n, n), F32)
    for place, (pick, val) in enumerate(((first, off), (second, off), (first, cnt), (second, cnt))):
        column = jnp.sum(pick * val, axis=1, keepdims=True)
        head = jnp.where(lane == place, column, head)
    out_ref[pl.ds(10, n, stride=ROWS), :] = head
    picks = jnp.concatenate([first, second], axis=0).astype(BF16)
    for k in range(5):
        x = vel_ref[:, k, :] if k < 3 else prop_ref[:, k - 3, :]
        total = jnp.zeros((2 * n, n), F32)
        for _ in range(3):
            part = x.astype(BF16)
            x = x - part.astype(F32)
            total = total + jnp.dot(picks, part, preferred_element_type=F32)
        out_ref[pl.ds(k, n, stride=ROWS), :] = total[:n]
        out_ref[pl.ds(5 + k, n, stride=ROWS), :] = total[n:]


def turn_kernel(gas_ref, low_ref, high_ref, out_ref, buf):
    cells_x, cells_y = gas_ref.shape[1], gas_ref.shape[2]
    buf[...] = jnp.zeros_like(buf)
    for x in range(cells_x):
        for k in range(4):
            buf[x, k * YS : k * YS + 2, :] = low_ref[k, x]
            buf[x, k * YS + 2 : k * YS + 2 + cells_y, :] = gas_ref[k, x]
            buf[x, k * YS + 2 + cells_y : k * YS + 4 + cells_y, :] = high_ref[k, x]
    for x in range(cells_x):
        out_ref[x] = buf[x].T


def base_kernel(mid_ref, zl_ref, zh_ref, xl_ref, xh_ref, pad_ref, base_ref):
    cells_x, cells_z = mid_ref.shape[0], mid_ref.shape[1]
    last = ZO + cells_z
    pad_ref[0:2] = xl_ref[...]
    pad_ref[cells_x + 2 : cells_x + 4] = xh_ref[...]
    pad_ref[2 : cells_x + 2, ZO:last, :] = mid_ref[...]
    pad_ref[2 : cells_x + 2, ZO - 2 : ZO, :] = zl_ref[...]
    pad_ref[2 : cells_x + 2, last : last + 2, :] = zh_ref[...]
    lane = iota((cells_z, LANES), 1)
    inside = (lane % YS >= 2) & (lane % YS < 18)
    rate = jnp.where(lane < 3 * YS, TIME_STEP, 0.5 * TIME_STEP).astype(F32)
    base_ref[0:2] = jnp.zeros((2, ZR, LANES), F32)
    base_ref[cells_x + 2 : cells_x + 4] = jnp.zeros((2, ZR, LANES), F32)

    @pl.loop(2, cells_x + 2)
    def _(x):
        here = pad_ref[x, ZO:last, :]
        beside = pad_ref[x + 1, ZO:last, :] + pad_ref[x - 1, ZO:last, :]
        beside = beside + pltpu.roll(here, LANES - 1, 1) + pltpu.roll(here, 1, 1)
        beside = beside + pad_ref[x, ZO + 1 : last + 1, :] + pad_ref[x, ZO - 1 : last - 1, :]
        value = here + rate * (beside - 6.0 * here)
        base_ref[x, 0:ZO, :] = jnp.zeros((ZO, LANES), F32)
        base_ref[x, ZO:last, :] = jnp.where(inside, value, 0.0)
        base_ref[x, last:ZR, :] = jnp.zeros((ZR - last, LANES), F32)


def parcel_kernel(
    recv_ref, pad_ref, base_ref, wt_ref, w_ref, pay_ref, sum_ref, xlo_ref, xhi_ref, code_v, code_s, acc, sem
):
    planes = pad_ref.shape[0] // ZR
    n = LANES
    off = recv_ref[pl.ds(10, n, stride=ROWS), :]
    rest = jnp.floor((off + 0.5) * (1.0 / 125.0))
    oz = off - rest * 125.0
    ox = jnp.floor((rest + 0.5) * (1.0 / 17.0))
    oy = rest - ox * 17.0
    code = oy * 4096.0 + ox * float(ZR) + oz + float(ZO - 2)
    code_v[...] = code.T[0:8].astype(jnp.int32)
    copy = pltpu.make_async_copy(code_v, code_s, sem)
    copy.start()
    acc[...] = base_ref[...]
    copy.wait()

    lane8 = iota((8, n), 1)
    group = (lane8 % YS) // 4
    quad = lane8 % 4
    lane = iota((YS, n), 1)

    @pl.loop(0, 8)
    def _(s):
        rank = s // 4
        q0 = (s % 4) * YS

        def place(b):
            c = code_s[rank, q0 + b]
            return jnp.bitwise_and(c, 4095), lax.shift_right_logical(c, 12)

        merged = []
        for g in range(4):
            total = [None] * 4
            for b8 in range(8):
                at, oy_b = place(b8 * 4 + g)
                shift = jnp.bitwise_and(4 * b8 - oy_b, n - 1)
                mine = group == b8
                for a in range(4):
                    x = pltpu.roll(pad_ref[pl.ds(at + a * ZR, 8), :], shift, 1)
                    total[a] = jnp.where(mine, x, 0.0 if total[a] is None else total[a])
            merged.append(total)
        cells = []
        for e in range(4):
            for a in range(4):
                x = merged[0][a]
                out = pltpu.roll(x, -e % n, 1) if e else x
                for g in range(1, 4):
                    x = merged[g][a]
                    x = pltpu.roll(x, (g - e) % n, 1) if g != e else x
                    out = jnp.where(quad == g, x, out)
                cells.append(out)
        near = jnp.concatenate(cells, axis=0).T
        gas_at = jnp.dot(near, wt_ref[...], precision=HI, preferred_element_type=F32)

        row = q0 * ROWS + rank * 5

        def take(k):
            return recv_ref[pl.ds(row + k, YS, stride=ROWS), :]

        head = recv_ref[pl.ds(q0 * ROWS + 10, YS, stride=ROWS), :]
        count = jnp.where(rank == 0, head[:, 2:3], head[:, 3:4])
        alive = lane.astype(F32) < count
        mass = jnp.where(alive, take(3), 0.0)
        relax = jnp.where(alive, take(4), 1.0)
        drag = TIME_STEP / relax
        forces = []
        for k in range(3):
            gas = gas_at[k * YS : (k + 1) * YS]
            settle = TIME_STEP * SETTLING if k == 2 else 0.0
            vel = (take(k) + drag * gas - settle) / (1.0 + drag)
            forces.append(-(mass * drag * (gas - vel)))
            pay_ref[k, rank, pl.ds(q0, YS), :] = jnp.where(alive, vel, 0.0)
        pay_ref[3, rank, pl.ds(q0, YS), :] = mass
        pay_ref[4, rank, pl.ds(q0, YS), :] = jnp.where(alive, relax, 0.0)
        forces.append(mass)
        force = jnp.concatenate(forces, axis=0)
        spread = lax.dot_general(
            w_ref[...], force, (((1,), (1,)), ((), ())), precision=HI, preferred_element_type=F32
        )
        for g in range(4):
            parts = []
            for a in range(4):
                out = None
                for e in range(4):
                    x = spread[(e * 4 + a) * 8 : (e * 4 + a) * 8 + 8]
                    x = pltpu.roll(x, (e - g) % n, 1) if e != g else x
                    out = x if out is None else jnp.where(quad == e, x, out)
                parts.append(out)
            for b8 in range(8):
                at, oy_b = place(b8 * 4 + g)
                shift = jnp.bitwise_and(oy_b - 4 * b8, n - 1)
                mine = group == b8
                for a in range(4):
                    x = pltpu.roll(jnp.where(mine, parts[a], 0.0), shift, 1)
                    acc[pl.ds(at + a * ZR, 8), :] = acc[pl.ds(at + a * ZR, 8), :] + x

    sum_ref[...] = acc[2 * ZR : (planes - 2) * ZR, :]
    xlo_ref[...] = acc[0 : 2 * ZR, :]
    xhi_ref[...] = acc[(planes - 2) * ZR :, :]


def back_kernel(sum_ref, xl_ref, xh_ref, zl_ref, zh_ref, out_ref, ylo_ref, yhi_ref, buf):
    cells_x = sum_ref.shape[0]
    cells_z = out_ref.shape[3]
    cells_y = out_ref.shape[2]
    for x in range(cells_x):
        value = sum_ref[x, ZO : ZO + cells_z, :]
        if x < 2:
            value = value + xl_ref[x, ZO : ZO + cells_z, :]
        if x >= cells_x - 2:
            value = value + xh_ref[x - cells_x + 2, ZO : ZO + cells_z, :]
        buf[x] = value
    buf[:, 0:2, :] += zl_ref[...]
    buf[:, cells_z - 2 : cells_z, :] += zh_ref[...]
    for x in range(cells_x):
        flat = buf[x].T
        for k in range(4):
            out_ref[k, x] = flat[k * YS + 2 : k * YS + 2 + cells_y]
            ylo_ref[k, x] = flat[k * YS : k * YS + 2]
            yhi_ref[k, x] = flat[k * YS + 2 + cells_y : k * YS + 4 + cells_y]


def shift_pair(to_low, to_high, axis):
    count = lax.axis_size(axis)
    up = [(i, i + 1) for i in range(count - 1)]
    down = [(j, i) for i, j in up]
    return lax.ppermute(to_high, axis, up), lax.ppermute(to_low, axis, down)


def call(kernel, outs, scratch=(), cost=None, **kw):
    return pl.pallas_call(
        kernel,
        out_shape=outs,
        scratch_shapes=list(scratch),
        compiler_params=pltpu.CompilerParams(vmem_limit_bytes=40 * 2**20),
        cost_estimate=cost,
        **kw,
    )


def arr(*shape, dtype=F32):
    return jax.ShapeDtypeStruct(shape, dtype)


def per_device(parcel_vel, parcel_props, fill_count, owner_peer, cell_offset, shell_weight, gas_state):
    _, nx, ny, nz = gas_state.shape
    blocks = parcel_vel.shape[0]
    send = call(pack_kernel, arr(blocks * ROWS, LANES))(
        owner_peer.reshape(1, blocks),
        cell_offset.reshape(1, blocks),
        fill_count.reshape(1, blocks),
        parcel_vel,
        parcel_props,
    )
    recv = lax.all_to_all(
        send.reshape(blocks, ROWS * LANES), ("gx", "gy"), split_axis=0, concat_axis=0, tiled=True
    ).reshape(blocks * ROWS, LANES)

    y_low, y_high = shift_pair(gas_state[:, :, :2], gas_state[:, :, ny - 2 :], "gy")
    mid = call(turn_kernel, arr(nx, nz, LANES), [pltpu.VMEM((nx, LANES, nz), F32)])(gas_state, y_low, y_high)
    z_low, z_high = shift_pair(mid[:, :2], mid[:, nz - 2 :], "gz")

    def face(lo, hi):
        zero = jnp.zeros((2, ZO - 2, LANES), F32)
        return jnp.concatenate([zero, z_low[lo:hi], mid[lo:hi], z_high[lo:hi], zero], axis=1)

    x_low, x_high = shift_pair(face(0, 2), face(nx - 2, nx), "gx")
    padded, base = call(base_kernel, [arr(nx + 4, ZR, LANES)] * 2)(mid, z_low, z_high, x_low, x_high)

    weight = shell_weight.reshape(LANES, 4, 4, 8).transpose(2, 1, 3, 0).reshape(LANES, LANES)
    rows = (nx + 4) * ZR
    pay, total, x_lo, x_hi = call(
        parcel_kernel,
        [arr(5, 2, blocks, LANES), arr(nx * ZR, LANES), arr(2 * ZR, LANES), arr(2 * ZR, LANES)],
        [
            pltpu.VMEM((8, LANES), jnp.int32),
            pltpu.SMEM((8, LANES), jnp.int32),
            pltpu.VMEM((rows, LANES), F32),
            pltpu.SemaphoreType.DMA,
        ],
    )(recv, padded.reshape(rows, LANES), base.reshape(rows, LANES), weight, weight)
    parcels_next = pay.transpose(2, 1, 0, 3).reshape(2 * blocks, 5, LANES)

    from_low, from_high = shift_pair(x_lo.reshape(2, ZR, LANES), x_hi.reshape(2, ZR, LANES), "gx")
    total = total.reshape(nx, ZR, LANES)

    def rim(lo, hi):
        part = total[:, lo:hi]
        return jnp.concatenate(
            [part[:2] + from_low[:, lo:hi], part[2 : nx - 2], part[nx - 2 :] + from_high[:, lo:hi]], axis=0
        )

    z_below, z_above = shift_pair(rim(ZO - 2, ZO), rim(ZO + nz, ZO + nz + 2), "gz")
    rows_out, y_lo, y_hi = call(
        back_kernel,
        [arr(4, nx, ny, nz), arr(4, nx, 2, nz), arr(4, nx, 2, nz)],
        [pltpu.VMEM((nx, nz, LANES), F32)],
    )(total, from_low, from_high, z_below, z_above)
    y_below, y_above = shift_pair(y_lo, y_hi, "gy")
    gas_next = jnp.concatenate(
        [rows_out[:, :, :2] + y_below, rows_out[:, :, 2 : ny - 2], rows_out[:, :, ny - 2 :] + y_above], axis=2
    )
    return parcels_next, gas_next


def solution(mesh):
    return jax.shard_map(
        per_device,
        mesh=mesh,
        in_specs=(
            P(("gx", "gy", "gz"), None, None),
            P(("gx", "gy", "gz"), None, None),
            P(("gx", "gy", "gz")),
            P(("gx", "gy", "gz"), None),
            P(("gx", "gy", "gz")),
            P(),
            P(None, "gx", "gy", "gz"),
        ),
        out_specs=(P(("gx", "gy", "gz"), None, None), P(None, "gx", "gy", "gz")),
        check_vma=False,
    )
```

profile of v0, /device:TPU:91, one launch (start us, length us, event | category | flops | bytes accessed | tf_op | source)
XLA Modules:
  0.0 108.5 jit_solution(13600145241550416250)
XLA Ops:
  4.6 2.5 %shard_map.86 = f32[1408,128]{1,0:T(8,128)} custom-call(s32[1,128]{1,0:T(1,128)S(1)} %bitcast.25, s32[1,128]{1,0:T(1,128)S(1)} %bitcast.26, s32[1,128]{1,0:T(1,128)S(1)} %bitcast.27, f32[128,3,128]{2,1,0:T(4,128)S(1)} %copy.15.vel_ref, f32[128,2,128]{2,1,0:T(2,128)S(1)} %copy-done.5), custom_call_target="tpu_custom_call" | custom-call | tf_op jit(solution)/shard_map/pallas_call | solution.py:239
  7.1 16.8 %all-to-all-start = ((f32[128,1,1408]{2,1,0:T(1,128)}), f32[128,1,1408]{2,1,0:T(1,128)S(1)}, u32[]{:S(2)}, u32[]{:S(2)}) async-start(f32[128,1,1408]{2,1,0:T(1,128)} %bitcast.3), calls=%async_computation | async-start | bytes 1441792 | tf_op jit(solution)/shard_map/all_to_all | solution.py:246
  24.0 2.2 %collective-permute-start.1 = (f32[4,16,2,128]{3,2,1,0:T(2,128)S(1)}, f32[4,16,2,128]{3,2,1,0:T(2,128)S(1)}, u32[]{:S(2)}, u32[]{:S(2)}) collective-permute-start(f32[4,16,2,128]{3,2,1,0:T(2,128)S(1)} %get-tuple-element.34), channel_id=1, source_target_pairs={{4,0},{8,4},{12,8},{16,12},{20,16},{24,20},{28,24},{5,1},{9,5},{13... | collective-permute-start | bytes 196616 | tf_op jit(solution)/shard_map/ppermute | solution.py:218
  26.2 3.2 %collective-permute-start = (f32[4,16,2,128]{3,2,1,0:T(2,128)S(1)}, f32[4,16,2,128]{3,2,1,0:T(2,128)S(1)}, u32[]{:S(2)}, u32[]{:S(2)}) collective-permute-start(f32[4,16,2,128]{3,2,1,0:T(2,128)S(1)} %get-tuple-element.35), channel_id=1, source_target_pairs={{0,4},{4,8},{8,12},{12,16},{16,20},{20,24},{24,28},{1,5},{5,9},{9,... | collective-permute-start | bytes 196616 | tf_op jit(solution)/shard_map/ppermute | solution.py:218
  29.4 6.5 %collective-permute-done.1.high_ref = f32[4,16,2,128]{3,2,1,0:T(2,128)S(1)} collective-permute-done((f32[4,16,2,128]{3,2,1,0:T(2,128)S(1)}, f32[4,16,2,128]{3,2,1,0:T(2,128)S(1)}, u32[]{:S(2)}, u32[]{:S(2)}) %collective-permute-start.1) | collective-permute-done | bytes 65568 | tf_op jit(solution)/shard_map/ppermute | solution.py:218
  35.9 4.0 %collective-permute-done.low_ref = f32[4,16,2,128]{3,2,1,0:T(2,128)S(1)} collective-permute-done((f32[4,16,2,128]{3,2,1,0:T(2,128)S(1)}, f32[4,16,2,128]{3,2,1,0:T(2,128)S(1)}, u32[]{:S(2)}, u32[]{:S(2)}) %collective-permute-start) | collective-permute-done | bytes 65568 | tf_op jit(solution)/shard_map/ppermute | solution.py:218
  40.3 2.2 %collective-permute-start.3 = (f32[16,2,128]{2,1,0:T(2,128)S(1)}, f32[16,2,128]{2,1,0:T(2,128)S(1)}, u32[]{:S(2)}, u32[]{:S(2)}) collective-permute-start(f32[16,2,128]{2,1,0:T(2,128)S(1)} %get-tuple-element.30), channel_id=1, source_target_pairs={{1,0},{2,1},{3,2},{5,4},{6,5},{7,6},{9,8},{10,9},{11,10},{13,12},{... | collective-permute-start | bytes 49160 | tf_op jit(solution)/shard_map/ppermute | solution.py:218
  42.5 3.1 %collective-permute-start.2 = (f32[16,2,128]{2,1,0:T(2,128)S(1)}, f32[16,2,128]{2,1,0:T(2,128)S(1)}, u32[]{:S(2)}, u32[]{:S(2)}) collective-permute-start(f32[16,2,128]{2,1,0:T(2,128)S(1)} %get-tuple-element.31), channel_id=1, source_target_pairs={{0,1},{1,2},{2,3},{4,5},{5,6},{6,7},{8,9},{9,10},{10,11},{12,13},{... | collective-permute-start | bytes 49160 | tf_op jit(solution)/shard_map/ppermute | solution.py:218
  47.0 8.1 %collective-permute-start.4 = (f32[2,144,128]{2,1,0:T(8,128)S(1)}, f32[2,144,128]{2,1,0:T(8,128)S(1)}, u32[]{:S(2)}, u32[]{:S(2)}) collective-permute-start(f32[2,144,128]{2,1,0:T(8,128)S(1)} %concatenate.15), channel_id=1, source_target_pairs={{0,32},{32,64},{64,96},{96,128},{128,160},{160,192},{192,224},{224... | collective-permute-start | bytes 442376 | tf_op jit(solution)/shard_map/ppermute | solution.py:218
  55.2 1.9 %collective-permute-start.5 = (f32[2,144,128]{2,1,0:T(8,128)S(1)}, f32[2,144,128]{2,1,0:T(8,128)S(1)}, u32[]{:S(2)}, u32[]{:S(2)}) collective-permute-start(f32[2,144,128]{2,1,0:T(8,128)S(1)} %concatenate.16), channel_id=1, source_target_pairs={{32,0},{64,32},{96,64},{128,96},{160,128},{192,160},{224,192},{256... | collective-permute-start | bytes 442376 | tf_op jit(solution)/shard_map/ppermute | solution.py:218
  57.2 5.6 %collective-permute-done.5.xh_ref = f32[2,144,128]{2,1,0:T(8,128)S(1)} collective-permute-done((f32[2,144,128]{2,1,0:T(8,128)S(1)}, f32[2,144,128]{2,1,0:T(8,128)S(1)}, u32[]{:S(2)}, u32[]{:S(2)}) %collective-permute-start.5) | collective-permute-done | bytes 147488 | tf_op jit(solution)/shard_map/ppermute | solution.py:218
  64.4 1.9 %shard_map.88 = (f32[20,144,128]{2,1,0:T(8,128)S(1)}, f32[20,144,128]{2,1,0:T(8,128)S(1)}) custom-call(f32[16,128,128]{2,1,0:T(8,128)S(1)} %shard_map.87.mid_ref, f32[16,2,128]{2,1,0:T(2,128)S(1)} %collective-permute-done.2.zl_ref, f32[16,2,128]{2,1,0:T(2,128)S(1)} %collective-permute-done.3.zh_ref, f32[2,144,128]{2,1,0:T(8,128)S(1)} %collective-permute-done.4.xl_ref, ...), custom_call_target="tpu_custom_call" | custom-call | tf_op jit(solution)/shard_map/pallas_call | solution.py:259
  67.5 1.4 %copy-done.1 = f32[20,144,128]{2,1,0:T(8,128)S(1)} copy-done((f32[20,144,128]{2,1,0:T(8,128)S(1)}, f32[20,144,128]{2,1,0:T(8,128)}, u32[]{:S(2)}) %copy-start.1) | copy-done | bytes 1474584
  68.8 11.2 %shard_map.89 = (f32[5,2,128,128]{3,2,1,0:T(8,128)S(1)}, f32[2304,128]{1,0:T(8,128)S(1)}, f32[288,128]{1,0:T(8,128)S(1)}, f32[288,128]{1,0:T(8,128)S(1)}) custom-call(f32[1408,128]{1,0:T(8,128)S(1)} %bitcast.16, f32[2880,128]{1,0:T(8,128)S(1)} %bitcast.17, f32[2880,128]{1,0:T(8,128)S(1)} %bitcast.18, f32[128,128]{1,0:T(8,128)S(1)} %bitcast.23, ...), custom_call_target="tpu_custom_call" | custom-call | tf_op jit(solution)/shard_map/pallas_call | solution.py:263
  80.1 1.9 %collective-permute-start.6 = (f32[2,144,128]{2,1,0:T(8,128)S(1)}, f32[2,144,128]{2,1,0:T(8,128)S(1)}, u32[]{:S(2)}, u32[]{:S(2)}) collective-permute-start(f32[2,144,128]{2,1,0:T(8,128)S(1)} %bitcast.29), channel_id=1, source_target_pairs={{0,32},{32,64},{64,96},{96,128},{128,160},{160,192},{192,224},{224... | collective-permute-start | bytes 442376 | tf_op jit(solution)/shard_map/ppermute | solution.py:218
  82.0 2.4 %collective-permute-start.7 = (f32[2,144,128]{2,1,0:T(8,128)S(1)}, f32[2,144,128]{2,1,0:T(8,128)S(1)}, u32[]{:S(2)}, u32[]{:S(2)}) collective-permute-start(f32[2,144,128]{2,1,0:T(8,128)S(1)} %bitcast.28), channel_id=1, source_target_pairs={{32,0},{64,32},{96,64},{128,96},{160,128},{192,160},{224,192},{256... | collective-permute-start | bytes 442376 | tf_op jit(solution)/shard_map/ppermute | solution.py:218
  84.4 5.2 %collective-permute-done.7.xh_ref = f32[2,144,128]{2,1,0:T(8,128)S(1)} collective-permute-done((f32[2,144,128]{2,1,0:T(8,128)S(1)}, f32[2,144,128]{2,1,0:T(8,128)S(1)}, u32[]{:S(2)}, u32[]{:S(2)}) %collective-permute-start.7) | collective-permute-done | bytes 147488 | tf_op jit(solution)/shard_map/ppermute | solution.py:218
  89.7 3.1 %collective-permute-start.8 = (f32[16,2,128]{2,1,0:T(2,128)S(1)}, f32[16,2,128]{2,1,0:T(2,128)S(1)}, u32[]{:S(2)}, u32[]{:S(2)}) collective-permute-start(f32[16,2,128]{2,1,0:T(2,128)S(1)} %pad_maximum_fusion.1), channel_id=1, source_target_pairs={{0,1},{1,2},{2,3},{4,5},{5,6},{6,7},{8,9},{9,10},{10,11},{12,13},{... | collective-permute-start | bytes 49160 | tf_op jit(solution)/shard_map/ppermute | solution.py:218
  92.8 2.2 %collective-permute-start.9 = (f32[16,2,128]{2,1,0:T(2,128)S(1)}, f32[16,2,128]{2,1,0:T(2,128)S(1)}, u32[]{:S(2)}, u32[]{:S(2)}) collective-permute-start(f32[16,2,128]{2,1,0:T(2,128)S(1)} %pad_maximum_fusion.2), channel_id=1, source_target_pairs={{1,0},{2,1},{3,2},{5,4},{6,5},{7,6},{9,8},{10,9},{11,10},{13,12},{... | collective-permute-start | bytes 49160 | tf_op jit(solution)/shard_map/ppermute | solution.py:218
  95.0 2.3 %collective-permute-done.9.zh_ref = f32[16,2,128]{2,1,0:T(2,128)S(1)} collective-permute-done((f32[16,2,128]{2,1,0:T(2,128)S(1)}, f32[16,2,128]{2,1,0:T(2,128)S(1)}, u32[]{:S(2)}, u32[]{:S(2)}) %collective-permute-start.9) | collective-permute-done | bytes 16416 | tf_op jit(solution)/shard_map/ppermute | solution.py:218
  97.7 3.3 %collective-permute-start.10 = (f32[4,16,2,128]{3,2,1,0:T(2,128)S(1)}, f32[4,16,2,128]{3,2,1,0:T(2,128)S(1)}, u32[]{:S(2)}, u32[]{:S(2)}) collective-permute-start(f32[4,16,2,128]{3,2,1,0:T(2,128)S(1)} %get-tuple-element.18), channel_id=1, source_target_pairs={{0,4},{4,8},{8,12},{12,16},{16,20},{20,24},{24,28},{1,5},{5,9},{9,... | collective-permute-start | bytes 196616 | tf_op jit(solution)/shard_map/ppermute | solution.py:218
  101.0 2.0 %collective-permute-start.11 = (f32[4,16,2,128]{3,2,1,0:T(2,128)S(1)}, f32[4,16,2,128]{3,2,1,0:T(2,128)S(1)}, u32[]{:S(2)}, u32[]{:S(2)}) collective-permute-start(f32[4,16,2,128]{3,2,1,0:T(2,128)S(1)} %get-tuple-element.19), channel_id=1, source_target_pairs={{4,0},{8,4},{12,8},{16,12},{20,16},{24,20},{28,24},{5,1},{9,5},{13... | collective-permute-start | bytes 196616 | tf_op jit(solution)/shard_map/ppermute | solution.py:218
  103.0 1.3 %copy.19 = f32[128,2,5,128]{3,1,0,2:T(2,128)} copy(f32[128,2,5,128]{3,0,1,2:T(8,128)S(1)} %bitcast.22) | data formatting | bytes 1310720 | tf_op jit(solution)/shard_map/transpose | solution.py:273
  104.4 3.2 %collective-permute-done.11 = f32[4,16,2,128]{3,2,1,0:T(2,128)S(1)} collective-permute-done((f32[4,16,2,128]{3,2,1,0:T(2,128)S(1)}, f32[4,16,2,128]{3,2,1,0:T(2,128)S(1)}, u32[]{:S(2)}, u32[]{:S(2)}) %collective-permute-start.11) | collective-permute-done | bytes 65568 | tf_op jit(solution)/shard_map/ppermute | solution.py:218
  (46 shorter events, 10.1 us)
Async XLA Ops:
  1.7 0.9 copy-start.5
  2.6 0.7 copy-start.6
  3.3 0.7 copy-start.7
  3.9 0.7 copy-start.8
  4.6 19.3 %copy-start.2 = (f32[4,16,16,128]{3,2,1,0:T(8,128)S(1)}, f32[4,16,16,128]{3,2,1,0:T(8,128)}, u32[]{:S(2)}) copy-start(f32[4,16,16,128]{3,2,1,0:T(8,128)} %gas_ref.1) | copy-start | bytes 1572868
  7.1 60.3 %all-to-all-start = ((f32[128,1,1408]{2,1,0:T(1,128)}), f32[128,1,1408]{2,1,0:T(1,128)S(1)}, u32[]{:S(2)}, u32[]{:S(2)}) async-start(f32[128,1,1408]{2,1,0:T(1,128)} %bitcast.3), calls=%async_computation | async-start | bytes 1441792 | tf_op jit(solution)/shard_map/all_to_all | solution.py:246
  24.0 11.9 %collective-permute-start.1 = (f32[4,16,2,128]{3,2,1,0:T(2,128)S(1)}, f32[4,16,2,128]{3,2,1,0:T(2,128)S(1)}, u32[]{:S(2)}, u32[]{:S(2)}) collective-permute-start(f32[4,16,2,128]{3,2,1,0:T(2,128)S(1)} %get-tuple-element.34), channel_id=1, source_target_pairs={{4,0},{8,4},{12,8},{16,12},{20,16},{24,20},{28,24},{5,1},{9,5},{13... | collective-permute-start | bytes 196616 | tf_op jit(solution)/shard_map/ppermute | solution.py:218
  26.2 30.9 %copy-start.9 = (f32[128,128]{1,0:T(8,128)S(1)}, f32[128,128]{1,0:T(8,128)}, u32[]{:S(2)}) copy-start(f32[128,128]{1,0:T(8,128)} %param.12) | copy-start | bytes 196612
  26.2 13.7 %collective-permute-start = (f32[4,16,2,128]{3,2,1,0:T(2,128)S(1)}, f32[4,16,2,128]{3,2,1,0:T(2,128)S(1)}, u32[]{:S(2)}, u32[]{:S(2)}) collective-permute-start(f32[4,16,2,128]{3,2,1,0:T(2,128)S(1)} %get-tuple-element.35), channel_id=1, source_target_pairs={{0,4},{4,8},{8,12},{12,16},{16,20},{20,24},{24,28},{1,5},{5,9},{9,... | collective-permute-start | bytes 196616 | tf_op jit(solution)/shard_map/ppermute | solution.py:218
  40.3 5.3 %collective-permute-start.3 = (f32[16,2,128]{2,1,0:T(2,128)S(1)}, f32[16,2,128]{2,1,0:T(2,128)S(1)}, u32[]{:S(2)}, u32[]{:S(2)}) collective-permute-start(f32[16,2,128]{2,1,0:T(2,128)S(1)} %get-tuple-element.30), channel_id=1, source_target_pairs={{1,0},{2,1},{3,2},{5,4},{6,5},{7,6},{9,8},{10,9},{11,10},{13,12},{... | collective-permute-start | bytes 49160 | tf_op jit(solution)/shard_map/ppermute | solution.py:218
  42.5 4.5 %collective-permute-start.2 = (f32[16,2,128]{2,1,0:T(2,128)S(1)}, f32[16,2,128]{2,1,0:T(2,128)S(1)}, u32[]{:S(2)}, u32[]{:S(2)}) collective-permute-start(f32[16,2,128]{2,1,0:T(2,128)S(1)} %get-tuple-element.31), channel_id=1, source_target_pairs={{0,1},{1,2},{2,3},{4,5},{5,6},{6,7},{8,9},{9,10},{10,11},{12,13},{... | collective-permute-start | bytes 49160 | tf_op jit(solution)/shard_map/ppermute | solution.py:218
  47.0 10.2 %collective-permute-start.4 = (f32[2,144,128]{2,1,0:T(8,128)S(1)}, f32[2,144,128]{2,1,0:T(8,128)S(1)}, u32[]{:S(2)}, u32[]{:S(2)}) collective-permute-start(f32[2,144,128]{2,1,0:T(8,128)S(1)} %concatenate.15), channel_id=1, source_target_pairs={{0,32},{32,64},{64,96},{96,128},{128,160},{160,192},{192,224},{224... | collective-permute-start | bytes 442376 | tf_op jit(solution)/shard_map/ppermute | solution.py:218
  55.2 7.7 %collective-permute-start.5 = (f32[2,144,128]{2,1,0:T(8,128)S(1)}, f32[2,144,128]{2,1,0:T(8,128)S(1)}, u32[]{:S(2)}, u32[]{:S(2)}) collective-permute-start(f32[2,144,128]{2,1,0:T(8,128)S(1)} %concatenate.16), channel_id=1, source_target_pairs={{32,0},{64,32},{96,64},{128,96},{160,128},{192,160},{224,192},{256... | collective-permute-start | bytes 442376 | tf_op jit(solution)/shard_map/ppermute | solution.py:218
  62.9 0.7 copy-start.3
  63.5 0.9 copy-start.4
  66.3 1.1 %copy-start = (f32[20,144,128]{2,1,0:T(8,128)}, f32[20,144,128]{2,1,0:T(8,128)S(1)}, u32[]{:S(2)}) copy-start(f32[20,144,128]{2,1,0:T(8,128)S(1)} %get-tuple-element.12) | copy-start | bytes 4423684
  67.5 1.4 %copy-start.1 = (f32[20,144,128]{2,1,0:T(8,128)S(1)}, f32[20,144,128]{2,1,0:T(8,128)}, u32[]{:S(2)}) copy-start(f32[20,144,128]{2,1,0:T(8,128)} %copy-done) | copy-start | bytes 4423684
  80.1 4.4 %collective-permute-start.6 = (f32[2,144,128]{2,1,0:T(8,128)S(1)}, f32[2,144,128]{2,1,0:T(8,128)S(1)}, u32[]{:S(2)}, u32[]{:S(2)}) collective-permute-start(f32[2,144,128]{2,1,0:T(8,128)S(1)} %bitcast.29), channel_id=1, source_target_pairs={{0,32},{32,64},{64,96},{96,128},{128,160},{160,192},{192,224},{224... | collective-permute-start | bytes 442376 | tf_op jit(solution)/shard_map/ppermute | solution.py:218
  82.0 7.7 %collective-permute-start.7 = (f32[2,144,128]{2,1,0:T(8,128)S(1)}, f32[2,144,128]{2,1,0:T(8,128)S(1)}, u32[]{:S(2)}, u32[]{:S(2)}) collective-permute-start(f32[2,144,128]{2,1,0:T(8,128)S(1)} %bitcast.28), channel_id=1, source_target_pairs={{32,0},{64,32},{96,64},{128,96},{160,128},{192,160},{224,192},{256... | collective-permute-start | bytes 442376 | tf_op jit(solution)/shard_map/ppermute | solution.py:218
  89.7 5.3 %collective-permute-start.8 = (f32[16,2,128]{2,1,0:T(2,128)S(1)}, f32[16,2,128]{2,1,0:T(2,128)S(1)}, u32[]{:S(2)}, u32[]{:S(2)}) collective-permute-start(f32[16,2,128]{2,1,0:T(2,128)S(1)} %pad_maximum_fusion.1), channel_id=1, source_target_pairs={{0,1},{1,2},{2,3},{4,5},{5,6},{6,7},{8,9},{9,10},{10,11},{12,13},{... | collective-permute-start | bytes 49160 | tf_op jit(solution)/shard_map/ppermute | solution.py:218
  92.8 4.5 %collective-permute-start.9 = (f32[16,2,128]{2,1,0:T(2,128)S(1)}, f32[16,2,128]{2,1,0:T(2,128)S(1)}, u32[]{:S(2)}, u32[]{:S(2)}) collective-permute-start(f32[16,2,128]{2,1,0:T(2,128)S(1)} %pad_maximum_fusion.2), channel_id=1, source_target_pairs={{1,0},{2,1},{3,2},{5,4},{6,5},{7,6},{9,8},{10,9},{11,10},{13,12},{... | collective-permute-start | bytes 49160 | tf_op jit(solution)/shard_map/ppermute | solution.py:218
  97.7 6.7 %collective-permute-start.10 = (f32[4,16,2,128]{3,2,1,0:T(2,128)S(1)}, f32[4,16,2,128]{3,2,1,0:T(2,128)S(1)}, u32[]{:S(2)}, u32[]{:S(2)}) collective-permute-start(f32[4,16,2,128]{3,2,1,0:T(2,128)S(1)} %get-tuple-element.18), channel_id=1, source_target_pairs={{0,4},{4,8},{8,12},{12,16},{16,20},{20,24},{24,28},{1,5},{5,9},{9,... | collective-permute-start | bytes 196616 | tf_op jit(solution)/shard_map/ppermute | solution.py:218
  101.0 6.5 %collective-permute-start.11 = (f32[4,16,2,128]{3,2,1,0:T(2,128)S(1)}, f32[4,16,2,128]{3,2,1,0:T(2,128)S(1)}, u32[]{:S(2)}, u32[]{:S(2)}) collective-permute-start(f32[4,16,2,128]{3,2,1,0:T(2,128)S(1)} %get-tuple-element.19), channel_id=1, source_target_pairs={{4,0},{8,4},{12,8},{16,12},{20,16},{24,20},{28,24},{5,1},{9,5},{13... | collective-permute-start | bytes 196616 | tf_op jit(solution)/shard_map/ppermute | solution.py:218
where the time goes:
time: 109 us
  starting transfers between devices  52.4 us (48%)
  waiting for transfers between devices  28.1 us (26%)
  Pallas kernels  16.4 us (15%)
  local copies, waits for them, and re-layouts  9.68 us (9%)
    ppermute x12, starting transfers between devices, shift_pair(): return (lax.ppermute(to_high, axis, up), lax.ppermute(to_low, axis, down))  35.6 us
    ppermute x12, waiting for transfers between devices, shift_pair(): return (lax.ppermute(to_high, axis, up), lax.ppermute(to_low, axis, down))  28.1 us
    all_to_all x1, starting transfers between devices, per_device(): lax.all_to_all(send.reshape(blocks, ROWS * LANES), ('gx', 'gy'), split_ax...  16.8 us
    pallas_call x1, Pallas kernels, per_device(): call(parcel_kernel, [arr(5, 2, blocks, LANES), arr(nx * ZR, LANES), arr(2...  11.2 us
    unnamed x22, local copies, waits for them, and re-layouts  8.11 us
    pallas_call x1, Pallas kernels, per_device(): call(pack_kernel, arr(blocks * ROWS, LANES))  2.55 us
  transfers between devices with their start and end apart: 13, of which 7 were waited for; matrix products, arithmetic and copies ran while one was open for 2% of the time, Pallas kernels for 2%

commit v1 on v0

v1 whole, which is shorter than its diff:
```python
import functools
import jax
import jax.numpy as jnp
from jax import lax
from jax.experimental import pallas as pl
from jax.experimental.pallas import tpu as pltpu
from jax.sharding import PartitionSpec as P

TIME_STEP = 0.05
SETTLING = 1.0
F32 = jnp.float32
BF16 = jnp.bfloat16
HI = lax.Precision.HIGHEST

LANES = 128
ROWS = 11
ZR = 144
ZO = 8
YS = 32


def iota(shape, dim):
    return lax.broadcasted_iota(jnp.int32, shape, dim)


def pack_kernel(tgt_ref, off_ref, cnt_ref, vel_ref, prop_ref, out_ref):
    n = LANES
    hot = (iota((n, n), 0) == tgt_ref[...]).astype(F32)
    earlier = (iota((n, n), 0) < iota((n, n), 1)).astype(BF16)
    rank = jnp.dot(hot.astype(BF16), earlier, preferred_element_type=F32)
    first = jnp.where(rank < 0.5, hot, 0.0)
    second = jnp.where(rank > 0.5, hot, 0.0)
    off = off_ref[...].astype(F32)
    cnt = cnt_ref[...].astype(F32)
    lane = iota((n, n), 1)
    head = jnp.zeros((n, n), F32)
    for place, (pick, val) in enumerate(((first, off), (second, off), (first, cnt), (second, cnt))):
        column = jnp.sum(pick * val, axis=1, keepdims=True)
        head = jnp.where(lane == place, column, head)
    out_ref[pl.ds(10, n, stride=ROWS), :] = head
    picks = jnp.concatenate([first, second], axis=0).astype(BF16)
    for k in range(5):
        x = vel_ref[k] if k < 3 else prop_ref[:, k - 3, :]
        total = jnp.zeros((2 * n, n), F32)
        for _ in range(3):
            part = x.astype(BF16)
            x = x - part.astype(F32)
            total = total + jnp.dot(picks, part, preferred_element_type=F32)
        out_ref[pl.ds(k, n, stride=ROWS), :] = total[:n]
        out_ref[pl.ds(5 + k, n, stride=ROWS), :] = total[n:]


def turn_kernel(gas_ref, low_ref, high_ref, send_ref, out_ref, same_ref, buf):
    del send_ref, same_ref
    cells_x, cells_y = gas_ref.shape[1], gas_ref.shape[2]
    buf[...] = jnp.zeros_like(buf)
    for x in range(cells_x):
        for k in range(4):
            buf[x, k * YS : k * YS + 2, :] = low_ref[k, x]
            buf[x, k * YS + 2 : k * YS + 2 + cells_y, :] = gas_ref[k, x]
            buf[x, k * YS + 2 + cells_y : k * YS + 4 + cells_y, :] = high_ref[k, x]
    for x in range(cells_x):
        out_ref[x] = buf[x].T


def diffuse_kernel(mid_ref, zl_ref, zh_ref, xl_ref, xh_ref, out_ref, col):
    cells_x, cells_z = mid_ref.shape[0], mid_ref.shape[1]
    last = ZO + cells_z
    lane = iota((cells_z, LANES), 1)
    rate = jnp.where(lane < 3 * YS, TIME_STEP, 0.5 * TIME_STEP).astype(F32)
    for x in range(cells_x):
        here = mid_ref[x]
        col[x % 2, ZO:last, :] = here
        col[x % 2, ZO - 2 : ZO, :] = zl_ref[x]
        col[x % 2, last : last + 2, :] = zh_ref[x]
        left = mid_ref[x - 1] if x else xl_ref[1, ZO:last, :]
        right = mid_ref[x + 1] if x < cells_x - 1 else xh_ref[0, ZO:last, :]
        beside = left + right + pltpu.roll(here, LANES - 1, 1) + pltpu.roll(here, 1, 1)
        beside = beside + col[x % 2, ZO + 1 : last + 1, :] + col[x % 2, ZO - 1 : last - 1, :]
        out_ref[x] = here + rate * (beside - 6.0 * here)


def parcel_kernel(
    recv_ref, mid_ref, zl_ref, zh_ref, xl_ref, xh_ref, w_ref,
    pay_ref, sum_ref, xlo_ref, xhi_ref,
    code_v, code_s, pad, acc, near, force, sem,
):
    cells_x, cells_z = mid_ref.shape[0], mid_ref.shape[1]
    planes = cells_x + 4
    last = ZO + cells_z
    n = LANES
    off = recv_ref[pl.ds(10, n, stride=ROWS), :]
    rest = jnp.floor((off + 0.5) * (1.0 / 125.0))
    oz = off - rest * 125.0
    ox = jnp.floor((rest + 0.5) * (1.0 / 17.0))
    oy = rest - ox * 17.0
    code = oy * 4096.0 + ox * float(ZR) + oz + float(ZO - 2)
    code_v[...] = code.T[0:8].astype(jnp.int32)
    copy = pltpu.make_async_copy(code_v, code_s, sem)
    copy.start()
    for p in range(2):
        pad[p * ZR : (p + 1) * ZR, :] = xl_ref[p]
        pad[(planes - 2 + p) * ZR : (planes - 1 + p) * ZR, :] = xh_ref[p]
    for x in range(cells_x):
        at = (x + 2) * ZR
        pad[at + ZO : at + last, :] = mid_ref[x]
        pad[at + ZO - 2 : at + ZO, :] = zl_ref[x]
        pad[at + last : at + last + 2, :] = zh_ref[x]
    acc[...] = jnp.zeros_like(acc)
    copy.wait()

    lane8 = iota((8, n), 1)
    group = (lane8 % YS) // 4
    quad = lane8 % 4
    lane = iota((YS, n), 1)

    def place(s, b):
        c = code_s[s // 4, (s % 4) * YS + b]
        return jnp.bitwise_and(c, 4095), lax.shift_right_logical(c, 12)

    @pl.loop(0, 8)
    def _(s):
        merged = []
        for g in range(4):
            total = [None] * 4
            for b8 in range(8):
                at, oy_b = place(s, b8 * 4 + g)
                shift = jnp.bitwise_and(4 * b8 - oy_b, n - 1)
                mine = group == b8
                for a in range(4):
                    x = pltpu.roll(pad[pl.ds(at + a * ZR, 8), :], shift, 1)
                    total[a] = jnp.where(mine, x, 0.0 if total[a] is None else total[a])
            merged.append(total)
        cells = []
        for e in range(4):
            for a in range(4):
                x = merged[0][a]
                out = pltpu.roll(x, -e % n, 1) if e else x
                for g in range(1, 4):
                    x = merged[g][a]
                    x = pltpu.roll(x, (g - e) % n, 1) if g != e else x
                    out = jnp.where(quad == g, x, out)
                cells.append(out)
        near[pl.ds(pl.multiple_of(s * n, n), n), :] = jnp.concatenate(cells, axis=0).T

    gas_all = jnp.dot(near[...], w_ref[...], precision=HI, preferred_element_type=F32)
    for s in range(8):
        rank, q0 = s // 4, (s % 4) * YS
        row = q0 * ROWS + rank * 5

        def take(k):
            return recv_ref[pl.ds(row + k, YS, stride=ROWS), :]

        head = recv_ref[pl.ds(q0 * ROWS + 10, YS, stride=ROWS), :]
        alive = lane.astype(F32) < head[:, 2 + rank : 3 + rank]
        mass = jnp.where(alive, take(3), 0.0)
        relax = jnp.where(alive, take(4), 1.0)
        drag = TIME_STEP / relax
        under = 1.0 / (1.0 + drag)
        slots = pl.ds(2 * q0 + rank, YS, stride=2)
        for k in range(3):
            gas = gas_all[s * n + k * YS : s * n + (k + 1) * YS]
            settle = TIME_STEP * SETTLING if k == 2 else 0.0
            vel = (take(k) + drag * gas - settle) * under
            force[s * n + k * YS : s * n + (k + 1) * YS, :] = -(mass * drag * (gas - vel))
            pay_ref[k, slots, :] = jnp.where(alive, vel, 0.0)
        pay_ref[3, slots, :] = mass
        pay_ref[4, slots, :] = jnp.where(alive, relax, 0.0)
        force[s * n + 3 * YS : (s + 1) * n, :] = mass
    for s in range(8):
        near[s * n : (s + 1) * n, :] = lax.dot_general(
            w_ref[...],
            force[s * n : (s + 1) * n, :],
            (((1,), (1,)), ((), ())),
            precision=HI,
            preferred_element_type=F32,
        )

    @pl.loop(0, 8)
    def _(s):
        spread = near[pl.ds(pl.multiple_of(s * n, n), n), :]
        for g in range(4):
            parts = []
            for a in range(4):
                out = None
                for e in range(4):
                    x = spread[(e * 4 + a) * 8 : (e * 4 + a) * 8 + 8]
                    x = pltpu.roll(x, (e - g) % n, 1) if e != g else x
                    out = x if out is None else jnp.where(quad == e, x, out)
                parts.append(out)
            for b8 in range(8):
                at, oy_b = place(s, b8 * 4 + g)
                shift = jnp.bitwise_and(oy_b - 4 * b8, n - 1)
                mine = group == b8
                adds = [pltpu.roll(jnp.where(mine, parts[a], 0.0), shift, 1) for a in range(4)]
                olds = [acc[pl.ds(at + a * ZR, 8), :] for a in range(4)]
                for a in range(4):
                    acc[pl.ds(at + a * ZR, 8), :] = olds[a] + adds[a]

    sum_ref[...] = acc[2 * ZR : (planes - 2) * ZR, :]
    xlo_ref[...] = acc[0 : 2 * ZR, :]
    xhi_ref[...] = acc[(planes - 2) * ZR :, :]


def back_kernel(sum_ref, base_ref, xl_ref, xh_ref, zl_ref, zh_ref, out_ref, ylo_ref, yhi_ref, buf):
    cells_x = sum_ref.shape[0]
    cells_z = out_ref.shape[3]
    cells_y = out_ref.shape[2]
    for x in range(cells_x):
        value = sum_ref[x, ZO : ZO + cells_z, :]
        if x < 2:
            value = value + xl_ref[x, ZO : ZO + cells_z, :]
        if x >= cells_x - 2:
            value = value + xh_ref[x - cells_x + 2, ZO : ZO + cells_z, :]
        buf[x] = value
    buf[:, 0:2, :] += zl_ref[...]
    buf[:, cells_z - 2 : cells_z, :] += zh_ref[...]
    lane = iota((cells_z, LANES), 1)
    inside = (lane % YS >= 2) & (lane % YS < 2 + cells_y)
    for x in range(cells_x):
        flat = (buf[x] + jnp.where(inside, base_ref[x], 0.0)).T
        for k in range(4):
            out_ref[k, x] = flat[k * YS + 2 : k * YS + 2 + cells_y]
            ylo_ref[k, x] = flat[k * YS : k * YS + 2]
            yhi_ref[k, x] = flat[k * YS + 2 + cells_y : k * YS + 4 + cells_y]


def shift_pair(to_low, to_high, axis):
    count = lax.axis_size(axis)
    up = [(i, i + 1) for i in range(count - 1)]
    down = [(j, i) for i, j in up]
    return lax.ppermute(to_high, axis, up), lax.ppermute(to_low, axis, down)


def call(kernel, outs, scratch=(), cost=None, **kw):
    return pl.pallas_call(
        kernel,
        out_shape=outs,
        scratch_shapes=list(scratch),
        compiler_params=pltpu.CompilerParams(vmem_limit_bytes=40 * 2**20),
        cost_estimate=cost,
        **kw,
    )


def arr(*shape, dtype=F32):
    return jax.ShapeDtypeStruct(shape, dtype)


def parcels(recv, mid, z_low, z_high, x_low, x_high, weight):
    nx = mid.shape[0]
    blocks = recv.shape[0] // ROWS
    rows = (nx + 4) * ZR
    return call(
        parcel_kernel,
        [arr(5, 2 * blocks, LANES), arr(nx * ZR, LANES), arr(2 * ZR, LANES), arr(2 * ZR, LANES)],
        [
            pltpu.VMEM((8, LANES), jnp.int32),
            pltpu.SMEM((8, LANES), jnp.int32),
            pltpu.VMEM((rows, LANES), F32),
            pltpu.VMEM((rows, LANES), F32),
            pltpu.VMEM((8 * LANES, LANES), F32),
            pltpu.VMEM((8 * LANES, LANES), F32),
            pltpu.SemaphoreType.DMA,
        ],
    )(recv, mid, z_low, z_high, x_low, x_high, weight)


def per_device(parcel_vel, parcel_props, fill_count, owner_peer, cell_offset, shell_weight, gas_state):
    _, nx, ny, nz = gas_state.shape
    blocks = parcel_vel.shape[0]
    send = call(pack_kernel, arr(blocks * ROWS, LANES))(
        owner_peer.reshape(1, blocks),
        cell_offset.reshape(1, blocks),
        fill_count.reshape(1, blocks),
        parcel_vel.transpose(1, 0, 2),
        parcel_props,
    )
    y_low, y_high = shift_pair(gas_state[:, :, :2], gas_state[:, :, ny - 2 :], "gy")
    whole = pl.BlockSpec(memory_space=pltpu.VMEM)
    where = pl.BlockSpec(memory_space=pl.ANY)
    mid, send = call(
        turn_kernel,
        [arr(nx, nz, LANES), arr(blocks * ROWS, LANES)],
        [pltpu.VMEM((nx, LANES, nz), F32)],
        in_specs=[whole, whole, whole, where],
        out_specs=[whole, where],
        input_output_aliases={3: 1},
    )(gas_state, y_low, y_high, send)
    recv = lax.all_to_all(
        send.reshape(blocks, ROWS * LANES), ("gx", "gy"), split_axis=0, concat_axis=0, tiled=True
    ).reshape(blocks * ROWS, LANES)
    z_low, z_high = shift_pair(mid[:, :2], mid[:, nz - 2 :], "gz")

    def face(lo, hi):
        zero = jnp.zeros((2, ZO - 2, LANES), F32)
        return jnp.concatenate([zero, z_low[lo:hi], mid[lo:hi], z_high[lo:hi], zero], axis=1)

    x_low, x_high = shift_pair(face(0, 2), face(nx - 2, nx), "gx")
    halo = (mid, z_low, z_high, x_low, x_high)

    weight = shell_weight.reshape(LANES, 4, 4, 8).transpose(2, 1, 3, 0).reshape(LANES, LANES)
    pay, total, x_lo, x_hi = parcels(recv, *halo, weight)
    parcels_next = pay.transpose(1, 0, 2)
    base = call(diffuse_kernel, arr(nx, nz, LANES), [pltpu.VMEM((2, ZR, LANES), F32)])(*halo)

    from_low, from_high = shift_pair(x_lo.reshape(2, ZR, LANES), x_hi.reshape(2, ZR, LANES), "gx")
    total = total.reshape(nx, ZR, LANES)

    def rim(lo, hi):
        part = total[:, lo:hi]
        return jnp.concatenate(
            [part[:2] + from_low[:, lo:hi], part[2 : nx - 2], part[nx - 2 :] + from_high[:, lo:hi]], axis=0
        )

    z_below, z_above = shift_pair(rim(ZO - 2, ZO), rim(ZO + nz, ZO + nz + 2), "gz")
    rows_out, y_lo, y_hi = call(
        back_kernel,
        [arr(4, nx, ny, nz), arr(4, nx, 2, nz), arr(4, nx, 2, nz)],
        [pltpu.VMEM((nx, nz, LANES), F32)],
    )(total, base, from_low, from_high, z_below, z_above)
    y_below, y_above = shift_pair(y_lo, y_hi, "gy")
    gas_next = jnp.concatenate(
        [rows_out[:, :, :2] + y_below, rows_out[:, :, 2 : ny - 2], rows_out[:, :, ny - 2 :] + y_above], axis=2
    )
    return parcels_next, gas_next


def solution(mesh):
    return jax.shard_map(
        per_device,
        mesh=mesh,
        in_specs=(
            P(("gx", "gy", "gz"), None, None),
            P(("gx", "gy", "gz"), None, None),
            P(("gx", "gy", "gz")),
            P(("gx", "gy", "gz"), None),
            P(("gx", "gy", "gz")),
            P(),
            P(None, "gx", "gy", "gz"),
        ),
        out_specs=(P(("gx", "gy", "gz"), None, None), P(None, "gx", "gy", "gz")),
        check_vma=False,
    )
```

time: 109 us -> 94.3 us (0.87)
  the two profiles are of different devices: /device:TPU:91 before, /device:TPU:1 now
where the time goes in v1:
time: 94.3 us; the launch traced here: 93.7 us
  starting transfers between devices  48.8 us (52%)
  waiting for transfers between devices  24.3 us (26%)
  Pallas kernels  13.5 us (14%)
  local copies, waits for them, and re-layouts  5.21 us (6%)
  other arithmetic  1.01 us (1%)
    ppermute x12, starting transfers between devices, shift_pair(): return (lax.ppermute(to_high, axis, up), lax.ppermute(to_low, axis, down))  29.3 us
    all_to_all x1, starting transfers between devices, per_device(): lax.all_to_all(send.reshape(blocks, ROWS * LANES), ('gx', 'gy'), split_ax...  19.5 us
    ppermute x12, waiting for transfers between devices, shift_pair(): return (lax.ppermute(to_high, axis, up), lax.ppermute(to_low, axis, down))  18.5 us
    pallas_call x1, Pallas kernels, parcels(): call(parcel_kernel, [arr(5, 2 * blocks, LANES), arr(nx * ZR, LANES), arr(...  10.2 us
    all_to_all x1, waiting for transfers between devices, per_device(): lax.all_to_all(send.reshape(blocks, ROWS * LANES), ('gx', 'gy'), split_ax...  5.81 us
    unnamed x15, local copies, waits for them, and re-layouts  3.89 us
  transfers between devices with their start and end apart: 13, of which 7 were waited for; matrix products, arithmetic and copies ran while one was open for 0% of the time, Pallas kernels for 3%

profile of v1, /device:TPU:1, one launch (start us, length us, event | category | flops | bytes accessed | tf_op | source)
XLA Modules:
  0.0 93.7 jit_solution(5680691640313753982)
XLA Ops:
  0.6 1.1 %fusion.3 = (f32[4,16,2,128]{3,2,1,0:T(2,128)S(1)}, f32[4,16,2,128]{3,2,1,0:T(2,128)S(1)}) fusion(f32[4,16,16,128]{3,2,1,0:T(8,128)} %gas_ref.1), kind=kLoop, calls=%fused_computation.12 | loop fusion | bytes 262144 | tf_op jit(solution)/shard_map/slice | solution.py:279
  1.8 4.8 %collective-permute-start = (f32[4,16,2,128]{3,2,1,0:T(2,128)S(1)}, f32[4,16,2,128]{3,2,1,0:T(2,128)S(1)}, u32[]{:S(2)}, u32[]{:S(2)}) collective-permute-start(f32[4,16,2,128]{3,2,1,0:T(2,128)S(1)} %get-tuple-element.35), channel_id=1, source_target_pairs={{0,4},{4,8},{8,12},{12,16},{16,20},{20,24},{24,28},{1,5},{5,9},{9,... | collective-permute-start | bytes 196616 | tf_op jit(solution)/shard_map/ppermute | solution.py:232
  6.6 1.3 %collective-permute-start.1 = (f32[4,16,2,128]{3,2,1,0:T(2,128)S(1)}, f32[4,16,2,128]{3,2,1,0:T(2,128)S(1)}, u32[]{:S(2)}, u32[]{:S(2)}) collective-permute-start(f32[4,16,2,128]{3,2,1,0:T(2,128)S(1)} %get-tuple-element.34), channel_id=1, source_target_pairs={{4,0},{8,4},{12,8},{16,12},{20,16},{24,20},{28,24},{5,1},{9,5},{13... | collective-permute-start | bytes 196616 | tf_op jit(solution)/shard_map/ppermute | solution.py:232
  7.9 0.9 copy-done.1
  11.7 1.9 %shard_map.86.send_ref = f32[1408,128]{1,0:T(8,128)} custom-call(s32[1,128]{1,0:T(1,128)S(1)} %bitcast.20, s32[1,128]{1,0:T(1,128)S(1)} %bitcast.21, s32[1,128]{1,0:T(1,128)S(1)} %bitcast.22, f32[3,128,128]{2,1,0:T(8,128)S(1)} %bitcast.19, f32[128,2,128]{2,1,0:T(2,128)S(1)} %copy-done.2), custom_call_target="tpu_custom_call" | custom-call | tf_op jit(solution)/shard_map/pallas_call | solution.py:272
  14.0 19.5 %all-to-all-start = ((f32[128,1,1408]{2,1,0:T(1,128)}), f32[128,1,1408]{2,1,0:T(1,128)S(1)}, u32[]{:S(2)}, u32[]{:S(2)}) async-start(f32[128,1,1408]{2,1,0:T(1,128)} %bitcast.4), calls=%async_computation | async-start | bytes 1441792 | tf_op jit(solution)/shard_map/all_to_all | solution.py:290
  33.5 3.1 %collective-permute-start.2 = (f32[16,2,128]{2,1,0:T(2,128)S(1)}, f32[16,2,128]{2,1,0:T(2,128)S(1)}, u32[]{:S(2)}, u32[]{:S(2)}) collective-permute-start(f32[16,2,128]{2,1,0:T(2,128)S(1)} %get-tuple-element.31), channel_id=1, source_target_pairs={{0,1},{1,2},{2,3},{4,5},{5,6},{6,7},{8,9},{9,10},{10,11},{12,13},{... | collective-permute-start | bytes 49160 | tf_op jit(solution)/shard_map/ppermute | solution.py:232
  36.7 1.3 %collective-permute-start.3 = (f32[16,2,128]{2,1,0:T(2,128)S(1)}, f32[16,2,128]{2,1,0:T(2,128)S(1)}, u32[]{:S(2)}, u32[]{:S(2)}) collective-permute-start(f32[16,2,128]{2,1,0:T(2,128)S(1)} %get-tuple-element.30), channel_id=1, source_target_pairs={{1,0},{2,1},{3,2},{5,4},{6,5},{7,6},{9,8},{10,9},{11,10},{13,12},{... | collective-permute-start | bytes 49160 | tf_op jit(solution)/shard_map/ppermute | solution.py:232
  38.0 3.5 %collective-permute-done.3.zh_ref = f32[16,2,128]{2,1,0:T(2,128)S(1)} collective-permute-done((f32[16,2,128]{2,1,0:T(2,128)S(1)}, f32[16,2,128]{2,1,0:T(2,128)S(1)}, u32[]{:S(2)}, u32[]{:S(2)}) %collective-permute-start.3) | collective-permute-done | bytes 16416 | tf_op jit(solution)/shard_map/ppermute | solution.py:232
  41.5 4.7 %collective-permute-start.4 = (f32[2,144,128]{2,1,0:T(8,128)S(1)}, f32[2,144,128]{2,1,0:T(8,128)S(1)}, u32[]{:S(2)}, u32[]{:S(2)}) collective-permute-start(f32[2,144,128]{2,1,0:T(8,128)S(1)} %concatenate.15), channel_id=1, source_target_pairs={{0,32},{32,64},{64,96},{96,128},{128,160},{160,192},{192,224},{224... | collective-permute-start | bytes 442376 | tf_op jit(solution)/shard_map/ppermute | solution.py:232
  46.2 1.9 %collective-permute-start.5 = (f32[2,144,128]{2,1,0:T(8,128)S(1)}, f32[2,144,128]{2,1,0:T(8,128)S(1)}, u32[]{:S(2)}, u32[]{:S(2)}) collective-permute-start(f32[2,144,128]{2,1,0:T(8,128)S(1)} %concatenate.16), channel_id=1, source_target_pairs={{32,0},{64,32},{96,64},{128,96},{160,128},{192,160},{224,192},{256... | collective-permute-start | bytes 442376 | tf_op jit(solution)/shard_map/ppermute | solution.py:232
  48.3 1.3 %collective-permute-done.4.xl_ref = f32[2,144,128]{2,1,0:T(8,128)S(1)} collective-permute-done((f32[2,144,128]{2,1,0:T(8,128)S(1)}, f32[2,144,128]{2,1,0:T(8,128)S(1)}, u32[]{:S(2)}, u32[]{:S(2)}) %collective-permute-start.4) | collective-permute-done | bytes 147488 | tf_op jit(solution)/shard_map/ppermute | solution.py:232
  49.5 3.4 %collective-permute-done.5.xh_ref = f32[2,144,128]{2,1,0:T(8,128)S(1)} collective-permute-done((f32[2,144,128]{2,1,0:T(8,128)S(1)}, f32[2,144,128]{2,1,0:T(8,128)S(1)}, u32[]{:S(2)}, u32[]{:S(2)}) %collective-permute-start.5) | collective-permute-done | bytes 147488 | tf_op jit(solution)/shard_map/ppermute | solution.py:232
  53.0 5.8 %all-to-all-done = f32[128,1,1408]{2,1,0:T(1,128)S(1)} async-done(((f32[128,1,1408]{2,1,0:T(1,128)}), f32[128,1,1408]{2,1,0:T(1,128)S(1)}, u32[]{:S(2)}, u32[]{:S(2)}) %all-to-all-start) | async-done | bytes 720928 | tf_op jit(solution)/shard_map/all_to_all | solution.py:290
  58.8 10.2 %shard_map.88 = (f32[5,256,128]{2,1,0:T(8,128)}, f32[2304,128]{1,0:T(8,128)S(1)}, f32[288,128]{1,0:T(8,128)S(1)}, f32[288,128]{1,0:T(8,128)S(1)}) custom-call(f32[1408,128]{1,0:T(8,128)S(1)} %bitcast.14, f32[16,128,128]{2,1,0:T(8,128)S(1)} %get-tuple-element.12.mid_ref, f32[16,2,128]{2,1,0:T(2,128)S(1)} %collective-permute-done.2.zl_ref, ...), custom_call_target="tpu_custom_call" | custom-call | tf_op jit(solution)/shard_map/pallas_call | solution.py:254
  69.0 1.9 %collective-permute-start.6 = (f32[2,144,128]{2,1,0:T(8,128)S(1)}, f32[2,144,128]{2,1,0:T(8,128)S(1)}, u32[]{:S(2)}, u32[]{:S(2)}) collective-permute-start(f32[2,144,128]{2,1,0:T(8,128)S(1)} %bitcast.24), channel_id=1, source_target_pairs={{0,32},{32,64},{64,96},{96,128},{128,160},{160,192},{192,224},{224... | collective-permute-start | bytes 442376 | tf_op jit(solution)/shard_map/ppermute | solution.py:232
  70.9 2.4 %collective-permute-start.7 = (f32[2,144,128]{2,1,0:T(8,128)S(1)}, f32[2,144,128]{2,1,0:T(8,128)S(1)}, u32[]{:S(2)}, u32[]{:S(2)}) collective-permute-start(f32[2,144,128]{2,1,0:T(8,128)S(1)} %bitcast.23), channel_id=1, source_target_pairs={{32,0},{64,32},{96,64},{128,96},{160,128},{192,160},{224,192},{256... | collective-permute-start | bytes 442376 | tf_op jit(solution)/shard_map/ppermute | solution.py:232
  73.3 4.0 %collective-permute-done.7.xh_ref = f32[2,144,128]{2,1,0:T(8,128)S(1)} collective-permute-done((f32[2,144,128]{2,1,0:T(8,128)S(1)}, f32[2,144,128]{2,1,0:T(8,128)S(1)}, u32[]{:S(2)}, u32[]{:S(2)}) %collective-permute-start.7) | collective-permute-done | bytes 147488 | tf_op jit(solution)/shard_map/ppermute | solution.py:232
  77.4 3.1 %collective-permute-start.8 = (f32[16,2,128]{2,1,0:T(2,128)S(1)}, f32[16,2,128]{2,1,0:T(2,128)S(1)}, u32[]{:S(2)}, u32[]{:S(2)}) collective-permute-start(f32[16,2,128]{2,1,0:T(2,128)S(1)} %pad_maximum_fusion.1), channel_id=1, source_target_pairs={{0,1},{1,2},{2,3},{4,5},{5,6},{6,7},{8,9},{9,10},{10,11},{12,13},{... | collective-permute-start | bytes 49160 | tf_op jit(solution)/shard_map/ppermute | solution.py:232
  80.5 1.3 %collective-permute-start.9 = (f32[16,2,128]{2,1,0:T(2,128)S(1)}, f32[16,2,128]{2,1,0:T(2,128)S(1)}, u32[]{:S(2)}, u32[]{:S(2)}) collective-permute-start(f32[16,2,128]{2,1,0:T(2,128)S(1)} %pad_maximum_fusion.2), channel_id=1, source_target_pairs={{1,0},{2,1},{3,2},{5,4},{6,5},{7,6},{9,8},{10,9},{11,10},{13,12},{... | collective-permute-start | bytes 49160 | tf_op jit(solution)/shard_map/ppermute | solution.py:232
  82.5 2.5 %collective-permute-done.9.zh_ref = f32[16,2,128]{2,1,0:T(2,128)S(1)} collective-permute-done((f32[16,2,128]{2,1,0:T(2,128)S(1)}, f32[16,2,128]{2,1,0:T(2,128)S(1)}, u32[]{:S(2)}, u32[]{:S(2)}) %collective-permute-start.9) | collective-permute-done | bytes 16416 | tf_op jit(solution)/shard_map/ppermute | solution.py:232
  85.4 2.2 %collective-permute-start.10 = (f32[4,16,2,128]{3,2,1,0:T(2,128)S(1)}, f32[4,16,2,128]{3,2,1,0:T(2,128)S(1)}, u32[]{:S(2)}, u32[]{:S(2)}) collective-permute-start(f32[4,16,2,128]{3,2,1,0:T(2,128)S(1)} %get-tuple-element.18), channel_id=1, source_target_pairs={{0,4},{4,8},{8,12},{12,16},{16,20},{20,24},{24,28},{1,5},{5,9},{9,... | collective-permute-start | bytes 196616 | tf_op jit(solution)/shard_map/ppermute | solution.py:232
  87.5 1.3 %collective-permute-start.11 = (f32[4,16,2,128]{3,2,1,0:T(2,128)S(1)}, f32[4,16,2,128]{3,2,1,0:T(2,128)S(1)}, u32[]{:S(2)}, u32[]{:S(2)}) collective-permute-start(f32[4,16,2,128]{3,2,1,0:T(2,128)S(1)} %get-tuple-element.19), channel_id=1, source_target_pairs={{4,0},{8,4},{12,8},{16,12},{20,16},{24,20},{28,24},{5,1},{9,5},{13... | collective-permute-start | bytes 196616 | tf_op jit(solution)/shard_map/ppermute | solution.py:232
  88.9 3.8 %collective-permute-done.11 = f32[4,16,2,128]{3,2,1,0:T(2,128)S(1)} collective-permute-done((f32[4,16,2,128]{3,2,1,0:T(2,128)S(1)}, f32[4,16,2,128]{3,2,1,0:T(2,128)S(1)}, u32[]{:S(2)}, u32[]{:S(2)}) %collective-permute-start.11) | collective-permute-done | bytes 65568 | tf_op jit(solution)/shard_map/ppermute | solution.py:232
  (38 shorter events, 5.6 us)
Async XLA Ops:
  0.6 13.0 %copy-start = (f32[4,16,16,128]{3,2,1,0:T(8,128)S(1)}, f32[4,16,16,128]{3,2,1,0:T(8,128)}, u32[]{:S(2)}) copy-start(f32[4,16,16,128]{3,2,1,0:T(8,128)} %gas_ref.1) | copy-start | bytes 1572868
  1.8 11.8 %collective-permute-start = (f32[4,16,2,128]{3,2,1,0:T(2,128)S(1)}, f32[4,16,2,128]{3,2,1,0:T(2,128)S(1)}, u32[]{:S(2)}, u32[]{:S(2)}) collective-permute-start(f32[4,16,2,128]{3,2,1,0:T(2,128)S(1)} %get-tuple-element.35), channel_id=1, source_target_pairs={{0,4},{4,8},{8,12},{12,16},{16,20},{20,24},{24,28},{1,5},{5,9},{9,... | collective-permute-start | bytes 196616 | tf_op jit(solution)/shard_map/ppermute | solution.py:232
  6.6 7.0 %collective-permute-start.1 = (f32[4,16,2,128]{3,2,1,0:T(2,128)S(1)}, f32[4,16,2,128]{3,2,1,0:T(2,128)S(1)}, u32[]{:S(2)}, u32[]{:S(2)}) collective-permute-start(f32[4,16,2,128]{3,2,1,0:T(2,128)S(1)} %get-tuple-element.34), channel_id=1, source_target_pairs={{4,0},{8,4},{12,8},{16,12},{20,16},{24,20},{28,24},{5,1},{9,5},{13... | collective-permute-start | bytes 196616 | tf_op jit(solution)/shard_map/ppermute | solution.py:232
  7.9 0.9 copy-start.1
  8.8 0.9 copy-start.2
  9.7 0.7 copy-start.3
  10.4 0.7 copy-start.4
  11.1 0.7 copy-start.5
  14.0 34.1 %copy-start.6 = (f32[128,128]{1,0:T(8,128)S(1)}, f32[128,128]{1,0:T(8,128)}, u32[]{:S(2)}) copy-start(f32[128,128]{1,0:T(8,128)} %param.12) | copy-start | bytes 196612
  14.0 44.7 %all-to-all-start = ((f32[128,1,1408]{2,1,0:T(1,128)}), f32[128,1,1408]{2,1,0:T(1,128)S(1)}, u32[]{:S(2)}, u32[]{:S(2)}) async-start(f32[128,1,1408]{2,1,0:T(1,128)} %bitcast.4), calls=%async_computation | async-start | bytes 1441792 | tf_op jit(solution)/shard_map/all_to_all | solution.py:290
  33.5 4.5 %collective-permute-start.2 = (f32[16,2,128]{2,1,0:T(2,128)S(1)}, f32[16,2,128]{2,1,0:T(2,128)S(1)}, u32[]{:S(2)}, u32[]{:S(2)}) collective-permute-start(f32[16,2,128]{2,1,0:T(2,128)S(1)} %get-tuple-element.31), channel_id=1, source_target_pairs={{0,1},{1,2},{2,3},{4,5},{5,6},{6,7},{8,9},{9,10},{10,11},{12,13},{... | collective-permute-start | bytes 49160 | tf_op jit(solution)/shard_map/ppermute | solution.py:232
  36.7 4.8 %collective-permute-start.3 = (f32[16,2,128]{2,1,0:T(2,128)S(1)}, f32[16,2,128]{2,1,0:T(2,128)S(1)}, u32[]{:S(2)}, u32[]{:S(2)}) collective-permute-start(f32[16,2,128]{2,1,0:T(2,128)S(1)} %get-tuple-element.30), channel_id=1, source_target_pairs={{1,0},{2,1},{3,2},{5,4},{6,5},{7,6},{9,8},{10,9},{11,10},{13,12},{... | collective-permute-start | bytes 49160 | tf_op jit(solution)/shard_map/ppermute | solution.py:232
  41.5 8.0 %collective-permute-start.4 = (f32[2,144,128]{2,1,0:T(8,128)S(1)}, f32[2,144,128]{2,1,0:T(8,128)S(1)}, u32[]{:S(2)}, u32[]{:S(2)}) collective-permute-start(f32[2,144,128]{2,1,0:T(8,128)S(1)} %concatenate.15), channel_id=1, source_target_pairs={{0,32},{32,64},{64,96},{96,128},{128,160},{160,192},{192,224},{224... | collective-permute-start | bytes 442376 | tf_op jit(solution)/shard_map/ppermute | solution.py:232
  46.2 6.7 %collective-permute-start.5 = (f32[2,144,128]{2,1,0:T(8,128)S(1)}, f32[2,144,128]{2,1,0:T(8,128)S(1)}, u32[]{:S(2)}, u32[]{:S(2)}) collective-permute-start(f32[2,144,128]{2,1,0:T(8,128)S(1)} %concatenate.16), channel_id=1, source_target_pairs={{32,0},{64,32},{96,64},{128,96},{160,128},{192,160},{224,192},{256... | collective-permute-start | bytes 442376 | tf_op jit(solution)/shard_map/ppermute | solution.py:232
  69.0 4.4 %collective-permute-start.6 = (f32[2,144,128]{2,1,0:T(8,128)S(1)}, f32[2,144,128]{2,1,0:T(8,128)S(1)}, u32[]{:S(2)}, u32[]{:S(2)}) collective-permute-start(f32[2,144,128]{2,1,0:T(8,128)S(1)} %bitcast.24), channel_id=1, source_target_pairs={{0,32},{32,64},{64,96},{96,128},{128,160},{160,192},{192,224},{224... | collective-permute-start | bytes 442376 | tf_op jit(solution)/shard_map/ppermute | solution.py:232
  70.9 6.5 %collective-permute-start.7 = (f32[2,144,128]{2,1,0:T(8,128)S(1)}, f32[2,144,128]{2,1,0:T(8,128)S(1)}, u32[]{:S(2)}, u32[]{:S(2)}) collective-permute-start(f32[2,144,128]{2,1,0:T(8,128)S(1)} %bitcast.23), channel_id=1, source_target_pairs={{32,0},{64,32},{96,64},{128,96},{160,128},{192,160},{224,192},{256... | collective-permute-start | bytes 442376 | tf_op jit(solution)/shard_map/ppermute | solution.py:232
  77.4 5.1 %collective-permute-start.8 = (f32[16,2,128]{2,1,0:T(2,128)S(1)}, f32[16,2,128]{2,1,0:T(2,128)S(1)}, u32[]{:S(2)}, u32[]{:S(2)}) collective-permute-start(f32[16,2,128]{2,1,0:T(2,128)S(1)} %pad_maximum_fusion.1), channel_id=1, source_target_pairs={{0,1},{1,2},{2,3},{4,5},{5,6},{6,7},{8,9},{9,10},{10,11},{12,13},{... | collective-permute-start | bytes 49160 | tf_op jit(solution)/shard_map/ppermute | solution.py:232
  80.5 4.5 %collective-permute-start.9 = (f32[16,2,128]{2,1,0:T(2,128)S(1)}, f32[16,2,128]{2,1,0:T(2,128)S(1)}, u32[]{:S(2)}, u32[]{:S(2)}) collective-permute-start(f32[16,2,128]{2,1,0:T(2,128)S(1)} %pad_maximum_fusion.2), channel_id=1, source_target_pairs={{1,0},{2,1},{3,2},{5,4},{6,5},{7,6},{9,8},{10,9},{11,10},{13,12},{... | collective-permute-start | bytes 49160 | tf_op jit(solution)/shard_map/ppermute | solution.py:232
  85.4 3.5 %collective-permute-start.10 = (f32[4,16,2,128]{3,2,1,0:T(2,128)S(1)}, f32[4,16,2,128]{3,2,1,0:T(2,128)S(1)}, u32[]{:S(2)}, u32[]{:S(2)}) collective-permute-start(f32[4,16,2,128]{3,2,1,0:T(2,128)S(1)} %get-tuple-element.18), channel_id=1, source_target_pairs={{0,4},{4,8},{8,12},{12,16},{16,20},{20,24},{24,28},{1,5},{5,9},{9,... | collective-permute-start | bytes 196616 | tf_op jit(solution)/shard_map/ppermute | solution.py:232
  87.5 5.2 %collective-permute-start.11 = (f32[4,16,2,128]{3,2,1,0:T(2,128)S(1)}, f32[4,16,2,128]{3,2,1,0:T(2,128)S(1)}, u32[]{:S(2)}, u32[]{:S(2)}) collective-permute-start(f32[4,16,2,128]{3,2,1,0:T(2,128)S(1)} %get-tuple-element.19), channel_id=1, source_target_pairs={{4,0},{8,4},{12,8},{16,12},{20,16},{24,20},{28,24},{5,1},{9,5},{13... | collective-permute-start | bytes 196616 | tf_op jit(solution)/shard_map/ppermute | solution.py:232

commit v2 on v1

--- a/solution.py
+++ b/solution.py
@@ -13,6 +13,7 @@
 HI = lax.Precision.HIGHEST
 
 LANES = 128
+NEARLY_ALL = 66200000
 ROWS = 11
 ZR = 144
 ZO = 8
@@ -23,8 +24,14 @@
     return lax.broadcasted_iota(jnp.int32, shape, dim)
 
 
-def pack_kernel(tgt_ref, off_ref, cnt_ref, vel_ref, prop_ref, out_ref):
+def pack_kernel(tgt_hbm, off_hbm, cnt_hbm, vel_hbm, prop_hbm, out_ref, tgt_ref, off_ref, cnt_ref, vel_ref, prop_ref, sems):
     n = LANES
+    pairs = ((tgt_hbm, tgt_ref), (off_hbm, off_ref), (cnt_hbm, cnt_ref), (vel_hbm, vel_ref), (prop_hbm, prop_ref))
+    copies = [pltpu.make_async_copy(src, dst, sems.at[i]) for i, (src, dst) in enumerate(pairs)]
+    for copy in copies:
+        copy.start()
+    for copy in copies:
+        copy.wait()
     hot = (iota((n, n), 0) == tgt_ref[...]).astype(F32)
     earlier = (iota((n, n), 0) < iota((n, n), 1)).astype(BF16)
     rank = jnp.dot(hot.astype(BF16), earlier, preferred_element_type=F32)
@@ -50,43 +57,40 @@
         out_ref[pl.ds(5 + k, n, stride=ROWS), :] = total[n:]
 
 
-def turn_kernel(gas_ref, low_ref, high_ref, send_ref, out_ref, same_ref, buf):
-    del send_ref, same_ref
+def turn_kernel(gas_ref, xl_ref, xh_ref, yl_ref, yh_ref, out_ref, buf):
     cells_x, cells_y = gas_ref.shape[1], gas_ref.shape[2]
     buf[...] = jnp.zeros_like(buf)
-    for x in range(cells_x):
+    for x in range(cells_x + 4):
+        ref, at = (xl_ref, x) if x < 2 else (gas_ref, x - 2) if x < cells_x + 2 else (xh_ref, x - cells_x - 2)
         for k in range(4):
-            buf[x, k * YS : k * YS + 2, :] = low_ref[k, x]
-            buf[x, k * YS + 2 : k * YS + 2 + cells_y, :] = gas_ref[k, x]
-            buf[x, k * YS + 2 + cells_y : k * YS + 4 + cells_y, :] = high_ref[k, x]
-    for x in range(cells_x):
+            buf[x, k * YS : k * YS + 2, :] = yl_ref[k, x]
+            buf[x, k * YS + 2 : k * YS + 2 + cells_y, :] = ref[k, at]
+            buf[x, k * YS + 2 + cells_y : k * YS + 4 + cells_y, :] = yh_ref[k, x]
+    for x in range(cells_x + 4):
         out_ref[x] = buf[x].T
 
 
-def diffuse_kernel(mid_ref, zl_ref, zh_ref, xl_ref, xh_ref, out_ref, col):
-    cells_x, cells_z = mid_ref.shape[0], mid_ref.shape[1]
+def diffuse_kernel(mid_ref, zl_ref, zh_ref, out_ref, col):
+    cells_x, cells_z = out_ref.shape[0], out_ref.shape[1]
     last = ZO + cells_z
     lane = iota((cells_z, LANES), 1)
     rate = jnp.where(lane < 3 * YS, TIME_STEP, 0.5 * TIME_STEP).astype(F32)
-    for x in range(cells_x):
+    for x in range(2, cells_x + 2):
         here = mid_ref[x]
         col[x % 2, ZO:last, :] = here
         col[x % 2, ZO - 2 : ZO, :] = zl_ref[x]
         col[x % 2, last : last + 2, :] = zh_ref[x]
-        left = mid_ref[x - 1] if x else xl_ref[1, ZO:last, :]
-        right = mid_ref[x + 1] if x < cells_x - 1 else xh_ref[0, ZO:last, :]
-        beside = left + right + pltpu.roll(here, LANES - 1, 1) + pltpu.roll(here, 1, 1)
+        beside = mid_ref[x - 1] + mid_ref[x + 1] + pltpu.roll(here, LANES - 1, 1) + pltpu.roll(here, 1, 1)
         beside = beside + col[x % 2, ZO + 1 : last + 1, :] + col[x % 2, ZO - 1 : last - 1, :]
-        out_ref[x] = here + rate * (beside - 6.0 * here)
+        out_ref[x - 2] = here + rate * (beside - 6.0 * here)
 
 
 def parcel_kernel(
-    recv_ref, mid_ref, zl_ref, zh_ref, xl_ref, xh_ref, w_ref,
+    recv_ref, mid_ref, zl_ref, zh_ref, w_ref,
     pay_ref, sum_ref, xlo_ref, xhi_ref,
-    code_v, code_s, pad, acc, near, force, sem,
+    code_v, code_s, pad, acc, more, near, force, sem,
 ):
-    cells_x, cells_z = mid_ref.shape[0], mid_ref.shape[1]
-    planes = cells_x + 4
+    planes, cells_z = mid_ref.shape[0], mid_ref.shape[1]
     last = ZO + cells_z
     n = LANES
     off = recv_ref[pl.ds(10, n, stride=ROWS), :]
@@ -98,15 +102,20 @@
     code_v[...] = code.T[0:8].astype(jnp.int32)
     copy = pltpu.make_async_copy(code_v, code_s, sem)
     copy.start()
-    for p in range(2):
-        pad[p * ZR : (p + 1) * ZR, :] = xl_ref[p]
-        pad[(planes - 2 + p) * ZR : (planes - 1 + p) * ZR, :] = xh_ref[p]
-    for x in range(cells_x):
-        at = (x + 2) * ZR
+    for x in range(planes):
+        at = x * ZR
         pad[at + ZO : at + last, :] = mid_ref[x]
         pad[at + ZO - 2 : at + ZO, :] = zl_ref[x]
         pad[at + last : at + last + 2, :] = zh_ref[x]
     acc[...] = jnp.zeros_like(acc)
+    more[...] = jnp.zeros_like(more)
+    w_hi = w_ref[...].astype(BF16)
+    w_lo = (w_ref[...] - w_hi.astype(F32)).astype(BF16)
+
+    def split(x):
+        hi = x.astype(BF16)
+        return hi, (x - hi.astype(F32)).astype(BF16)
+
     copy.wait()
 
     lane8 = iota((8, n), 1)
@@ -143,7 +152,10 @@
                 cells.append(out)
         near[pl.ds(pl.multiple_of(s * n, n), n), :] = jnp.concatenate(cells, axis=0).T
 
-    gas_all = jnp.dot(near[...], w_ref[...], precision=HI, preferred_element_type=F32)
+    near_hi, near_lo = split(near[...])
+    gas_all = jnp.dot(
+        jnp.concatenate([near_hi, near_lo], axis=1), jnp.concatenate([w_hi, w_hi], axis=0), preferred_element_type=F32
+    ) + jnp.dot(near_hi, w_lo, preferred_element_type=F32)
     for s in range(8):
         rank, q0 = s // 4, (s % 4) * YS
         row = q0 * ROWS + rank * 5
@@ -167,14 +179,15 @@
         pay_ref[3, slots, :] = mass
         pay_ref[4, slots, :] = jnp.where(alive, relax, 0.0)
         force[s * n + 3 * YS : (s + 1) * n, :] = mass
+    across = (((1,), (1,)), ((), ()))
     for s in range(8):
+        f_hi, f_lo = split(force[s * n : (s + 1) * n, :])
         near[s * n : (s + 1) * n, :] = lax.dot_general(
-            w_ref[...],
-            force[s * n : (s + 1) * n, :],
-            (((1,), (1,)), ((), ())),
-            precision=HI,
+            jnp.concatenate([w_hi, w_lo], axis=1),
+            jnp.concatenate([f_hi, f_hi], axis=1),
+            across,
             preferred_element_type=F32,
-        )
+        ) + lax.dot_general(w_hi, f_lo, across, preferred_element_type=F32)
 
     @pl.loop(0, 8)
     def _(s):
@@ -188,18 +201,23 @@
                     x = pltpu.roll(x, (e - g) % n, 1) if e != g else x
                     out = x if out is None else jnp.where(quad == e, x, out)
                 parts.append(out)
-            for b8 in range(8):
-                at, oy_b = place(s, b8 * 4 + g)
-                shift = jnp.bitwise_and(oy_b - 4 * b8, n - 1)
-                mine = group == b8
-                adds = [pltpu.roll(jnp.where(mine, parts[a], 0.0), shift, 1) for a in range(4)]
-                olds = [acc[pl.ds(at + a * ZR, 8), :] for a in range(4)]
-                for a in range(4):
-                    acc[pl.ds(at + a * ZR, 8), :] = olds[a] + adds[a]
-
-    sum_ref[...] = acc[2 * ZR : (planes - 2) * ZR, :]
-    xlo_ref[...] = acc[0 : 2 * ZR, :]
-    xhi_ref[...] = acc[(planes - 2) * ZR :, :]
+            for b8 in range(0, 8, 2):
+                work = []
+                for half, sums in enumerate((acc, more)):
+                    at, oy_b = place(s, (b8 + half) * 4 + g)
+                    shift = jnp.bitwise_and(oy_b - 4 * (b8 + half), n - 1)
+                    mine = group == b8 + half
+                    for a in range(4):
+                        add = pltpu.roll(jnp.where(mine, parts[a], 0.0), shift, 1)
+                        work.append((sums, pl.ds(at + a * ZR, 8), add))
+                olds = [sums[rows, :] for sums, rows, _ in work]
+                for (sums, rows, add), old in zip(work, olds):
+                    sums[rows, :] = old + add
+
+    low, high = 2 * ZR, (planes - 2) * ZR
+    sum_ref[...] = acc[low:high, :] + more[low:high, :]
+    xlo_ref[...] = acc[0:low, :] + more[0:low, :]
+    xhi_ref[...] = acc[high:, :] + more[high:, :]
 
 
 def back_kernel(sum_ref, base_ref, xl_ref, xh_ref, zl_ref, zh_ref, out_ref, ylo_ref, yhi_ref, buf):
@@ -225,20 +243,25 @@
             yhi_ref[k, x] = flat[k * YS + 2 + cells_y : k * YS + 4 + cells_y]
 
 
-def shift_pair(to_low, to_high, axis):
+def shift_pair(to_low, to_high, axis, ring=False):
     count = lax.axis_size(axis)
-    up = [(i, i + 1) for i in range(count - 1)]
+    if not ring:
+        up = [(i, i + 1) for i in range(count - 1)]
+        down = [(j, i) for i, j in up]
+        return lax.ppermute(to_high, axis, up), lax.ppermute(to_low, axis, down)
+    up = [(i, (i + 1) % count) for i in range(count)]
     down = [(j, i) for i, j in up]
-    return lax.ppermute(to_high, axis, up), lax.ppermute(to_low, axis, down)
-
-
-def call(kernel, outs, scratch=(), cost=None, **kw):
+    here = lax.axis_index(axis)
+    low, high = lax.ppermute(to_high, axis, up), lax.ppermute(to_low, axis, down)
+    return jnp.where(here > 0, low, 0.0), jnp.where(here < count - 1, high, 0.0)
+
+
+def call(kernel, outs, scratch=(), vmem=40 * 2**20, **kw):
     return pl.pallas_call(
         kernel,
         out_shape=outs,
         scratch_shapes=list(scratch),
-        compiler_params=pltpu.CompilerParams(vmem_limit_bytes=40 * 2**20),
-        cost_estimate=cost,
+        compiler_params=pltpu.CompilerParams(vmem_limit_bytes=vmem),
         **kw,
     )
 
@@ -247,8 +270,8 @@
     return jax.ShapeDtypeStruct(shape, dtype)
 
 
-def parcels(recv, mid, z_low, z_high, x_low, x_high, weight):
-    nx = mid.shape[0]
+def parcels(recv, mid, z_low, z_high, weight):
+    nx = mid.shape[0] - 4
     blocks = recv.shape[0] // ROWS
     rows = (nx + 4) * ZR
     return call(
@@ -259,52 +282,57 @@
             pltpu.SMEM((8, LANES), jnp.int32),
             pltpu.VMEM((rows, LANES), F32),
             pltpu.VMEM((rows, LANES), F32),
+            pltpu.VMEM((rows, LANES), F32),
             pltpu.VMEM((8 * LANES, LANES), F32),
             pltpu.VMEM((8 * LANES, LANES), F32),
             pltpu.SemaphoreType.DMA,
         ],
-    )(recv, mid, z_low, z_high, x_low, x_high, weight)
+    )(recv, mid, z_low, z_high, weight)
 
 
 def per_device(parcel_vel, parcel_props, fill_count, owner_peer, cell_offset, shell_weight, gas_state):
     _, nx, ny, nz = gas_state.shape
     blocks = parcel_vel.shape[0]
-    send = call(pack_kernel, arr(blocks * ROWS, LANES))(
+    x_low, x_high = shift_pair(gas_state[:, :2], gas_state[:, nx - 2 :], "gx", ring=True)
+    send = call(
+        pack_kernel,
+        arr(blocks * ROWS, LANES),
+        [pltpu.VMEM((1, blocks), jnp.int32)] * 3
+        + [
+            pltpu.VMEM((3, blocks, LANES), F32),
+            pltpu.VMEM((blocks, 2, LANES), F32),
+            pltpu.SemaphoreType.DMA((5,)),
+        ],
+        in_specs=[pl.BlockSpec(memory_space=pltpu.HBM)] * 5,
+        vmem=NEARLY_ALL,
+    )(
         owner_peer.reshape(1, blocks),
         cell_offset.reshape(1, blocks),
         fill_count.reshape(1, blocks),
         parcel_vel.transpose(1, 0, 2),
         parcel_props,
     )
-    y_low, y_high = shift_pair(gas_state[:, :, :2], gas_state[:, :, ny - 2 :], "gy")
-    whole = pl.BlockSpec(memory_space=pltpu.VMEM)
-    where = pl.BlockSpec(memory_space=pl.ANY)
-    mid, send = call(
-        turn_kernel,
-        [arr(nx, nz, LANES), arr(blocks * ROWS, LANES)],
-        [pltpu.VMEM((nx, LANES, nz), F32)],
-        in_specs=[whole, whole, whole, where],
-        out_specs=[whole, where],
-        input_output_aliases={3: 1},
-    )(gas_state, y_low, y_high, send)
+    send, x_low, x_high = lax.optimization_barrier((send, x_low, x_high))
+
+    def y_face(lo):
+        return jnp.concatenate([x_low[:, :, lo : lo + 2], gas_state[:, :, lo : lo + 2], x_high[:, :, lo : lo + 2]], axis=1)
+
+    y_lo, y_hi = y_face(0), y_face(ny - 2)
     recv = lax.all_to_all(
         send.reshape(blocks, ROWS * LANES), ("gx", "gy"), split_axis=0, concat_axis=0, tiled=True
     ).reshape(blocks * ROWS, LANES)
-    z_low, z_high = shift_pair(mid[:, :2], mid[:, nz - 2 :], "gz")
-
-    def face(lo, hi):
-        zero = jnp.zeros((2, ZO - 2, LANES), F32)
-        return jnp.concatenate([zero, z_low[lo:hi], mid[lo:hi], z_high[lo:hi], zero], axis=1)
-
-    x_low, x_high = shift_pair(face(0, 2), face(nx - 2, nx), "gx")
-    halo = (mid, z_low, z_high, x_low, x_high)
+    y_low, y_high = shift_pair(y_lo, y_hi, "gy")
+    mid = call(turn_kernel, arr(nx + 4, nz, LANES), [pltpu.VMEM((nx + 4, LANES, nz), F32)])(
+        gas_state, x_low, x_high, y_low, y_high
+    )
+    halo = (mid, *shift_pair(mid[:, :2], mid[:, nz - 2 :], "gz"))
 
     weight = shell_weight.reshape(LANES, 4, 4, 8).transpose(2, 1, 3, 0).reshape(LANES, LANES)
     pay, total, x_lo, x_hi = parcels(recv, *halo, weight)
     parcels_next = pay.transpose(1, 0, 2)
     base = call(diffuse_kernel, arr(nx, nz, LANES), [pltpu.VMEM((2, ZR, LANES), F32)])(*halo)
 
-    from_low, from_high = shift_pair(x_lo.reshape(2, ZR, LANES), x_hi.reshape(2, ZR, LANES), "gx")
+    from_low, from_high = shift_pair(x_lo.reshape(2, ZR, LANES), x_hi.reshape(2, ZR, LANES), "gx", ring=True)
     total = total.reshape(nx, ZR, LANES)
 
     def rim(lo, hi):

time: 94.3 us -> 88.5 us (0.938)
  the two profiles are of different devices: /device:TPU:1 before, /device:TPU:25 now
where the time goes in v2:
time: 88.5 us; the launch traced here: 88 us
  starting transfers between devices  39.7 us (45%)
  waiting for transfers between devices  32.3 us (36%)
  Pallas kernels  12.9 us (15%)
  other arithmetic  1.13 us (1%)
  local copies, waits for them, and re-layouts  1.12 us (1%)
  between operations  0.92 us (1%)
    ppermute x8, waiting for transfers between devices, shift_pair(): return (lax.ppermute(to_high, axis, up), lax.ppermute(to_low, axis, down))  24.7 us
    ppermute x8, starting transfers between devices, shift_pair(): return (lax.ppermute(to_high, axis, up), lax.ppermute(to_low, axis, down))  17.2 us
    all_to_all x1, starting transfers between devices, per_device(): lax.all_to_all(send.reshape(blocks, ROWS * LANES), ('gx', 'gy'), split_ax...  15.7 us
    pallas_call x1, Pallas kernels, parcels(): call(parcel_kernel, [arr(5, 2 * blocks, LANES), arr(nx * ZR, LANES), arr(...  8.34 us
    ppermute x2, starting transfers between devices, shift_pair(): lax.ppermute(to_high, axis, up)  6.8 us
    ppermute x2, waiting for transfers between devices, shift_pair(): lax.ppermute(to_low, axis, down)  5.52 us
    pallas_call x1, Pallas kernels, per_device(): call(pack_kernel, arr(blocks * ROWS, LANES), [pltpu.VMEM((1, blocks), jnp...  3 us
    ppermute x2, waiting for transfers between devices, shift_pair(): lax.ppermute(to_high, axis, up)  2.09 us
  transfers between devices with their start and end apart: 13, of which 8 were waited for; matrix products, arithmetic and copies ran while one was open for 0% of the time, Pallas kernels for 5%

profile of v2, /device:TPU:25, one launch (start us, length us, event | category | flops | bytes accessed | tf_op | source)
XLA Modules:
  0.0 88.0 jit_solution(11926829229772818288)
XLA Ops:
  0.6 0.9 %fusion.3 = (f32[4,2,16,128]{3,2,1,0:T(8,128)S(1)}, f32[4,2,16,128]{3,2,1,0:T(8,128)S(1)}) fusion(f32[4,16,16,128]{3,2,1,0:T(8,128)} %gas_ref.1), kind=kLoop, calls=%fused_computation.18 | loop fusion | bytes 262144 | tf_op jit(solution)/shard_map/slice | solution.py:296
  1.5 3.1 %collective-permute-start = (f32[4,2,16,128]{3,2,1,0:T(8,128)S(1)}, f32[4,2,16,128]{3,2,1,0:T(8,128)S(1)}, u32[]{:S(2)}, u32[]{:S(2)}) collective-permute-start(f32[4,2,16,128]{3,2,1,0:T(8,128)S(1)} %get-tuple-element.37), channel_id=1, source_target_pairs={{0,32},{32,64},{64,96},{96,128},{128,160},{160,192},{192,224},{224... | collective-permute-start | bytes 196616 | tf_op jit(solution)/shard_map/ppermute | solution.py:255
  4.6 3.0 %shard_map.86 = f32[1408,128]{1,0:T(8,128)} custom-call(s32[1,128]{1,0:T(1,128)} %bitcast.24, s32[1,128]{1,0:T(1,128)} %bitcast.25, s32[1,128]{1,0:T(1,128)} %bitcast.26, f32[3,128,128]{2,1,0:T(8,128)} %bitcast.23, f32[128,2,128]{2,1,0:T(2,128)} %prop_hbm.1), custom_call_target="tpu_custom_call" | custom-call | tf_op jit(solution)/shard_map/pallas_call | solution.py:297
  7.6 1.9 %collective-permute-done.1 = f32[4,2,16,128]{3,2,1,0:T(8,128)S(1)} collective-permute-done((f32[4,2,16,128]{3,2,1,0:T(8,128)S(1)}, f32[4,2,16,128]{3,2,1,0:T(8,128)S(1)}, u32[]{:S(2)}, u32[]{:S(2)}) %collective-permute-start.1) | collective-permute-done | bytes 65568 | tf_op jit(solution)/shard_map/ppermute | solution.py:255
  9.5 15.7 %all-to-all-start = ((f32[128,1,1408]{2,1,0:T(1,128)}), f32[128,1,1408]{2,1,0:T(1,128)S(1)}, u32[]{:S(2)}, u32[]{:S(2)}) async-start(f32[128,1,1408]{2,1,0:T(1,128)} %bitcast.21), calls=%async_computation | async-start | bytes 1441792 | tf_op jit(solution)/shard_map/all_to_all | solution.py:321
  25.4 3.1 %collective-permute-start.2 = (f32[4,20,2,128]{3,2,1,0:T(2,128)S(1)}, f32[4,20,2,128]{3,2,1,0:T(2,128)S(1)}, u32[]{:S(2)}, u32[]{:S(2)}) collective-permute-start(f32[4,20,2,128]{3,2,1,0:T(2,128)S(1)} %pad_maximum_fusion.1), channel_id=1, source_target_pairs={{0,4},{4,8},{8,12},{12,16},{16,20},{20,24},{24,28},{1,5},{5,9},{9,... | collective-permute-start | bytes 245768 | tf_op jit(solution)/shard_map/ppermute | solution.py:251
  28.6 1.3 %collective-permute-start.3 = (f32[4,20,2,128]{3,2,1,0:T(2,128)S(1)}, f32[4,20,2,128]{3,2,1,0:T(2,128)S(1)}, u32[]{:S(2)}, u32[]{:S(2)}) collective-permute-start(f32[4,20,2,128]{3,2,1,0:T(2,128)S(1)} %pad_maximum_fusion.2), channel_id=1, source_target_pairs={{4,0},{8,4},{12,8},{16,12},{20,16},{24,20},{28,24},{5,1},{9,5},{13... | collective-permute-start | bytes 245768 | tf_op jit(solution)/shard_map/ppermute | solution.py:251
  29.9 10.6 %collective-permute-done.2.yl_ref = f32[4,20,2,128]{3,2,1,0:T(2,128)S(1)} collective-permute-done((f32[4,20,2,128]{3,2,1,0:T(2,128)S(1)}, f32[4,20,2,128]{3,2,1,0:T(2,128)S(1)}, u32[]{:S(2)}, u32[]{:S(2)}) %collective-permute-start.2) | collective-permute-done | bytes 81952 | tf_op jit(solution)/shard_map/ppermute | solution.py:251
  40.5 4.2 %collective-permute-done.3.yh_ref = f32[4,20,2,128]{3,2,1,0:T(2,128)S(1)} collective-permute-done((f32[4,20,2,128]{3,2,1,0:T(2,128)S(1)}, f32[4,20,2,128]{3,2,1,0:T(2,128)S(1)}, u32[]{:S(2)}, u32[]{:S(2)}) %collective-permute-start.3) | collective-permute-done | bytes 81952 | tf_op jit(solution)/shard_map/ppermute | solution.py:251
  45.2 3.1 %collective-permute-start.4 = (f32[20,2,128]{2,1,0:T(2,128)S(1)}, f32[20,2,128]{2,1,0:T(2,128)S(1)}, u32[]{:S(2)}, u32[]{:S(2)}) collective-permute-start(f32[20,2,128]{2,1,0:T(2,128)S(1)} %get-tuple-element.27), channel_id=1, source_target_pairs={{0,1},{1,2},{2,3},{4,5},{5,6},{6,7},{8,9},{9,10},{10,11},{12,13},{... | collective-permute-start | bytes 61448 | tf_op jit(solution)/shard_map/ppermute | solution.py:251
  48.3 1.3 %collective-permute-start.5 = (f32[20,2,128]{2,1,0:T(2,128)S(1)}, f32[20,2,128]{2,1,0:T(2,128)S(1)}, u32[]{:S(2)}, u32[]{:S(2)}) collective-permute-start(f32[20,2,128]{2,1,0:T(2,128)S(1)} %get-tuple-element.26), channel_id=1, source_target_pairs={{1,0},{2,1},{3,2},{5,4},{6,5},{7,6},{9,8},{10,9},{11,10},{13,12},{... | collective-permute-start | bytes 61448 | tf_op jit(solution)/shard_map/ppermute | solution.py:251
  49.7 3.1 %collective-permute-done.5.zh_ref = f32[20,2,128]{2,1,0:T(2,128)S(1)} collective-permute-done((f32[20,2,128]{2,1,0:T(2,128)S(1)}, f32[20,2,128]{2,1,0:T(2,128)S(1)}, u32[]{:S(2)}, u32[]{:S(2)}) %collective-permute-start.5) | collective-permute-done | bytes 20512 | tf_op jit(solution)/shard_map/ppermute | solution.py:251
  52.8 8.3 %shard_map.88 = (f32[5,256,128]{2,1,0:T(8,128)}, f32[2304,128]{1,0:T(8,128)S(1)}, f32[288,128]{1,0:T(8,128)S(1)}, f32[288,128]{1,0:T(8,128)S(1)}) custom-call(f32[1408,128]{1,0:T(8,128)S(1)} %bitcast.14, f32[20,128,128]{2,1,0:T(8,128)S(1)} %shard_map.87.mid_ref, f32[20,2,128]{2,1,0:T(2,128)S(1)} %collective-permute-done.4.zl_ref, ...), custom_call_target="tpu_custom_call" | custom-call | tf_op jit(solution)/shard_map/pallas_call | solution.py:277
  61.2 3.7 %collective-permute-start.6 = (f32[2,144,128]{2,1,0:T(8,128)S(1)}, f32[2,144,128]{2,1,0:T(8,128)S(1)}, u32[]{:S(2)}, u32[]{:S(2)}) collective-permute-start(f32[2,144,128]{2,1,0:T(8,128)S(1)} %bitcast.20), channel_id=1, source_target_pairs={{0,32},{32,64},{64,96},{96,128},{128,160},{160,192},{192,224},{224... | collective-permute-start | bytes 442376 | tf_op jit(solution)/shard_map/ppermute | solution.py:255
  64.9 2.1 %collective-permute-done.6 = f32[2,144,128]{2,1,0:T(8,128)S(1)} collective-permute-done((f32[2,144,128]{2,1,0:T(8,128)S(1)}, f32[2,144,128]{2,1,0:T(8,128)S(1)}, u32[]{:S(2)}, u32[]{:S(2)}) %collective-permute-start.6) | collective-permute-done | bytes 147488 | tf_op jit(solution)/shard_map/ppermute | solution.py:255
  67.0 3.7 %collective-permute-done.7 = f32[2,144,128]{2,1,0:T(8,128)S(1)} collective-permute-done((f32[2,144,128]{2,1,0:T(8,128)S(1)}, f32[2,144,128]{2,1,0:T(8,128)S(1)}, u32[]{:S(2)}, u32[]{:S(2)}) %collective-permute-start.7) | collective-permute-done | bytes 147488 | tf_op jit(solution)/shard_map/ppermute | solution.py:255
  70.7 3.1 %collective-permute-start.8 = (f32[16,2,128]{2,1,0:T(2,128)S(1)}, f32[16,2,128]{2,1,0:T(2,128)S(1)}, u32[]{:S(2)}, u32[]{:S(2)}) collective-permute-start(f32[16,2,128]{2,1,0:T(2,128)S(1)} %pad_maximum_fusion.3), channel_id=1, source_target_pairs={{0,1},{1,2},{2,3},{4,5},{5,6},{6,7},{8,9},{9,10},{10,11},{12,13},{... | collective-permute-start | bytes 49160 | tf_op jit(solution)/shard_map/ppermute | solution.py:251
  73.9 1.3 %collective-permute-start.9 = (f32[16,2,128]{2,1,0:T(2,128)S(1)}, f32[16,2,128]{2,1,0:T(2,128)S(1)}, u32[]{:S(2)}, u32[]{:S(2)}) collective-permute-start(f32[16,2,128]{2,1,0:T(2,128)S(1)} %pad_maximum_fusion.4), channel_id=1, source_target_pairs={{1,0},{2,1},{3,2},{5,4},{6,5},{7,6},{9,8},{10,9},{11,10},{13,12},{... | collective-permute-start | bytes 49160 | tf_op jit(solution)/shard_map/ppermute | solution.py:251
  75.2 0.7 shard_map.89.base_ref
  75.9 2.5 %collective-permute-done.9.zh_ref = f32[16,2,128]{2,1,0:T(2,128)S(1)} collective-permute-done((f32[16,2,128]{2,1,0:T(2,128)S(1)}, f32[16,2,128]{2,1,0:T(2,128)S(1)}, u32[]{:S(2)}, u32[]{:S(2)}) %collective-permute-start.9) | collective-permute-done | bytes 16416 | tf_op jit(solution)/shard_map/ppermute | solution.py:251
  78.7 2.7 %collective-permute-start.10 = (f32[4,16,2,128]{3,2,1,0:T(2,128)S(1)}, f32[4,16,2,128]{3,2,1,0:T(2,128)S(1)}, u32[]{:S(2)}, u32[]{:S(2)}) collective-permute-start(f32[4,16,2,128]{3,2,1,0:T(2,128)S(1)} %get-tuple-element.20), channel_id=1, source_target_pairs={{0,4},{4,8},{8,12},{12,16},{16,20},{20,24},{24,28},{1,5},{5,9},{9,... | collective-permute-start | bytes 196616 | tf_op jit(solution)/shard_map/ppermute | solution.py:251
  81.4 1.3 %collective-permute-start.11 = (f32[4,16,2,128]{3,2,1,0:T(2,128)S(1)}, f32[4,16,2,128]{3,2,1,0:T(2,128)S(1)}, u32[]{:S(2)}, u32[]{:S(2)}) collective-permute-start(f32[4,16,2,128]{3,2,1,0:T(2,128)S(1)} %get-tuple-element.21), channel_id=1, source_target_pairs={{4,0},{8,4},{12,8},{16,12},{20,16},{24,20},{28,24},{5,1},{9,5},{13... | collective-permute-start | bytes 196616 | tf_op jit(solution)/shard_map/ppermute | solution.py:251
  82.8 4.3 %collective-permute-done.11 = f32[4,16,2,128]{3,2,1,0:T(2,128)S(1)} collective-permute-done((f32[4,16,2,128]{3,2,1,0:T(2,128)S(1)}, f32[4,16,2,128]{3,2,1,0:T(2,128)S(1)}, u32[]{:S(2)}, u32[]{:S(2)}) %collective-permute-start.11) | collective-permute-done | bytes 65568 | tf_op jit(solution)/shard_map/ppermute | solution.py:251
  87.2 0.9 %pad_maximum_fusion = f32[4,16,16,128]{3,2,1,0:T(8,128)} fusion(f32[4,16,2,128]{3,2,1,0:T(2,128)S(1)} %get-tuple-element.33, f32[4,16,12,128]{3,2,1,0:T(8,128)S(1)} %slice.98, f32[4,16,2,128]{3,2,1,0:T(2,128)S(1)} %get-tuple-element.32), kind=kLoop, calls=%fused_computation | loop fusion | flops 262144 | bytes 1048576 | tf_op jit(solution)/shard_map/concatenate | solution.py:351
  (30 shorter events, 1.4 us)
Async XLA Ops:
  1.5 6.1 %collective-permute-start = (f32[4,2,16,128]{3,2,1,0:T(8,128)S(1)}, f32[4,2,16,128]{3,2,1,0:T(8,128)S(1)}, u32[]{:S(2)}, u32[]{:S(2)}) collective-permute-start(f32[4,2,16,128]{3,2,1,0:T(8,128)S(1)} %get-tuple-element.37), channel_id=1, source_target_pairs={{0,32},{32,64},{64,96},{96,128},{128,160},{160,192},{192,224},{224... | collective-permute-start | bytes 196616 | tf_op jit(solution)/shard_map/ppermute | solution.py:255
  4.6 4.9 %collective-permute-start.1 = (f32[4,2,16,128]{3,2,1,0:T(8,128)S(1)}, f32[4,2,16,128]{3,2,1,0:T(8,128)S(1)}, u32[]{:S(2)}, u32[]{:S(2)}) collective-permute-start(f32[4,2,16,128]{3,2,1,0:T(8,128)S(1)} %get-tuple-element.36), channel_id=1, source_target_pairs={{32,0},{64,32},{96,64},{128,96},{160,128},{192,160},{224,192},{256... | collective-permute-start | bytes 196616 | tf_op jit(solution)/shard_map/ppermute | solution.py:255
  4.6 20.7 %copy-start = (f32[4,16,16,128]{3,2,1,0:T(8,128)S(1)}, f32[4,16,16,128]{3,2,1,0:T(8,128)}, u32[]{:S(2)}) copy-start(f32[4,16,16,128]{3,2,1,0:T(8,128)} %gas_ref.1) | copy-start | bytes 1572868
  9.5 43.3 %all-to-all-start = ((f32[128,1,1408]{2,1,0:T(1,128)}), f32[128,1,1408]{2,1,0:T(1,128)S(1)}, u32[]{:S(2)}, u32[]{:S(2)}) async-start(f32[128,1,1408]{2,1,0:T(1,128)} %bitcast.21), calls=%async_computation | async-start | bytes 1441792 | tf_op jit(solution)/shard_map/all_to_all | solution.py:321
  25.4 15.1 %collective-permute-start.2 = (f32[4,20,2,128]{3,2,1,0:T(2,128)S(1)}, f32[4,20,2,128]{3,2,1,0:T(2,128)S(1)}, u32[]{:S(2)}, u32[]{:S(2)}) collective-permute-start(f32[4,20,2,128]{3,2,1,0:T(2,128)S(1)} %pad_maximum_fusion.1), channel_id=1, source_target_pairs={{0,4},{4,8},{8,12},{12,16},{16,20},{20,24},{24,28},{1,5},{5,9},{9,... | collective-permute-start | bytes 245768 | tf_op jit(solution)/shard_map/ppermute | solution.py:251
  28.5 21.1 %copy-start.1 = (f32[128,128]{1,0:T(8,128)S(1)}, f32[128,128]{1,0:T(8,128)}, u32[]{:S(2)}) copy-start(f32[128,128]{1,0:T(8,128)} %param.12) | copy-start | bytes 196612
  28.6 16.1 %collective-permute-start.3 = (f32[4,20,2,128]{3,2,1,0:T(2,128)S(1)}, f32[4,20,2,128]{3,2,1,0:T(2,128)S(1)}, u32[]{:S(2)}, u32[]{:S(2)}) collective-permute-start(f32[4,20,2,128]{3,2,1,0:T(2,128)S(1)} %pad_maximum_fusion.2), channel_id=1, source_target_pairs={{4,0},{8,4},{12,8},{16,12},{20,16},{24,20},{28,24},{5,1},{9,5},{13... | collective-permute-start | bytes 245768 | tf_op jit(solution)/shard_map/ppermute | solution.py:251
  45.2 4.5 %collective-permute-start.4 = (f32[20,2,128]{2,1,0:T(2,128)S(1)}, f32[20,2,128]{2,1,0:T(2,128)S(1)}, u32[]{:S(2)}, u32[]{:S(2)}) collective-permute-start(f32[20,2,128]{2,1,0:T(2,128)S(1)} %get-tuple-element.27), channel_id=1, source_target_pairs={{0,1},{1,2},{2,3},{4,5},{5,6},{6,7},{8,9},{9,10},{10,11},{12,13},{... | collective-permute-start | bytes 61448 | tf_op jit(solution)/shard_map/ppermute | solution.py:251
  48.3 4.5 %collective-permute-start.5 = (f32[20,2,128]{2,1,0:T(2,128)S(1)}, f32[20,2,128]{2,1,0:T(2,128)S(1)}, u32[]{:S(2)}, u32[]{:S(2)}) collective-permute-start(f32[20,2,128]{2,1,0:T(2,128)S(1)} %get-tuple-element.26), channel_id=1, source_target_pairs={{1,0},{2,1},{3,2},{5,4},{6,5},{7,6},{9,8},{10,9},{11,10},{13,12},{... | collective-permute-start | bytes 61448 | tf_op jit(solution)/shard_map/ppermute | solution.py:251
  61.2 5.8 %collective-permute-start.6 = (f32[2,144,128]{2,1,0:T(8,128)S(1)}, f32[2,144,128]{2,1,0:T(8,128)S(1)}, u32[]{:S(2)}, u32[]{:S(2)}) collective-permute-start(f32[2,144,128]{2,1,0:T(8,128)S(1)} %bitcast.20), channel_id=1, source_target_pairs={{0,32},{32,64},{64,96},{96,128},{128,160},{160,192},{192,224},{224... | collective-permute-start | bytes 442376 | tf_op jit(solution)/shard_map/ppermute | solution.py:255
  64.9 5.8 %collective-permute-start.7 = (f32[2,144,128]{2,1,0:T(8,128)S(1)}, f32[2,144,128]{2,1,0:T(8,128)S(1)}, u32[]{:S(2)}, u32[]{:S(2)}) collective-permute-start(f32[2,144,128]{2,1,0:T(8,128)S(1)} %bitcast.19), channel_id=1, source_target_pairs={{32,0},{64,32},{96,64},{128,96},{160,128},{192,160},{224,192},{256... | collective-permute-start | bytes 442376 | tf_op jit(solution)/shard_map/ppermute | solution.py:255
  70.7 5.1 %collective-permute-start.8 = (f32[16,2,128]{2,1,0:T(2,128)S(1)}, f32[16,2,128]{2,1,0:T(2,128)S(1)}, u32[]{:S(2)}, u32[]{:S(2)}) collective-permute-start(f32[16,2,128]{2,1,0:T(2,128)S(1)} %pad_maximum_fusion.3), channel_id=1, source_target_pairs={{0,1},{1,2},{2,3},{4,5},{5,6},{6,7},{8,9},{9,10},{10,11},{12,13},{... | collective-permute-start | bytes 49160 | tf_op jit(solution)/shard_map/ppermute | solution.py:251
  73.9 4.5 %collective-permute-start.9 = (f32[16,2,128]{2,1,0:T(2,128)S(1)}, f32[16,2,128]{2,1,0:T(2,128)S(1)}, u32[]{:S(2)}, u32[]{:S(2)}) collective-permute-start(f32[16,2,128]{2,1,0:T(2,128)S(1)} %pad_maximum_fusion.4), channel_id=1, source_target_pairs={{1,0},{2,1},{3,2},{5,4},{6,5},{7,6},{9,8},{10,9},{11,10},{13,12},{... | collective-permute-start | bytes 49160 | tf_op jit(solution)/shard_map/ppermute | solution.py:251
  78.7 4.1 %collective-permute-start.10 = (f32[4,16,2,128]{3,2,1,0:T(2,128)S(1)}, f32[4,16,2,128]{3,2,1,0:T(2,128)S(1)}, u32[]{:S(2)}, u32[]{:S(2)}) collective-permute-start(f32[4,16,2,128]{3,2,1,0:T(2,128)S(1)} %get-tuple-element.20), channel_id=1, source_target_pairs={{0,4},{4,8},{8,12},{12,16},{16,20},{20,24},{24,28},{1,5},{5,9},{9,... | collective-permute-start | bytes 196616 | tf_op jit(solution)/shard_map/ppermute | solution.py:251
  81.4 5.6 %collective-permute-start.11 = (f32[4,16,2,128]{3,2,1,0:T(2,128)S(1)}, f32[4,16,2,128]{3,2,1,0:T(2,128)S(1)}, u32[]{:S(2)}, u32[]{:S(2)}) collective-permute-start(f32[4,16,2,128]{3,2,1,0:T(2,128)S(1)} %get-tuple-element.21), channel_id=1, source_target_pairs={{4,0},{8,4},{12,8},{16,12},{20,16},{24,20},{28,24},{5,1},{9,5},{13... | collective-permute-start | bytes 196616 | tf_op jit(solution)/shard_map/ppermute | solution.py:251

commit v3 on v2

--- a/solution.py
+++ b/solution.py
@@ -57,16 +57,40 @@
         out_ref[pl.ds(5 + k, n, stride=ROWS), :] = total[n:]
 
 
-def turn_kernel(gas_ref, xl_ref, xh_ref, yl_ref, yh_ref, out_ref, buf):
+def fill_rows(buf, gas_ref, xl_ref, xh_ref):
     cells_x, cells_y = gas_ref.shape[1], gas_ref.shape[2]
-    buf[...] = jnp.zeros_like(buf)
     for x in range(cells_x + 4):
         ref, at = (xl_ref, x) if x < 2 else (gas_ref, x - 2) if x < cells_x + 2 else (xh_ref, x - cells_x - 2)
         for k in range(4):
-            buf[x, k * YS : k * YS + 2, :] = yl_ref[k, x]
             buf[x, k * YS + 2 : k * YS + 2 + cells_y, :] = ref[k, at]
-            buf[x, k * YS + 2 + cells_y : k * YS + 4 + cells_y, :] = yh_ref[k, x]
-    for x in range(cells_x + 4):
+
+
+def edge_kernel(gas_ref, xl_ref, xh_ref, lo_ref, hi_ref, buf):
+    cells_z = gas_ref.shape[3]
+    buf[...] = jnp.zeros_like(buf)
+    fill_rows(buf, gas_ref, xl_ref, xh_ref)
+    for x in range(lo_ref.shape[0]):
+        flat = buf[x].T
+        lo_ref[x] = flat[0:2]
+        hi_ref[x] = flat[cells_z - 2 : cells_z]
+
+
+def turn_kernel(gas_ref, xl_ref, xh_ref, zl_ref, zh_ref, yl_ref, yh_ref, out_ref, zlo_ref, zhi_ref, buf):
+    planes, cells_y = out_ref.shape[0], gas_ref.shape[2]
+    buf[...] = jnp.zeros_like(buf)
+    fill_rows(buf, gas_ref, xl_ref, xh_ref)
+    y = iota((2, LANES), 1) % YS
+    for x in range(planes):
+        for k in range(4):
+            row = (k * planes + x) * 2
+            buf[x, k * YS : k * YS + 2, :] = yl_ref[row : row + 2]
+            buf[x, k * YS + 2 + cells_y : k * YS + 4 + cells_y, :] = yh_ref[row : row + 2]
+        for part, (z_ref, o_ref) in enumerate(((zl_ref, zlo_ref), (zh_ref, zhi_ref))):
+            row = (4 + part) * planes * 2 + x * 2
+            below = pltpu.roll(yl_ref[row : row + 2], LANES - cells_y, 1)
+            above = pltpu.roll(yh_ref[row : row + 2], cells_y, 1)
+            o_ref[x] = jnp.where(y < 2, below, jnp.where(y < 2 + cells_y, z_ref[x], jnp.where(y < 4 + cells_y, above, 0.0)))
+    for x in range(planes):
         out_ref[x] = buf[x].T
 
 
@@ -313,19 +337,23 @@
         parcel_props,
     )
     send, x_low, x_high = lax.optimization_barrier((send, x_low, x_high))
-
-    def y_face(lo):
-        return jnp.concatenate([x_low[:, :, lo : lo + 2], gas_state[:, :, lo : lo + 2], x_high[:, :, lo : lo + 2]], axis=1)
-
-    y_lo, y_hi = y_face(0), y_face(ny - 2)
     recv = lax.all_to_all(
         send.reshape(blocks, ROWS * LANES), ("gx", "gy"), split_axis=0, concat_axis=0, tiled=True
     ).reshape(blocks * ROWS, LANES)
-    y_low, y_high = shift_pair(y_lo, y_hi, "gy")
-    mid = call(turn_kernel, arr(nx + 4, nz, LANES), [pltpu.VMEM((nx + 4, LANES, nz), F32)])(
-        gas_state, x_low, x_high, y_low, y_high
+    planes = nx + 4
+    rows_buf = [pltpu.VMEM((planes, LANES, nz), F32)]
+    z_lo, z_hi = call(edge_kernel, [arr(planes, 2, LANES)] * 2, rows_buf)(gas_state, x_low, x_high)
+    z_low, z_high = shift_pair(z_lo, z_hi, "gz")
+
+    def y_face(lo):
+        parts = [part[:, :, lo : lo + 2] for part in (x_low, gas_state, x_high)]
+        face = jnp.concatenate(parts, axis=1).reshape(8 * planes, nz)
+        return jnp.concatenate([face, z_low.reshape(2 * planes, LANES), z_high.reshape(2 * planes, LANES)], axis=0)
+
+    y_low, y_high = shift_pair(y_face(0), y_face(ny - 2), "gy")
+    halo = call(turn_kernel, [arr(planes, nz, LANES), arr(planes, 2, LANES), arr(planes, 2, LANES)], rows_buf)(
+        gas_state, x_low, x_high, z_low, z_high, y_low, y_high
     )
-    halo = (mid, *shift_pair(mid[:, :2], mid[:, nz - 2 :], "gz"))
 
     weight = shell_weight.reshape(LANES, 4, 4, 8).transpose(2, 1, 3, 0).reshape(LANES, LANES)
     pay, total, x_lo, x_hi = parcels(recv, *halo, weight)

time: 88.5 us -> 83 us (0.938)
  the two profiles are of different devices: /device:TPU:25 before, /device:TPU:2 now
where the time goes in v3:
time: 83 us; the launch traced here: 82.5 us
  starting transfers between devices  44.2 us (53%)
  waiting for transfers between devices  21.8 us (26%)
  Pallas kernels  13.3 us (16%)
  other arithmetic  1.15 us (1%)
  local copies, waits for them, and re-layouts  1.11 us (1%)
  between operations  0.94 us (1%)
    ppermute x8, starting transfers between devices, shift_pair(): return (lax.ppermute(to_high, axis, up), lax.ppermute(to_low, axis, down))  20.4 us
    ppermute x8, waiting for transfers between devices, shift_pair(): return (lax.ppermute(to_high, axis, up), lax.ppermute(to_low, axis, down))  18.3 us
    all_to_all x1, starting transfers between devices, per_device(): lax.all_to_all(send.reshape(blocks, ROWS * LANES), ('gx', 'gy'), split_ax...  17.8 us
    pallas_call x1, Pallas kernels, parcels(): call(parcel_kernel, [arr(5, 2 * blocks, LANES), arr(nx * ZR, LANES), arr(...  8.32 us
    ppermute x2, starting transfers between devices, shift_pair(): lax.ppermute(to_low, axis, down)  4.44 us
    pallas_call x1, Pallas kernels, per_device(): call(pack_kernel, arr(blocks * ROWS, LANES), [pltpu.VMEM((1, blocks), jnp...  3 us
    ppermute x2, waiting for transfers between devices, shift_pair(): lax.ppermute(to_high, axis, up)  2.81 us
  transfers between devices with their start and end apart: 13, of which 8 were waited for; matrix products, arithmetic and copies ran while one was open for 0% of the time, Pallas kernels for 6%

profile of v3, /device:TPU:2, one launch (start us, length us, event | category | flops | bytes accessed | tf_op | source)
XLA Modules:
  0.0 82.5 jit_solution(9463367815908864377)
XLA Ops:
  0.6 0.9 %fusion.2 = (f32[4,2,16,128]{3,2,1,0:T(8,128)S(1)}, f32[4,2,16,128]{3,2,1,0:T(8,128)S(1)}) fusion(f32[4,16,16,128]{3,2,1,0:T(8,128)} %gas_ref.3), kind=kLoop, calls=%fused_computation.21 | loop fusion | bytes 262144 | tf_op jit(solution)/shard_map/slice | solution.py:320
  1.5 2.9 %collective-permute-start.1 = (f32[4,2,16,128]{3,2,1,0:T(8,128)S(1)}, f32[4,2,16,128]{3,2,1,0:T(8,128)S(1)}, u32[]{:S(2)}, u32[]{:S(2)}) collective-permute-start(f32[4,2,16,128]{3,2,1,0:T(8,128)S(1)} %get-tuple-element.44), channel_id=1, source_target_pairs={{32,0},{64,32},{96,64},{128,96},{160,128},{192,160},{224,192},{256... | collective-permute-start | bytes 196616 | tf_op jit(solution)/shard_map/ppermute | solution.py:279
  4.5 3.0 %shard_map.86 = f32[1408,128]{1,0:T(8,128)} custom-call(s32[1,128]{1,0:T(1,128)} %bitcast.32, s32[1,128]{1,0:T(1,128)} %bitcast.33, s32[1,128]{1,0:T(1,128)} %bitcast.34, f32[3,128,128]{2,1,0:T(8,128)} %bitcast.31, f32[128,2,128]{2,1,0:T(2,128)} %prop_hbm.1), custom_call_target="tpu_custom_call" | custom-call | tf_op jit(solution)/shard_map/pallas_call | solution.py:321
  7.6 17.8 %all-to-all-start = ((f32[128,1,1408]{2,1,0:T(1,128)}), f32[128,1,1408]{2,1,0:T(1,128)S(1)}, u32[]{:S(2)}, u32[]{:S(2)}) async-start(f32[128,1,1408]{2,1,0:T(1,128)} %bitcast.27), calls=%async_computation | async-start | bytes 1441792 | tf_op jit(solution)/shard_map/all_to_all | solution.py:340
  25.9 3.4 %collective-permute-start.2 = (f32[20,2,128]{2,1,0:T(2,128)S(1)}, f32[20,2,128]{2,1,0:T(2,128)S(1)}, u32[]{:S(2)}, u32[]{:S(2)}) collective-permute-start(f32[20,2,128]{2,1,0:T(2,128)S(1)} %get-tuple-element.20), channel_id=1, source_target_pairs={{0,1},{1,2},{2,3},{4,5},{5,6},{6,7},{8,9},{9,10},{10,11},{12,13},{... | collective-permute-start | bytes 61448 | tf_op jit(solution)/shard_map/ppermute | solution.py:275
  29.3 2.4 %collective-permute-start.3 = (f32[20,2,128]{2,1,0:T(2,128)S(1)}, f32[20,2,128]{2,1,0:T(2,128)S(1)}, u32[]{:S(2)}, u32[]{:S(2)}) collective-permute-start(f32[20,2,128]{2,1,0:T(2,128)S(1)} %get-tuple-element.21), channel_id=1, source_target_pairs={{1,0},{2,1},{3,2},{5,4},{6,5},{7,6},{9,8},{10,9},{11,10},{13,12},{... | collective-permute-start | bytes 61448 | tf_op jit(solution)/shard_map/ppermute | solution.py:275
  31.9 3.1 %collective-permute-done.3.zh_ref = f32[20,2,128]{2,1,0:T(2,128)S(1)} collective-permute-done((f32[20,2,128]{2,1,0:T(2,128)S(1)}, f32[20,2,128]{2,1,0:T(2,128)S(1)}, u32[]{:S(2)}, u32[]{:S(2)}) %collective-permute-start.3) | collective-permute-done | bytes 20512 | tf_op jit(solution)/shard_map/ppermute | solution.py:275
  35.0 3.0 %collective-permute-start.4 = (f32[240,128]{1,0:T(8,128)S(1)}, f32[240,128]{1,0:T(8,128)S(1)}, u32[]{:S(2)}, u32[]{:S(2)}) collective-permute-start(f32[240,128]{1,0:T(8,128)S(1)} %get-tuple-element.51), channel_id=1, source_target_pairs={{0,4},{4,8},{8,12},{12,16},{16,20},{20,24},{24,28},{1,5},{5,9},{9,... | collective-permute-start | bytes 368648 | tf_op jit(solution)/shard_map/ppermute | solution.py:275
  38.1 1.3 %collective-permute-start.5 = (f32[240,128]{1,0:T(8,128)S(1)}, f32[240,128]{1,0:T(8,128)S(1)}, u32[]{:S(2)}, u32[]{:S(2)}) collective-permute-start(f32[240,128]{1,0:T(8,128)S(1)} %get-tuple-element.50), channel_id=1, source_target_pairs={{4,0},{8,4},{12,8},{16,12},{20,16},{24,20},{28,24},{5,1},{9,5},{13... | collective-permute-start | bytes 368648 | tf_op jit(solution)/shard_map/ppermute | solution.py:275
  39.5 5.9 %collective-permute-done.4.yl_ref = f32[240,128]{1,0:T(8,128)S(1)} collective-permute-done((f32[240,128]{1,0:T(8,128)S(1)}, f32[240,128]{1,0:T(8,128)S(1)}, u32[]{:S(2)}, u32[]{:S(2)}) %collective-permute-start.4) | collective-permute-done | bytes 122912 | tf_op jit(solution)/shard_map/ppermute | solution.py:275
  45.5 1.9 %collective-permute-done.5.yh_ref = f32[240,128]{1,0:T(8,128)S(1)} collective-permute-done((f32[240,128]{1,0:T(8,128)S(1)}, f32[240,128]{1,0:T(8,128)S(1)}, u32[]{:S(2)}, u32[]{:S(2)}) %collective-permute-start.5) | collective-permute-done | bytes 122912 | tf_op jit(solution)/shard_map/ppermute | solution.py:275
  47.9 0.8 all-to-all-done
  48.6 8.3 %shard_map.89 = (f32[5,256,128]{2,1,0:T(8,128)}, f32[2304,128]{1,0:T(8,128)S(1)}, f32[288,128]{1,0:T(8,128)S(1)}, f32[288,128]{1,0:T(8,128)S(1)}) custom-call(f32[1408,128]{1,0:T(8,128)S(1)} %bitcast.18, f32[20,128,128]{2,1,0:T(8,128)S(1)} %get-tuple-element.22.mid_ref, f32[20,2,128]{2,1,0:T(2,128)S(1)} %get-tuple-element.23.zl_ref, ...), custom_call_target="tpu_custom_call" | custom-call | tf_op jit(solution)/shard_map/pallas_call | solution.py:301
  57.0 1.5 %collective-permute-start.6 = (f32[2,144,128]{2,1,0:T(8,128)S(1)}, f32[2,144,128]{2,1,0:T(8,128)S(1)}, u32[]{:S(2)}, u32[]{:S(2)}) collective-permute-start(f32[2,144,128]{2,1,0:T(8,128)S(1)} %bitcast.26), channel_id=1, source_target_pairs={{0,32},{32,64},{64,96},{96,128},{128,160},{160,192},{192,224},{224... | collective-permute-start | bytes 442376 | tf_op jit(solution)/shard_map/ppermute | solution.py:279
  58.4 1.5 %collective-permute-start.7 = (f32[2,144,128]{2,1,0:T(8,128)S(1)}, f32[2,144,128]{2,1,0:T(8,128)S(1)}, u32[]{:S(2)}, u32[]{:S(2)}) collective-permute-start(f32[2,144,128]{2,1,0:T(8,128)S(1)} %bitcast.25), channel_id=1, source_target_pairs={{32,0},{64,32},{96,64},{128,96},{160,128},{192,160},{224,192},{256... | collective-permute-start | bytes 442376 | tf_op jit(solution)/shard_map/ppermute | solution.py:279
  59.9 2.8 %collective-permute-done.6 = f32[2,144,128]{2,1,0:T(8,128)S(1)} collective-permute-done((f32[2,144,128]{2,1,0:T(8,128)S(1)}, f32[2,144,128]{2,1,0:T(8,128)S(1)}, u32[]{:S(2)}, u32[]{:S(2)}) %collective-permute-start.6) | collective-permute-done | bytes 147488 | tf_op jit(solution)/shard_map/ppermute | solution.py:279
  62.8 3.4 %collective-permute-start.8 = (f32[16,2,128]{2,1,0:T(2,128)S(1)}, f32[16,2,128]{2,1,0:T(2,128)S(1)}, u32[]{:S(2)}, u32[]{:S(2)}) collective-permute-start(f32[16,2,128]{2,1,0:T(2,128)S(1)} %pad_maximum_fusion.7), channel_id=1, source_target_pairs={{0,1},{1,2},{2,3},{4,5},{5,6},{6,7},{8,9},{9,10},{10,11},{12,13},{... | collective-permute-start | bytes 49160 | tf_op jit(solution)/shard_map/ppermute | solution.py:275
  66.3 2.4 %collective-permute-start.9 = (f32[16,2,128]{2,1,0:T(2,128)S(1)}, f32[16,2,128]{2,1,0:T(2,128)S(1)}, u32[]{:S(2)}, u32[]{:S(2)}) collective-permute-start(f32[16,2,128]{2,1,0:T(2,128)S(1)} %pad_maximum_fusion.8), channel_id=1, source_target_pairs={{1,0},{2,1},{3,2},{5,4},{6,5},{7,6},{9,8},{10,9},{11,10},{13,12},{... | collective-permute-start | bytes 49160 | tf_op jit(solution)/shard_map/ppermute | solution.py:275
  68.7 0.7 shard_map.90.base_ref
  69.4 2.5 %collective-permute-done.9.zh_ref = f32[16,2,128]{2,1,0:T(2,128)S(1)} collective-permute-done((f32[16,2,128]{2,1,0:T(2,128)S(1)}, f32[16,2,128]{2,1,0:T(2,128)S(1)}, u32[]{:S(2)}, u32[]{:S(2)}) %collective-permute-start.9) | collective-permute-done | bytes 16416 | tf_op jit(solution)/shard_map/ppermute | solution.py:275
  72.3 3.1 %collective-permute-start.10 = (f32[4,16,2,128]{3,2,1,0:T(2,128)S(1)}, f32[4,16,2,128]{3,2,1,0:T(2,128)S(1)}, u32[]{:S(2)}, u32[]{:S(2)}) collective-permute-start(f32[4,16,2,128]{3,2,1,0:T(2,128)S(1)} %get-tuple-element.30), channel_id=1, source_target_pairs={{0,4},{4,8},{8,12},{12,16},{16,20},{20,24},{24,28},{1,5},{5,9},{9,... | collective-permute-start | bytes 196616 | tf_op jit(solution)/shard_map/ppermute | solution.py:275
  75.4 1.3 %collective-permute-start.11 = (f32[4,16,2,128]{3,2,1,0:T(2,128)S(1)}, f32[4,16,2,128]{3,2,1,0:T(2,128)S(1)}, u32[]{:S(2)}, u32[]{:S(2)}) collective-permute-start(f32[4,16,2,128]{3,2,1,0:T(2,128)S(1)} %get-tuple-element.31), channel_id=1, source_target_pairs={{4,0},{8,4},{12,8},{16,12},{20,16},{24,20},{28,24},{5,1},{9,5},{13... | collective-permute-start | bytes 196616 | tf_op jit(solution)/shard_map/ppermute | solution.py:275
  77.3 4.3 %collective-permute-done.11 = f32[4,16,2,128]{3,2,1,0:T(2,128)S(1)} collective-permute-done((f32[4,16,2,128]{3,2,1,0:T(2,128)S(1)}, f32[4,16,2,128]{3,2,1,0:T(2,128)S(1)}, u32[]{:S(2)}, u32[]{:S(2)}) %collective-permute-start.11) | collective-permute-done | bytes 65568 | tf_op jit(solution)/shard_map/ppermute | solution.py:275
  81.7 0.9 %pad_maximum_fusion = f32[4,16,16,128]{3,2,1,0:T(8,128)} fusion(f32[4,16,2,128]{3,2,1,0:T(2,128)S(1)} %get-tuple-element.41, f32[4,16,12,128]{3,2,1,0:T(8,128)S(1)} %slice.90, f32[4,16,2,128]{3,2,1,0:T(2,128)S(1)} %get-tuple-element.40), kind=kLoop, calls=%fused_computation | loop fusion | flops 262144 | bytes 1048576 | tf_op jit(solution)/shard_map/concatenate | solution.py:379
  (31 shorter events, 2.4 us)
Async XLA Ops:
  1.5 6.0 %collective-permute-start = (f32[4,2,16,128]{3,2,1,0:T(8,128)S(1)}, f32[4,2,16,128]{3,2,1,0:T(8,128)S(1)}, u32[]{:S(2)}, u32[]{:S(2)}) collective-permute-start(f32[4,2,16,128]{3,2,1,0:T(8,128)S(1)} %get-tuple-element.45), channel_id=1, source_target_pairs={{0,32},{32,64},{64,96},{96,128},{128,160},{160,192},{192,224},{224... | collective-permute-start | bytes 196616 | tf_op jit(solution)/shard_map/ppermute | solution.py:279
  1.5 6.0 %collective-permute-start.1 = (f32[4,2,16,128]{3,2,1,0:T(8,128)S(1)}, f32[4,2,16,128]{3,2,1,0:T(8,128)S(1)}, u32[]{:S(2)}, u32[]{:S(2)}) collective-permute-start(f32[4,2,16,128]{3,2,1,0:T(8,128)S(1)} %get-tuple-element.44), channel_id=1, source_target_pairs={{32,0},{64,32},{96,64},{128,96},{160,128},{192,160},{224,192},{256... | collective-permute-start | bytes 196616 | tf_op jit(solution)/shard_map/ppermute | solution.py:279
  4.5 20.9 %copy-start = (f32[4,16,16,128]{3,2,1,0:T(8,128)S(1)}, f32[4,16,16,128]{3,2,1,0:T(8,128)}, u32[]{:S(2)}) copy-start(f32[4,16,16,128]{3,2,1,0:T(8,128)} %gas_ref.3) | copy-start | bytes 1572868
  7.6 41.1 %all-to-all-start = ((f32[128,1,1408]{2,1,0:T(1,128)}), f32[128,1,1408]{2,1,0:T(1,128)S(1)}, u32[]{:S(2)}, u32[]{:S(2)}) async-start(f32[128,1,1408]{2,1,0:T(1,128)} %bitcast.27), calls=%async_computation | async-start | bytes 1441792 | tf_op jit(solution)/shard_map/all_to_all | solution.py:340
  25.4 14.0 %copy-start.1 = (f32[128,128]{1,0:T(8,128)S(1)}, f32[128,128]{1,0:T(8,128)}, u32[]{:S(2)}) copy-start(f32[128,128]{1,0:T(8,128)} %param.12) | copy-start | bytes 196612
  25.9 6.0 %collective-permute-start.2 = (f32[20,2,128]{2,1,0:T(2,128)S(1)}, f32[20,2,128]{2,1,0:T(2,128)S(1)}, u32[]{:S(2)}, u32[]{:S(2)}) collective-permute-start(f32[20,2,128]{2,1,0:T(2,128)S(1)} %get-tuple-element.20), channel_id=1, source_target_pairs={{0,1},{1,2},{2,3},{4,5},{5,6},{6,7},{8,9},{9,10},{10,11},{12,13},{... | collective-permute-start | bytes 61448 | tf_op jit(solution)/shard_map/ppermute | solution.py:275
  29.3 5.7 %collective-permute-start.3 = (f32[20,2,128]{2,1,0:T(2,128)S(1)}, f32[20,2,128]{2,1,0:T(2,128)S(1)}, u32[]{:S(2)}, u32[]{:S(2)}) collective-permute-start(f32[20,2,128]{2,1,0:T(2,128)S(1)} %get-tuple-element.21), channel_id=1, source_target_pairs={{1,0},{2,1},{3,2},{5,4},{6,5},{7,6},{9,8},{10,9},{11,10},{13,12},{... | collective-permute-start | bytes 61448 | tf_op jit(solution)/shard_map/ppermute | solution.py:275
  35.0 10.4 %collective-permute-start.4 = (f32[240,128]{1,0:T(8,128)S(1)}, f32[240,128]{1,0:T(8,128)S(1)}, u32[]{:S(2)}, u32[]{:S(2)}) collective-permute-start(f32[240,128]{1,0:T(8,128)S(1)} %get-tuple-element.51), channel_id=1, source_target_pairs={{0,4},{4,8},{8,12},{12,16},{16,20},{20,24},{24,28},{1,5},{5,9},{9,... | collective-permute-start | bytes 368648 | tf_op jit(solution)/shard_map/ppermute | solution.py:275
  38.1 9.3 %collective-permute-start.5 = (f32[240,128]{1,0:T(8,128)S(1)}, f32[240,128]{1,0:T(8,128)S(1)}, u32[]{:S(2)}, u32[]{:S(2)}) collective-permute-start(f32[240,128]{1,0:T(8,128)S(1)} %get-tuple-element.50), channel_id=1, source_target_pairs={{4,0},{8,4},{12,8},{16,12},{20,16},{24,20},{28,24},{5,1},{9,5},{13... | collective-permute-start | bytes 368648 | tf_op jit(solution)/shard_map/ppermute | solution.py:275
  57.0 5.8 %collective-permute-start.6 = (f32[2,144,128]{2,1,0:T(8,128)S(1)}, f32[2,144,128]{2,1,0:T(8,128)S(1)}, u32[]{:S(2)}, u32[]{:S(2)}) collective-permute-start(f32[2,144,128]{2,1,0:T(8,128)S(1)} %bitcast.26), channel_id=1, source_target_pairs={{0,32},{32,64},{64,96},{96,128},{128,160},{160,192},{192,224},{224... | collective-permute-start | bytes 442376 | tf_op jit(solution)/shard_map/ppermute | solution.py:279
  58.4 4.3 %collective-permute-start.7 = (f32[2,144,128]{2,1,0:T(8,128)S(1)}, f32[2,144,128]{2,1,0:T(8,128)S(1)}, u32[]{:S(2)}, u32[]{:S(2)}) collective-permute-start(f32[2,144,128]{2,1,0:T(8,128)S(1)} %bitcast.25), channel_id=1, source_target_pairs={{32,0},{64,32},{96,64},{128,96},{160,128},{192,160},{224,192},{256... | collective-permute-start | bytes 442376 | tf_op jit(solution)/shard_map/ppermute | solution.py:279
  62.8 6.6 %collective-permute-start.8 = (f32[16,2,128]{2,1,0:T(2,128)S(1)}, f32[16,2,128]{2,1,0:T(2,128)S(1)}, u32[]{:S(2)}, u32[]{:S(2)}) collective-permute-start(f32[16,2,128]{2,1,0:T(2,128)S(1)} %pad_maximum_fusion.7), channel_id=1, source_target_pairs={{0,1},{1,2},{2,3},{4,5},{5,6},{6,7},{8,9},{9,10},{10,11},{12,13},{... | collective-permute-start | bytes 49160 | tf_op jit(solution)/shard_map/ppermute | solution.py:275
  66.3 5.6 %collective-permute-start.9 = (f32[16,2,128]{2,1,0:T(2,128)S(1)}, f32[16,2,128]{2,1,0:T(2,128)S(1)}, u32[]{:S(2)}, u32[]{:S(2)}) collective-permute-start(f32[16,2,128]{2,1,0:T(2,128)S(1)} %pad_maximum_fusion.8), channel_id=1, source_target_pairs={{1,0},{2,1},{3,2},{5,4},{6,5},{7,6},{9,8},{10,9},{11,10},{13,12},{... | collective-permute-start | bytes 49160 | tf_op jit(solution)/shard_map/ppermute | solution.py:275
  72.3 5.0 %collective-permute-start.10 = (f32[4,16,2,128]{3,2,1,0:T(2,128)S(1)}, f32[4,16,2,128]{3,2,1,0:T(2,128)S(1)}, u32[]{:S(2)}, u32[]{:S(2)}) collective-permute-start(f32[4,16,2,128]{3,2,1,0:T(2,128)S(1)} %get-tuple-element.30), channel_id=1, source_target_pairs={{0,4},{4,8},{8,12},{12,16},{16,20},{20,24},{24,28},{1,5},{5,9},{9,... | collective-permute-start | bytes 196616 | tf_op jit(solution)/shard_map/ppermute | solution.py:275
  75.4 6.2 %collective-permute-start.11 = (f32[4,16,2,128]{3,2,1,0:T(2,128)S(1)}, f32[4,16,2,128]{3,2,1,0:T(2,128)S(1)}, u32[]{:S(2)}, u32[]{:S(2)}) collective-permute-start(f32[4,16,2,128]{3,2,1,0:T(2,128)S(1)} %get-tuple-element.31), channel_id=1, source_target_pairs={{4,0},{8,4},{12,8},{16,12},{20,16},{24,20},{28,24},{5,1},{9,5},{13... | collective-permute-start | bytes 196616 | tf_op jit(solution)/shard_map/ppermute | solution.py:275

commit v4 on v3

--- a/solution.py
+++ b/solution.py
@@ -111,8 +111,8 @@
 
 def parcel_kernel(
     recv_ref, mid_ref, zl_ref, zh_ref, w_ref,
-    pay_ref, sum_ref, xlo_ref, xhi_ref,
-    code_v, code_s, pad, acc, more, near, force, sem,
+    pay_hbm, sum_ref, xlo_ref, xhi_ref,
+    code_v, code_s, pad, acc, more, near, force, pay_ref, sem, pay_sem,
 ):
     planes, cells_z = mid_ref.shape[0], mid_ref.shape[1]
     last = ZO + cells_z
@@ -151,7 +151,7 @@
         c = code_s[s // 4, (s % 4) * YS + b]
         return jnp.bitwise_and(c, 4095), lax.shift_right_logical(c, 12)
 
-    @pl.loop(0, 8)
+    @pl.loop(0, 8, unroll=2)
     def _(s):
         merged = []
         for g in range(4):
@@ -203,6 +203,8 @@
         pay_ref[3, slots, :] = mass
         pay_ref[4, slots, :] = jnp.where(alive, relax, 0.0)
         force[s * n + 3 * YS : (s + 1) * n, :] = mass
+    leave = pltpu.make_async_copy(pay_ref, pay_hbm, pay_sem)
+    leave.start()
     across = (((1,), (1,)), ((), ()))
     for s in range(8):
         f_hi, f_lo = split(force[s * n : (s + 1) * n, :])
@@ -242,6 +244,7 @@
     sum_ref[...] = acc[low:high, :] + more[low:high, :]
     xlo_ref[...] = acc[0:low, :] + more[0:low, :]
     xhi_ref[...] = acc[high:, :] + more[high:, :]
+    leave.wait()
 
 
 def back_kernel(sum_ref, base_ref, xl_ref, xh_ref, zl_ref, zh_ref, out_ref, ylo_ref, yhi_ref, buf):
@@ -267,16 +270,20 @@
             yhi_ref[k, x] = flat[k * YS + 2 + cells_y : k * YS + 4 + cells_y]
 
 
-def shift_pair(to_low, to_high, axis, ring=False):
+def shift_pair(to_low, to_high, axis):
     count = lax.axis_size(axis)
-    if not ring:
-        up = [(i, i + 1) for i in range(count - 1)]
+    here = lax.axis_index(axis)
+    if axis == "gx":
+        up = [(i, (i + 1) % count) for i in range(count)]
         down = [(j, i) for i, j in up]
-        return lax.ppermute(to_high, axis, up), lax.ppermute(to_low, axis, down)
-    up = [(i, (i + 1) % count) for i in range(count)]
-    down = [(j, i) for i, j in up]
-    here = lax.axis_index(axis)
-    low, high = lax.ppermute(to_high, axis, up), lax.ppermute(to_low, axis, down)
+        low, high = lax.ppermute(to_high, axis, up), lax.ppermute(to_low, axis, down)
+    else:
+        even = here % 2 == 0
+        first = [(i, i + 1 - 2 * (i % 2)) for i in range(count)]
+        second = [(i, (i - 1 + 2 * (i % 2)) % count) for i in range(count)]
+        one = lax.ppermute(jnp.where(even, to_high, to_low), axis, first)
+        two = lax.ppermute(jnp.where(even, to_low, to_high), axis, second)
+        low, high = jnp.where(even, two, one), jnp.where(even, one, two)
     return jnp.where(here > 0, low, 0.0), jnp.where(here < count - 1, high, 0.0)
 
 
@@ -309,15 +316,18 @@
             pltpu.VMEM((rows, LANES), F32),
             pltpu.VMEM((8 * LANES, LANES), F32),
             pltpu.VMEM((8 * LANES, LANES), F32),
+            pltpu.VMEM((5, 2 * blocks, LANES), F32),
+            pltpu.SemaphoreType.DMA,
             pltpu.SemaphoreType.DMA,
         ],
+        out_specs=[pl.BlockSpec(memory_space=pl.ANY)] + [pl.BlockSpec(memory_space=pltpu.VMEM)] * 3,
     )(recv, mid, z_low, z_high, weight)
 
 
 def per_device(parcel_vel, parcel_props, fill_count, owner_peer, cell_offset, shell_weight, gas_state):
     _, nx, ny, nz = gas_state.shape
     blocks = parcel_vel.shape[0]
-    x_low, x_high = shift_pair(gas_state[:, :2], gas_state[:, nx - 2 :], "gx", ring=True)
+    x_low, x_high = shift_pair(gas_state[:, :2], gas_state[:, nx - 2 :], "gx")
     send = call(
         pack_kernel,
         arr(blocks * ROWS, LANES),
@@ -360,7 +370,7 @@
     parcels_next = pay.transpose(1, 0, 2)
     base = call(diffuse_kernel, arr(nx, nz, LANES), [pltpu.VMEM((2, ZR, LANES), F32)])(*halo)
 
-    from_low, from_high = shift_pair(x_lo.reshape(2, ZR, LANES), x_hi.reshape(2, ZR, LANES), "gx", ring=True)
+    from_low, from_high = shift_pair(x_lo.reshape(2, ZR, LANES), x_hi.reshape(2, ZR, LANES), "gx")
     total = total.reshape(nx, ZR, LANES)
 
     def rim(lo, hi):

time: 83 us -> 84.4 us (1.017)
  the two profiles are of different devices: /device:TPU:2 before, /device:TPU:6 now
where the time goes in v4:
time: 84.4 us; the launch traced here: 84 us
  starting transfers between devices  48.9 us (58%)
  waiting for transfers between devices  19.3 us (23%)
  Pallas kernels  12.4 us (15%)
  other arithmetic  1.24 us (1%)
  local copies, waits for them, and re-layouts  1.11 us (1%)
  between operations  1.01 us (1%)
    all_to_all x1, starting transfers between devices, per_device(): lax.all_to_all(send.reshape(blocks, ROWS * LANES), ('gx', 'gy'), split_ax...  17.8 us
    ppermute x4, starting transfers between devices, shift_pair(): two = lax.ppermute(jnp.where(even, to_low, to_high), axis, second)  14.8 us
    ppermute x4, starting transfers between devices, shift_pair(): one = lax.ppermute(jnp.where(even, to_high, to_low), axis, first)  10.4 us
    ppermute x4, waiting for transfers between devices, shift_pair(): two = lax.ppermute(jnp.where(even, to_low, to_high), axis, second)  9.68 us
    pallas_call x1, Pallas kernels, parcels(): call(parcel_kernel, [arr(5, 2 * blocks, LANES), arr(nx * ZR, LANES), arr(...  7.35 us
    ppermute x4, waiting for transfers between devices, shift_pair(): one = lax.ppermute(jnp.where(even, to_high, to_low), axis, first)  6.84 us
    ppermute x2, starting transfers between devices, shift_pair(): lax.ppermute(to_low, axis, down)  5.25 us
    pallas_call x1, Pallas kernels, per_device(): call(pack_kernel, arr(blocks * ROWS, LANES), [pltpu.VMEM((1, blocks), jnp...  3.01 us
  transfers between devices with their start and end apart: 13, of which 7 were waited for; matrix products, arithmetic and copies ran while one was open for 0% of the time, Pallas kernels for 6%

profile of v4, /device:TPU:6, one launch (start us, length us, event | category | flops | bytes accessed | tf_op | source)
XLA Modules:
  0.0 84.0 jit_solution(4735218833185757973)
XLA Ops:
  0.6 0.9 %fusion.4 = (f32[4,2,16,128]{3,2,1,0:T(8,128)S(1)}, f32[4,2,16,128]{3,2,1,0:T(8,128)S(1)}) fusion(f32[4,16,16,128]{3,2,1,0:T(8,128)} %gas_ref.3), kind=kLoop, calls=%fused_computation.35 | loop fusion | bytes 262144 | tf_op jit(solution)/shard_map/slice | solution.py:330
  1.5 2.9 %collective-permute-start.1 = (f32[4,2,16,128]{3,2,1,0:T(8,128)S(1)}, f32[4,2,16,128]{3,2,1,0:T(8,128)S(1)}, u32[]{:S(2)}, u32[]{:S(2)}) collective-permute-start(f32[4,2,16,128]{3,2,1,0:T(8,128)S(1)} %get-tuple-element.44), channel_id=1, source_target_pairs={{32,0},{64,32},{96,64},{128,96},{160,128},{192,160},{224,192},{256... | collective-permute-start | bytes 196616 | tf_op jit(solution)/shard_map/ppermute | solution.py:279
  4.5 3.0 %shard_map.86 = f32[1408,128]{1,0:T(8,128)} custom-call(s32[1,128]{1,0:T(1,128)} %bitcast.48, s32[1,128]{1,0:T(1,128)} %bitcast.49, s32[1,128]{1,0:T(1,128)} %bitcast.50, f32[3,128,128]{2,1,0:T(8,128)} %bitcast.43, f32[128,2,128]{2,1,0:T(2,128)} %prop_hbm.1), custom_call_target="tpu_custom_call" | custom-call | tf_op jit(solution)/shard_map/pallas_call | solution.py:331
  7.6 17.8 %all-to-all-start = ((f32[128,1,1408]{2,1,0:T(1,128)}), f32[128,1,1408]{2,1,0:T(1,128)S(1)}, u32[]{:S(2)}, u32[]{:S(2)}) async-start(f32[128,1,1408]{2,1,0:T(1,128)} %bitcast.39), calls=%async_computation | async-start | bytes 1441792 | tf_op jit(solution)/shard_map/all_to_all | solution.py:350
  26.0 2.7 %collective-permute-start.3 = (f32[20,2,128]{2,1,0:T(2,128)S(1)}, f32[20,2,128]{2,1,0:T(2,128)S(1)}, u32[]{:S(2)}, u32[]{:S(2)}) collective-permute-start(f32[20,2,128]{2,1,0:T(2,128)S(1)} %bitcast.47), channel_id=1, source_target_pairs={{0,1},{1,0},{2,3},{3,2},{4,5},{5,4},{6,7},{7,6},{8,9},{9,8},{10,11... | collective-permute-start | bytes 61448 | tf_op jit(solution)/shard_map/ppermute | solution.py:284
  28.7 3.0 %collective-permute-start.2 = (f32[20,2,128]{2,1,0:T(2,128)S(1)}, f32[20,2,128]{2,1,0:T(2,128)S(1)}, u32[]{:S(2)}, u32[]{:S(2)}) collective-permute-start(f32[20,2,128]{2,1,0:T(2,128)S(1)} %bitcast.46), channel_id=1, source_target_pairs={{0,3},{1,2},{2,1},{3,0},{4,7},{5,6},{6,5},{7,4},{8,11},{9,10},{10,... | collective-permute-start | bytes 61448 | tf_op jit(solution)/shard_map/ppermute | solution.py:285
  31.9 3.7 %collective-permute-done.2 = f32[20,2,128]{2,1,0:T(2,128)S(1)} collective-permute-done((f32[20,2,128]{2,1,0:T(2,128)S(1)}, f32[20,2,128]{2,1,0:T(2,128)S(1)}, u32[]{:S(2)}, u32[]{:S(2)}) %collective-permute-start.2) | collective-permute-done | bytes 20512 | tf_op jit(solution)/shard_map/ppermute | solution.py:285
  35.7 3.0 %collective-permute-start.5 = (f32[240,128]{1,0:T(8,128)S(1)}, f32[240,128]{1,0:T(8,128)S(1)}, u32[]{:S(2)}, u32[]{:S(2)}) collective-permute-start(f32[240,128]{1,0:T(8,128)S(1)} %get-tuple-element.48), channel_id=1, source_target_pairs={{0,4},{4,0},{8,12},{12,8},{16,20},{20,16},{24,28},{28,24},{1,5},{5... | collective-permute-start | bytes 368648 | tf_op jit(solution)/shard_map/ppermute | solution.py:284
  38.7 4.6 %collective-permute-start.4 = (f32[240,128]{1,0:T(8,128)S(1)}, f32[240,128]{1,0:T(8,128)S(1)}, u32[]{:S(2)}, u32[]{:S(2)}) collective-permute-start(f32[240,128]{1,0:T(8,128)S(1)} %get-tuple-element.49), channel_id=1, source_target_pairs={{0,28},{4,8},{8,4},{12,16},{16,12},{20,24},{24,20},{28,0},{1,29},{... | collective-permute-start | bytes 368648 | tf_op jit(solution)/shard_map/ppermute | solution.py:285
  43.4 3.9 %collective-permute-done.5 = f32[240,128]{1,0:T(8,128)S(1)} collective-permute-done((f32[240,128]{1,0:T(8,128)S(1)}, f32[240,128]{1,0:T(8,128)S(1)}, u32[]{:S(2)}, u32[]{:S(2)}) %collective-permute-start.5) | collective-permute-done | bytes 122912 | tf_op jit(solution)/shard_map/ppermute | solution.py:284
  47.3 1.6 %collective-permute-done.4 = f32[240,128]{1,0:T(8,128)S(1)} collective-permute-done((f32[240,128]{1,0:T(8,128)S(1)}, f32[240,128]{1,0:T(8,128)S(1)}, u32[]{:S(2)}, u32[]{:S(2)}) %collective-permute-start.4) | collective-permute-done | bytes 122912 | tf_op jit(solution)/shard_map/ppermute | solution.py:285
  49.5 7.4 %shard_map.89 = (f32[5,256,128]{2,1,0:T(8,128)}, f32[2304,128]{1,0:T(8,128)S(1)}, f32[288,128]{1,0:T(8,128)S(1)}, f32[288,128]{1,0:T(8,128)S(1)}) custom-call(f32[1408,128]{1,0:T(8,128)S(1)} %bitcast.26, f32[20,128,128]{2,1,0:T(8,128)S(1)} %get-tuple-element.22.mid_ref, f32[20,2,128]{2,1,0:T(2,128)S(1)} %get-tuple-element.23.zl_ref, ...), custom_call_target="tpu_custom_call" | custom-call | tf_op jit(solution)/shard_map/pallas_call | solution.py:308
  56.8 0.7 collective-permute-start.6
  57.5 2.3 %collective-permute-start.7 = (f32[2,144,128]{2,1,0:T(8,128)S(1)}, f32[2,144,128]{2,1,0:T(8,128)S(1)}, u32[]{:S(2)}, u32[]{:S(2)}) collective-permute-start(f32[2,144,128]{2,1,0:T(8,128)S(1)} %bitcast.37), channel_id=1, source_target_pairs={{32,0},{64,32},{96,64},{128,96},{160,128},{192,160},{224,192},{256... | collective-permute-start | bytes 442376 | tf_op jit(solution)/shard_map/ppermute | solution.py:279
  59.8 2.8 %collective-permute-done.6 = f32[2,144,128]{2,1,0:T(8,128)S(1)} collective-permute-done((f32[2,144,128]{2,1,0:T(8,128)S(1)}, f32[2,144,128]{2,1,0:T(8,128)S(1)}, u32[]{:S(2)}, u32[]{:S(2)}) %collective-permute-start.6) | collective-permute-done | bytes 147488 | tf_op jit(solution)/shard_map/ppermute | solution.py:279
  62.7 2.7 %collective-permute-start.9 = (f32[16,2,128]{2,1,0:T(2,128)S(1)}, f32[16,2,128]{2,1,0:T(2,128)S(1)}, u32[]{:S(2)}, u32[]{:S(2)}) collective-permute-start(f32[16,2,128]{2,1,0:T(2,128)S(1)} %get-tuple-element.62), channel_id=1, source_target_pairs={{0,1},{1,0},{2,3},{3,2},{4,5},{5,4},{6,7},{7,6},{8,9},{9,8},{10,11... | collective-permute-start | bytes 49160 | tf_op jit(solution)/shard_map/ppermute | solution.py:284
  65.4 3.0 %collective-permute-start.8 = (f32[16,2,128]{2,1,0:T(2,128)S(1)}, f32[16,2,128]{2,1,0:T(2,128)S(1)}, u32[]{:S(2)}, u32[]{:S(2)}) collective-permute-start(f32[16,2,128]{2,1,0:T(2,128)S(1)} %get-tuple-element.63), channel_id=1, source_target_pairs={{0,3},{1,2},{2,1},{3,0},{4,7},{5,6},{6,5},{7,4},{8,11},{9,10},{10,... | collective-permute-start | bytes 49160 | tf_op jit(solution)/shard_map/ppermute | solution.py:285
  68.4 0.7 shard_map.90.base_ref
  69.0 3.2 %collective-permute-done.8 = f32[16,2,128]{2,1,0:T(2,128)S(1)} collective-permute-done((f32[16,2,128]{2,1,0:T(2,128)S(1)}, f32[16,2,128]{2,1,0:T(2,128)S(1)}, u32[]{:S(2)}, u32[]{:S(2)}) %collective-permute-start.8) | collective-permute-done | bytes 16416 | tf_op jit(solution)/shard_map/ppermute | solution.py:285
  72.6 4.2 %collective-permute-start.10 = (f32[4,16,2,128]{3,2,1,0:T(2,128)S(1)}, f32[4,16,2,128]{3,2,1,0:T(2,128)S(1)}, u32[]{:S(2)}, u32[]{:S(2)}) collective-permute-start(f32[4,16,2,128]{3,2,1,0:T(2,128)S(1)} %bitcast.45), channel_id=1, source_target_pairs={{0,28},{4,8},{8,4},{12,16},{16,12},{20,24},{24,20},{28,0},{1,29},{... | collective-permute-start | bytes 196616 | tf_op jit(solution)/shard_map/ppermute | solution.py:285
  76.8 1.9 %collective-permute-start.11 = (f32[4,16,2,128]{3,2,1,0:T(2,128)S(1)}, f32[4,16,2,128]{3,2,1,0:T(2,128)S(1)}, u32[]{:S(2)}, u32[]{:S(2)}) collective-permute-start(f32[4,16,2,128]{3,2,1,0:T(2,128)S(1)} %bitcast.44), channel_id=1, source_target_pairs={{0,4},{4,0},{8,12},{12,8},{16,20},{20,16},{24,28},{28,24},{1,5},{5... | collective-permute-start | bytes 196616 | tf_op jit(solution)/shard_map/ppermute | solution.py:284
  78.8 1.2 %collective-permute-done.10 = f32[4,16,2,128]{3,2,1,0:T(2,128)S(1)} collective-permute-done((f32[4,16,2,128]{3,2,1,0:T(2,128)S(1)}, f32[4,16,2,128]{3,2,1,0:T(2,128)S(1)}, u32[]{:S(2)}, u32[]{:S(2)}) %collective-permute-start.10) | collective-permute-done | bytes 65568 | tf_op jit(solution)/shard_map/ppermute | solution.py:285
  80.0 3.0 %collective-permute-done.11 = f32[4,16,2,128]{3,2,1,0:T(2,128)S(1)} collective-permute-done((f32[4,16,2,128]{3,2,1,0:T(2,128)S(1)}, f32[4,16,2,128]{3,2,1,0:T(2,128)S(1)}, u32[]{:S(2)}, u32[]{:S(2)}) %collective-permute-start.11) | collective-permute-done | bytes 65568 | tf_op jit(solution)/shard_map/ppermute | solution.py:284
  83.1 0.9 %pad_maximum_fusion = f32[4,16,16,128]{3,2,1,0:T(8,128)} fusion(f32[4,16,2,128]{3,2,1,0:T(2,128)S(1)} %get-tuple-element.41, f32[4,16,12,128]{3,2,1,0:T(8,128)S(1)} %slice.90, f32[4,16,2,128]{3,2,1,0:T(2,128)S(1)} %get-tuple-element.40), kind=kLoop, calls=%fused_computation | loop fusion | flops 262144 | bytes 1048576 | tf_op jit(solution)/shard_map/concatenate | solution.py:389
  (35 shorter events, 1.9 us)
Async XLA Ops:
  1.5 6.0 %collective-permute-start = (f32[4,2,16,128]{3,2,1,0:T(8,128)S(1)}, f32[4,2,16,128]{3,2,1,0:T(8,128)S(1)}, u32[]{:S(2)}, u32[]{:S(2)}) collective-permute-start(f32[4,2,16,128]{3,2,1,0:T(8,128)S(1)} %get-tuple-element.45), channel_id=1, source_target_pairs={{0,32},{32,64},{64,96},{96,128},{128,160},{160,192},{192,224},{224... | collective-permute-start | bytes 196616 | tf_op jit(solution)/shard_map/ppermute | solution.py:279
  1.5 6.0 %collective-permute-start.1 = (f32[4,2,16,128]{3,2,1,0:T(8,128)S(1)}, f32[4,2,16,128]{3,2,1,0:T(8,128)S(1)}, u32[]{:S(2)}, u32[]{:S(2)}) collective-permute-start(f32[4,2,16,128]{3,2,1,0:T(8,128)S(1)} %get-tuple-element.44), channel_id=1, source_target_pairs={{32,0},{64,32},{96,64},{128,96},{160,128},{192,160},{224,192},{256... | collective-permute-start | bytes 196616 | tf_op jit(solution)/shard_map/ppermute | solution.py:279
  4.5 20.9 %copy-start = (f32[4,16,16,128]{3,2,1,0:T(8,128)S(1)}, f32[4,16,16,128]{3,2,1,0:T(8,128)}, u32[]{:S(2)}) copy-start(f32[4,16,16,128]{3,2,1,0:T(8,128)} %gas_ref.3) | copy-start | bytes 1572868
  7.6 41.9 %all-to-all-start = ((f32[128,1,1408]{2,1,0:T(1,128)}), f32[128,1,1408]{2,1,0:T(1,128)S(1)}, u32[]{:S(2)}, u32[]{:S(2)}) async-start(f32[128,1,1408]{2,1,0:T(1,128)} %bitcast.39), calls=%async_computation | async-start | bytes 1441792 | tf_op jit(solution)/shard_map/all_to_all | solution.py:350
  25.4 17.9 %copy-start.1 = (f32[128,128]{1,0:T(8,128)S(1)}, f32[128,128]{1,0:T(8,128)}, u32[]{:S(2)}) copy-start(f32[128,128]{1,0:T(8,128)} %param.12) | copy-start | bytes 196612
  26.0 5.9 %collective-permute-start.3 = (f32[20,2,128]{2,1,0:T(2,128)S(1)}, f32[20,2,128]{2,1,0:T(2,128)S(1)}, u32[]{:S(2)}, u32[]{:S(2)}) collective-permute-start(f32[20,2,128]{2,1,0:T(2,128)S(1)} %bitcast.47), channel_id=1, source_target_pairs={{0,1},{1,0},{2,3},{3,2},{4,5},{5,4},{6,7},{7,6},{8,9},{9,8},{10,11... | collective-permute-start | bytes 61448 | tf_op jit(solution)/shard_map/ppermute | solution.py:284
  28.7 6.9 %collective-permute-start.2 = (f32[20,2,128]{2,1,0:T(2,128)S(1)}, f32[20,2,128]{2,1,0:T(2,128)S(1)}, u32[]{:S(2)}, u32[]{:S(2)}) collective-permute-start(f32[20,2,128]{2,1,0:T(2,128)S(1)} %bitcast.46), channel_id=1, source_target_pairs={{0,3},{1,2},{2,1},{3,0},{4,7},{5,6},{6,5},{7,4},{8,11},{9,10},{10,... | collective-permute-start | bytes 61448 | tf_op jit(solution)/shard_map/ppermute | solution.py:285
  35.7 11.6 %collective-permute-start.5 = (f32[240,128]{1,0:T(8,128)S(1)}, f32[240,128]{1,0:T(8,128)S(1)}, u32[]{:S(2)}, u32[]{:S(2)}) collective-permute-start(f32[240,128]{1,0:T(8,128)S(1)} %get-tuple-element.48), channel_id=1, source_target_pairs={{0,4},{4,0},{8,12},{12,8},{16,20},{20,16},{24,28},{28,24},{1,5},{5... | collective-permute-start | bytes 368648 | tf_op jit(solution)/shard_map/ppermute | solution.py:284
  38.7 10.2 %collective-permute-start.4 = (f32[240,128]{1,0:T(8,128)S(1)}, f32[240,128]{1,0:T(8,128)S(1)}, u32[]{:S(2)}, u32[]{:S(2)}) collective-permute-start(f32[240,128]{1,0:T(8,128)S(1)} %get-tuple-element.49), channel_id=1, source_target_pairs={{0,28},{4,8},{8,4},{12,16},{16,12},{20,24},{24,20},{28,0},{1,29},{... | collective-permute-start | bytes 368648 | tf_op jit(solution)/shard_map/ppermute | solution.py:285
  56.8 5.8 %collective-permute-start.6 = (f32[2,144,128]{2,1,0:T(8,128)S(1)}, f32[2,144,128]{2,1,0:T(8,128)S(1)}, u32[]{:S(2)}, u32[]{:S(2)}) collective-permute-start(f32[2,144,128]{2,1,0:T(8,128)S(1)} %bitcast.38), channel_id=1, source_target_pairs={{0,32},{32,64},{64,96},{96,128},{128,160},{160,192},{192,224},{224... | collective-permute-start | bytes 442376 | tf_op jit(solution)/shard_map/ppermute | solution.py:279
  57.5 5.1 %collective-permute-start.7 = (f32[2,144,128]{2,1,0:T(8,128)S(1)}, f32[2,144,128]{2,1,0:T(8,128)S(1)}, u32[]{:S(2)}, u32[]{:S(2)}) collective-permute-start(f32[2,144,128]{2,1,0:T(8,128)S(1)} %bitcast.37), channel_id=1, source_target_pairs={{32,0},{64,32},{96,64},{128,96},{160,128},{192,160},{224,192},{256... | collective-permute-start | bytes 442376 | tf_op jit(solution)/shard_map/ppermute | solution.py:279
  62.7 6.3 %collective-permute-start.9 = (f32[16,2,128]{2,1,0:T(2,128)S(1)}, f32[16,2,128]{2,1,0:T(2,128)S(1)}, u32[]{:S(2)}, u32[]{:S(2)}) collective-permute-start(f32[16,2,128]{2,1,0:T(2,128)S(1)} %get-tuple-element.62), channel_id=1, source_target_pairs={{0,1},{1,0},{2,3},{3,2},{4,5},{5,4},{6,7},{7,6},{8,9},{9,8},{10,11... | collective-permute-start | bytes 49160 | tf_op jit(solution)/shard_map/ppermute | solution.py:284
  65.4 6.8 %collective-permute-start.8 = (f32[16,2,128]{2,1,0:T(2,128)S(1)}, f32[16,2,128]{2,1,0:T(2,128)S(1)}, u32[]{:S(2)}, u32[]{:S(2)}) collective-permute-start(f32[16,2,128]{2,1,0:T(2,128)S(1)} %get-tuple-element.63), channel_id=1, source_target_pairs={{0,3},{1,2},{2,1},{3,0},{4,7},{5,6},{6,5},{7,4},{8,11},{9,10},{10,... | collective-permute-start | bytes 49160 | tf_op jit(solution)/shard_map/ppermute | solution.py:285
  72.6 7.4 %collective-permute-start.10 = (f32[4,16,2,128]{3,2,1,0:T(2,128)S(1)}, f32[4,16,2,128]{3,2,1,0:T(2,128)S(1)}, u32[]{:S(2)}, u32[]{:S(2)}) collective-permute-start(f32[4,16,2,128]{3,2,1,0:T(2,128)S(1)} %bitcast.45), channel_id=1, source_target_pairs={{0,28},{4,8},{8,4},{12,16},{16,12},{20,24},{24,20},{28,0},{1,29},{... | collective-permute-start | bytes 196616 | tf_op jit(solution)/shard_map/ppermute | solution.py:285
  76.8 6.2 %collective-permute-start.11 = (f32[4,16,2,128]{3,2,1,0:T(2,128)S(1)}, f32[4,16,2,128]{3,2,1,0:T(2,128)S(1)}, u32[]{:S(2)}, u32[]{:S(2)}) collective-permute-start(f32[4,16,2,128]{3,2,1,0:T(2,128)S(1)} %bitcast.44), channel_id=1, source_target_pairs={{0,4},{4,0},{8,12},{12,8},{16,20},{20,16},{24,28},{28,24},{1,5},{5... | collective-permute-start | bytes 196616 | tf_op jit(solution)/shard_map/ppermute | solution.py:284

commit v5 on v3

--- a/solution.py
+++ b/solution.py
@@ -30,7 +30,7 @@
     copies = [pltpu.make_async_copy(src, dst, sems.at[i]) for i, (src, dst) in enumerate(pairs)]
     for copy in copies:
         copy.start()
-    for copy in copies:
+    for copy in copies[:3]:
         copy.wait()
     hot = (iota((n, n), 0) == tgt_ref[...]).astype(F32)
     earlier = (iota((n, n), 0) < iota((n, n), 1)).astype(BF16)
@@ -46,6 +46,8 @@
         head = jnp.where(lane == place, column, head)
     out_ref[pl.ds(10, n, stride=ROWS), :] = head
     picks = jnp.concatenate([first, second], axis=0).astype(BF16)
+    for copy in copies[3:]:
+        copy.wait()
     for k in range(5):
         x = vel_ref[k] if k < 3 else prop_ref[:, k - 3, :]
         total = jnp.zeros((2 * n, n), F32)
@@ -75,8 +77,8 @@
         hi_ref[x] = flat[cells_z - 2 : cells_z]
 
 
-def turn_kernel(gas_ref, xl_ref, xh_ref, zl_ref, zh_ref, yl_ref, yh_ref, out_ref, zlo_ref, zhi_ref, buf):
-    planes, cells_y = out_ref.shape[0], gas_ref.shape[2]
+def turn_kernel(gas_ref, xl_ref, xh_ref, zl_ref, zh_ref, yl_ref, yh_ref, out_ref, buf):
+    planes, cells_y, cells_z = out_ref.shape[0], gas_ref.shape[2], gas_ref.shape[3]
     buf[...] = jnp.zeros_like(buf)
     fill_rows(buf, gas_ref, xl_ref, xh_ref)
     y = iota((2, LANES), 1) % YS
@@ -85,37 +87,37 @@
             row = (k * planes + x) * 2
             buf[x, k * YS : k * YS + 2, :] = yl_ref[row : row + 2]
             buf[x, k * YS + 2 + cells_y : k * YS + 4 + cells_y, :] = yh_ref[row : row + 2]
-        for part, (z_ref, o_ref) in enumerate(((zl_ref, zlo_ref), (zh_ref, zhi_ref))):
+        for part, z_ref in enumerate((zl_ref, zh_ref)):
             row = (4 + part) * planes * 2 + x * 2
             below = pltpu.roll(yl_ref[row : row + 2], LANES - cells_y, 1)
             above = pltpu.roll(yh_ref[row : row + 2], cells_y, 1)
-            o_ref[x] = jnp.where(y < 2, below, jnp.where(y < 2 + cells_y, z_ref[x], jnp.where(y < 4 + cells_y, above, 0.0)))
+            at = ZO - 2 + part * (cells_z + 2)
+            out_ref[x, at : at + 2, :] = jnp.where(
+                y < 2, below, jnp.where(y < 2 + cells_y, z_ref[x], jnp.where(y < 4 + cells_y, above, 0.0))
+            )
     for x in range(planes):
-        out_ref[x] = buf[x].T
-
-
-def diffuse_kernel(mid_ref, zl_ref, zh_ref, out_ref, col):
+        out_ref[x, ZO : ZO + cells_z, :] = buf[x].T
+
+
+def diffuse_kernel(pad_ref, out_ref):
     cells_x, cells_z = out_ref.shape[0], out_ref.shape[1]
     last = ZO + cells_z
     lane = iota((cells_z, LANES), 1)
     rate = jnp.where(lane < 3 * YS, TIME_STEP, 0.5 * TIME_STEP).astype(F32)
     for x in range(2, cells_x + 2):
-        here = mid_ref[x]
-        col[x % 2, ZO:last, :] = here
-        col[x % 2, ZO - 2 : ZO, :] = zl_ref[x]
-        col[x % 2, last : last + 2, :] = zh_ref[x]
-        beside = mid_ref[x - 1] + mid_ref[x + 1] + pltpu.roll(here, LANES - 1, 1) + pltpu.roll(here, 1, 1)
-        beside = beside + col[x % 2, ZO + 1 : last + 1, :] + col[x % 2, ZO - 1 : last - 1, :]
+        here = pad_ref[x, ZO:last, :]
+        beside = pad_ref[x - 1, ZO:last, :] + pad_ref[x + 1, ZO:last, :]
+        beside = beside + pltpu.roll(here, LANES - 1, 1) + pltpu.roll(here, 1, 1)
+        beside = beside + pad_ref[x, ZO + 1 : last + 1, :] + pad_ref[x, ZO - 1 : last - 1, :]
         out_ref[x - 2] = here + rate * (beside - 6.0 * here)
 
 
 def parcel_kernel(
-    recv_ref, mid_ref, zl_ref, zh_ref, w_ref,
-    pay_ref, sum_ref, xlo_ref, xhi_ref,
-    code_v, code_s, pad, acc, more, near, force, sem,
+    recv_ref, pad, w_ref,
+    pay_hbm, sum_ref, xlo_ref, xhi_ref,
+    code_v, code_s, acc, more, near, force, pay_ref, sem, pay_sem,
 ):
-    planes, cells_z = mid_ref.shape[0], mid_ref.shape[1]
-    last = ZO + cells_z
+    planes = pad.shape[0] // ZR
     n = LANES
     off = recv_ref[pl.ds(10, n, stride=ROWS), :]
     rest = jnp.floor((off + 0.5) * (1.0 / 125.0))
@@ -126,11 +128,6 @@
     code_v[...] = code.T[0:8].astype(jnp.int32)
     copy = pltpu.make_async_copy(code_v, code_s, sem)
     copy.start()
-    for x in range(planes):
-        at = x * ZR
-        pad[at + ZO : at + last, :] = mid_ref[x]
-        pad[at + ZO - 2 : at + ZO, :] = zl_ref[x]
-        pad[at + last : at + last + 2, :] = zh_ref[x]
     acc[...] = jnp.zeros_like(acc)
     more[...] = jnp.zeros_like(more)
     w_hi = w_ref[...].astype(BF16)
@@ -151,7 +148,7 @@
         c = code_s[s // 4, (s % 4) * YS + b]
         return jnp.bitwise_and(c, 4095), lax.shift_right_logical(c, 12)
 
-    @pl.loop(0, 8)
+    @pl.loop(0, 8, unroll=2)
     def _(s):
         merged = []
         for g in range(4):
@@ -203,6 +200,8 @@
         pay_ref[3, slots, :] = mass
         pay_ref[4, slots, :] = jnp.where(alive, relax, 0.0)
         force[s * n + 3 * YS : (s + 1) * n, :] = mass
+    leave = pltpu.make_async_copy(pay_ref, pay_hbm, pay_sem)
+    leave.start()
     across = (((1,), (1,)), ((), ()))
     for s in range(8):
         f_hi, f_lo = split(force[s * n : (s + 1) * n, :])
@@ -242,6 +241,7 @@
     sum_ref[...] = acc[low:high, :] + more[low:high, :]
     xlo_ref[...] = acc[0:low, :] + more[0:low, :]
     xhi_ref[...] = acc[high:, :] + more[high:, :]
+    leave.wait()
 
 
 def back_kernel(sum_ref, base_ref, xl_ref, xh_ref, zl_ref, zh_ref, out_ref, ylo_ref, yhi_ref, buf):
@@ -294,10 +294,10 @@
     return jax.ShapeDtypeStruct(shape, dtype)
 
 
-def parcels(recv, mid, z_low, z_high, weight):
-    nx = mid.shape[0] - 4
+def parcels(recv, padded, weight):
+    rows = padded.shape[0]
+    nx = rows // ZR - 4
     blocks = recv.shape[0] // ROWS
-    rows = (nx + 4) * ZR
     return call(
         parcel_kernel,
         [arr(5, 2 * blocks, LANES), arr(nx * ZR, LANES), arr(2 * ZR, LANES), arr(2 * ZR, LANES)],
@@ -306,12 +306,14 @@
             pltpu.SMEM((8, LANES), jnp.int32),
             pltpu.VMEM((rows, LANES), F32),
             pltpu.VMEM((rows, LANES), F32),
-            pltpu.VMEM((rows, LANES), F32),
             pltpu.VMEM((8 * LANES, LANES), F32),
             pltpu.VMEM((8 * LANES, LANES), F32),
+            pltpu.VMEM((5, 2 * blocks, LANES), F32),
+            pltpu.SemaphoreType.DMA,
             pltpu.SemaphoreType.DMA,
         ],
-    )(recv, mid, z_low, z_high, weight)
+        out_specs=[pl.BlockSpec(memory_space=pl.ANY)] + [pl.BlockSpec(memory_space=pltpu.VMEM)] * 3,
+    )(recv, padded, weight)
 
 
 def per_device(parcel_vel, parcel_props, fill_count, owner_peer, cell_offset, shell_weight, gas_state):
@@ -351,14 +353,14 @@
         return jnp.concatenate([face, z_low.reshape(2 * planes, LANES), z_high.reshape(2 * planes, LANES)], axis=0)
 
     y_low, y_high = shift_pair(y_face(0), y_face(ny - 2), "gy")
-    halo = call(turn_kernel, [arr(planes, nz, LANES), arr(planes, 2, LANES), arr(planes, 2, LANES)], rows_buf)(
+    padded = call(turn_kernel, arr(planes, ZR, LANES), rows_buf)(
         gas_state, x_low, x_high, z_low, z_high, y_low, y_high
     )
 
     weight = shell_weight.reshape(LANES, 4, 4, 8).transpose(2, 1, 3, 0).reshape(LANES, LANES)
-    pay, total, x_lo, x_hi = parcels(recv, *halo, weight)
+    pay, total, x_lo, x_hi = parcels(recv, padded.reshape(planes * ZR, LANES), weight)
     parcels_next = pay.transpose(1, 0, 2)
-    base = call(diffuse_kernel, arr(nx, nz, LANES), [pltpu.VMEM((2, ZR, LANES), F32)])(*halo)
+    base = call(diffuse_kernel, arr(nx, nz, LANES))(padded)
 
     from_low, from_high = shift_pair(x_lo.reshape(2, ZR, LANES), x_hi.reshape(2, ZR, LANES), "gx", ring=True)
     total = total.reshape(nx, ZR, LANES)

time: 83 us -> 81.8 us (0.986)
  Pallas kernels: 13.3 us -> 12 us
    pallas_call x1, Pallas kernels: 8.32 us -> 7.18 us  [parcels(): call(parcel_kernel, [arr(5, 2 * blocks, LANES), arr(nx * ZR, LANES), arr(...]
  transfers between devices with their start and end apart: 13 -> 13, of which waited for: 8 -> 8; matrix products, arithmetic and copies ran while one was open for 0% -> 0% of each run, Pallas kernels for 6% -> 5%
where the time goes in v5:
time: 81.8 us; the launch traced here: 81.4 us
  starting transfers between devices  44.3 us (54%)
  waiting for transfers between devices  21.9 us (27%)
  Pallas kernels  12 us (15%)
  other arithmetic  1.15 us (1%)
  local copies, waits for them, and re-layouts  1.11 us (1%)
  between operations  0.94 us (1%)
    ppermute x8, starting transfers between devices, shift_pair(): return (lax.ppermute(to_high, axis, up), lax.ppermute(to_low, axis, down))  20.6 us
    ppermute x8, waiting for transfers between devices, shift_pair(): return (lax.ppermute(to_high, axis, up), lax.ppermute(to_low, axis, down))  18.3 us
    all_to_all x1, starting transfers between devices, per_device(): lax.all_to_all(send.reshape(blocks, ROWS * LANES), ('gx', 'gy'), split_ax...  17.8 us
    pallas_call x1, Pallas kernels, parcels(): call(parcel_kernel, [arr(5, 2 * blocks, LANES), arr(nx * ZR, LANES), arr(...  7.18 us
    ppermute x2, starting transfers between devices, shift_pair(): lax.ppermute(to_low, axis, down)  4.32 us
    pallas_call x1, Pallas kernels, per_device(): call(pack_kernel, arr(blocks * ROWS, LANES), [pltpu.VMEM((1, blocks), jnp...  2.85 us
    ppermute x2, waiting for transfers between devices, shift_pair(): lax.ppermute(to_high, axis, up)  2.81 us
  transfers between devices with their start and end apart: 13, of which 8 were waited for; matrix products, arithmetic and copies ran while one was open for 0% of the time, Pallas kernels for 5%

profile of v5, /device:TPU:2, one launch (start us, length us, event | category | flops | bytes accessed | tf_op | source)
XLA Modules:
  0.0 81.4 jit_solution(1387225985738726024)
XLA Ops:
  0.6 0.9 %fusion.2 = (f32[4,2,16,128]{3,2,1,0:T(8,128)S(1)}, f32[4,2,16,128]{3,2,1,0:T(8,128)S(1)}) fusion(f32[4,16,16,128]{3,2,1,0:T(8,128)} %gas_ref.3), kind=kLoop, calls=%fused_computation.21 | loop fusion | bytes 262144 | tf_op jit(solution)/shard_map/slice | solution.py:322
  1.5 2.9 %collective-permute-start.1 = (f32[4,2,16,128]{3,2,1,0:T(8,128)S(1)}, f32[4,2,16,128]{3,2,1,0:T(8,128)S(1)}, u32[]{:S(2)}, u32[]{:S(2)}) collective-permute-start(f32[4,2,16,128]{3,2,1,0:T(8,128)S(1)} %get-tuple-element.38), channel_id=1, source_target_pairs={{32,0},{64,32},{96,64},{128,96},{160,128},{192,160},{224,192},{256... | collective-permute-start | bytes 196616 | tf_op jit(solution)/shard_map/ppermute | solution.py:279
  4.5 2.8 %shard_map.86 = f32[1408,128]{1,0:T(8,128)} custom-call(s32[1,128]{1,0:T(1,128)} %bitcast.34, s32[1,128]{1,0:T(1,128)} %bitcast.35, s32[1,128]{1,0:T(1,128)} %bitcast.36, f32[3,128,128]{2,1,0:T(8,128)} %bitcast.33, f32[128,2,128]{2,1,0:T(2,128)} %prop_hbm.1), custom_call_target="tpu_custom_call" | custom-call | tf_op jit(solution)/shard_map/pallas_call | solution.py:323
  7.4 17.8 %all-to-all-start = ((f32[128,1,1408]{2,1,0:T(1,128)}), f32[128,1,1408]{2,1,0:T(1,128)S(1)}, u32[]{:S(2)}, u32[]{:S(2)}) async-start(f32[128,1,1408]{2,1,0:T(1,128)} %bitcast.29), calls=%async_computation | async-start | bytes 1441792 | tf_op jit(solution)/shard_map/all_to_all | solution.py:342
  25.8 3.4 %collective-permute-start.2 = (f32[20,2,128]{2,1,0:T(2,128)S(1)}, f32[20,2,128]{2,1,0:T(2,128)S(1)}, u32[]{:S(2)}, u32[]{:S(2)}) collective-permute-start(f32[20,2,128]{2,1,0:T(2,128)S(1)} %get-tuple-element.17), channel_id=1, source_target_pairs={{0,1},{1,2},{2,3},{4,5},{5,6},{6,7},{8,9},{9,10},{10,11},{12,13},{... | collective-permute-start | bytes 61448 | tf_op jit(solution)/shard_map/ppermute | solution.py:275
  29.2 2.4 %collective-permute-start.3 = (f32[20,2,128]{2,1,0:T(2,128)S(1)}, f32[20,2,128]{2,1,0:T(2,128)S(1)}, u32[]{:S(2)}, u32[]{:S(2)}) collective-permute-start(f32[20,2,128]{2,1,0:T(2,128)S(1)} %get-tuple-element.18), channel_id=1, source_target_pairs={{1,0},{2,1},{3,2},{5,4},{6,5},{7,6},{9,8},{10,9},{11,10},{13,12},{... | collective-permute-start | bytes 61448 | tf_op jit(solution)/shard_map/ppermute | solution.py:275
  31.8 3.1 %collective-permute-done.3.zh_ref = f32[20,2,128]{2,1,0:T(2,128)S(1)} collective-permute-done((f32[20,2,128]{2,1,0:T(2,128)S(1)}, f32[20,2,128]{2,1,0:T(2,128)S(1)}, u32[]{:S(2)}, u32[]{:S(2)}) %collective-permute-start.3) | collective-permute-done | bytes 20512 | tf_op jit(solution)/shard_map/ppermute | solution.py:275
  34.9 3.0 %collective-permute-start.4 = (f32[240,128]{1,0:T(8,128)S(1)}, f32[240,128]{1,0:T(8,128)S(1)}, u32[]{:S(2)}, u32[]{:S(2)}) collective-permute-start(f32[240,128]{1,0:T(8,128)S(1)} %get-tuple-element.45), channel_id=1, source_target_pairs={{0,4},{4,8},{8,12},{12,16},{16,20},{20,24},{24,28},{1,5},{5,9},{9,... | collective-permute-start | bytes 368648 | tf_op jit(solution)/shard_map/ppermute | solution.py:275
  37.9 1.3 %collective-permute-start.5 = (f32[240,128]{1,0:T(8,128)S(1)}, f32[240,128]{1,0:T(8,128)S(1)}, u32[]{:S(2)}, u32[]{:S(2)}) collective-permute-start(f32[240,128]{1,0:T(8,128)S(1)} %get-tuple-element.44), channel_id=1, source_target_pairs={{4,0},{8,4},{12,8},{16,12},{20,16},{24,20},{28,24},{5,1},{9,5},{13... | collective-permute-start | bytes 368648 | tf_op jit(solution)/shard_map/ppermute | solution.py:275
  39.4 5.9 %collective-permute-done.4.yl_ref = f32[240,128]{1,0:T(8,128)S(1)} collective-permute-done((f32[240,128]{1,0:T(8,128)S(1)}, f32[240,128]{1,0:T(8,128)S(1)}, u32[]{:S(2)}, u32[]{:S(2)}) %collective-permute-start.4) | collective-permute-done | bytes 122912 | tf_op jit(solution)/shard_map/ppermute | solution.py:275
  45.3 1.9 %collective-permute-done.5.yh_ref = f32[240,128]{1,0:T(8,128)S(1)} collective-permute-done((f32[240,128]{1,0:T(8,128)S(1)}, f32[240,128]{1,0:T(8,128)S(1)}, u32[]{:S(2)}, u32[]{:S(2)}) %collective-permute-start.5) | collective-permute-done | bytes 122912 | tf_op jit(solution)/shard_map/ppermute | solution.py:275
  47.7 0.8 all-to-all-done
  48.5 7.2 %shard_map.89 = (f32[5,256,128]{2,1,0:T(8,128)}, f32[2304,128]{1,0:T(8,128)S(1)}, f32[288,128]{1,0:T(8,128)S(1)}, f32[288,128]{1,0:T(8,128)S(1)}) custom-call(f32[1408,128]{1,0:T(8,128)S(1)} %bitcast.20, f32[2880,128]{1,0:T(8,128)S(1)} %bitcast.19, f32[128,128]{1,0:T(8,128)S(1)} %bitcast.24), custom_call_target="tpu_custom_call" | custom-call | tf_op jit(solution)/shard_map/pallas_call | solution.py:301
  55.7 1.6 %collective-permute-start.6 = (f32[2,144,128]{2,1,0:T(8,128)S(1)}, f32[2,144,128]{2,1,0:T(8,128)S(1)}, u32[]{:S(2)}, u32[]{:S(2)}) collective-permute-start(f32[2,144,128]{2,1,0:T(8,128)S(1)} %bitcast.28), channel_id=1, source_target_pairs={{0,32},{32,64},{64,96},{96,128},{128,160},{160,192},{192,224},{224... | collective-permute-start | bytes 442376 | tf_op jit(solution)/shard_map/ppermute | solution.py:279
  57.2 1.4 %collective-permute-start.7 = (f32[2,144,128]{2,1,0:T(8,128)S(1)}, f32[2,144,128]{2,1,0:T(8,128)S(1)}, u32[]{:S(2)}, u32[]{:S(2)}) collective-permute-start(f32[2,144,128]{2,1,0:T(8,128)S(1)} %bitcast.27), channel_id=1, source_target_pairs={{32,0},{64,32},{96,64},{128,96},{160,128},{192,160},{224,192},{256... | collective-permute-start | bytes 442376 | tf_op jit(solution)/shard_map/ppermute | solution.py:279
  58.6 2.8 %collective-permute-done.6 = f32[2,144,128]{2,1,0:T(8,128)S(1)} collective-permute-done((f32[2,144,128]{2,1,0:T(8,128)S(1)}, f32[2,144,128]{2,1,0:T(8,128)S(1)}, u32[]{:S(2)}, u32[]{:S(2)}) %collective-permute-start.6) | collective-permute-done | bytes 147488 | tf_op jit(solution)/shard_map/ppermute | solution.py:279
  61.5 3.4 %collective-permute-start.8 = (f32[16,2,128]{2,1,0:T(2,128)S(1)}, f32[16,2,128]{2,1,0:T(2,128)S(1)}, u32[]{:S(2)}, u32[]{:S(2)}) collective-permute-start(f32[16,2,128]{2,1,0:T(2,128)S(1)} %pad_maximum_fusion.7), channel_id=1, source_target_pairs={{0,1},{1,2},{2,3},{4,5},{5,6},{6,7},{8,9},{9,10},{10,11},{12,13},{... | collective-permute-start | bytes 49160 | tf_op jit(solution)/shard_map/ppermute | solution.py:275
  65.0 2.4 %collective-permute-start.9 = (f32[16,2,128]{2,1,0:T(2,128)S(1)}, f32[16,2,128]{2,1,0:T(2,128)S(1)}, u32[]{:S(2)}, u32[]{:S(2)}) collective-permute-start(f32[16,2,128]{2,1,0:T(2,128)S(1)} %pad_maximum_fusion.8), channel_id=1, source_target_pairs={{1,0},{2,1},{3,2},{5,4},{6,5},{7,6},{9,8},{10,9},{11,10},{13,12},{... | collective-permute-start | bytes 49160 | tf_op jit(solution)/shard_map/ppermute | solution.py:275
  67.4 0.6 shard_map.90.base_ref
  68.1 2.5 %collective-permute-done.9.zh_ref = f32[16,2,128]{2,1,0:T(2,128)S(1)} collective-permute-done((f32[16,2,128]{2,1,0:T(2,128)S(1)}, f32[16,2,128]{2,1,0:T(2,128)S(1)}, u32[]{:S(2)}, u32[]{:S(2)}) %collective-permute-start.9) | collective-permute-done | bytes 16416 | tf_op jit(solution)/shard_map/ppermute | solution.py:275
  71.0 3.2 %collective-permute-start.10 = (f32[4,16,2,128]{3,2,1,0:T(2,128)S(1)}, f32[4,16,2,128]{3,2,1,0:T(2,128)S(1)}, u32[]{:S(2)}, u32[]{:S(2)}) collective-permute-start(f32[4,16,2,128]{3,2,1,0:T(2,128)S(1)} %get-tuple-element.24), channel_id=1, source_target_pairs={{0,4},{4,8},{8,12},{12,16},{16,20},{20,24},{24,28},{1,5},{5,9},{9,... | collective-permute-start | bytes 196616 | tf_op jit(solution)/shard_map/ppermute | solution.py:275
  74.2 1.3 %collective-permute-start.11 = (f32[4,16,2,128]{3,2,1,0:T(2,128)S(1)}, f32[4,16,2,128]{3,2,1,0:T(2,128)S(1)}, u32[]{:S(2)}, u32[]{:S(2)}) collective-permute-start(f32[4,16,2,128]{3,2,1,0:T(2,128)S(1)} %get-tuple-element.25), channel_id=1, source_target_pairs={{4,0},{8,4},{12,8},{16,12},{20,16},{24,20},{28,24},{5,1},{9,5},{13... | collective-permute-start | bytes 196616 | tf_op jit(solution)/shard_map/ppermute | solution.py:275
  76.1 4.3 %collective-permute-done.11 = f32[4,16,2,128]{3,2,1,0:T(2,128)S(1)} collective-permute-done((f32[4,16,2,128]{3,2,1,0:T(2,128)S(1)}, f32[4,16,2,128]{3,2,1,0:T(2,128)S(1)}, u32[]{:S(2)}, u32[]{:S(2)}) %collective-permute-start.11) | collective-permute-done | bytes 65568 | tf_op jit(solution)/shard_map/ppermute | solution.py:275
  80.5 0.9 %pad_maximum_fusion = f32[4,16,16,128]{3,2,1,0:T(8,128)} fusion(f32[4,16,2,128]{3,2,1,0:T(2,128)S(1)} %get-tuple-element.35, f32[4,16,12,128]{3,2,1,0:T(8,128)S(1)} %slice.90, f32[4,16,2,128]{3,2,1,0:T(2,128)S(1)} %get-tuple-element.34), kind=kLoop, calls=%fused_computation | loop fusion | flops 262144 | bytes 1048576 | tf_op jit(solution)/shard_map/concatenate | solution.py:381
  (31 shorter events, 2.4 us)
Async XLA Ops:
  1.5 5.8 %collective-permute-start = (f32[4,2,16,128]{3,2,1,0:T(8,128)S(1)}, f32[4,2,16,128]{3,2,1,0:T(8,128)S(1)}, u32[]{:S(2)}, u32[]{:S(2)}) collective-permute-start(f32[4,2,16,128]{3,2,1,0:T(8,128)S(1)} %get-tuple-element.39), channel_id=1, source_target_pairs={{0,32},{32,64},{64,96},{96,128},{128,160},{160,192},{192,224},{224... | collective-permute-start | bytes 196616 | tf_op jit(solution)/shard_map/ppermute | solution.py:279
  1.5 5.8 %collective-permute-start.1 = (f32[4,2,16,128]{3,2,1,0:T(8,128)S(1)}, f32[4,2,16,128]{3,2,1,0:T(8,128)S(1)}, u32[]{:S(2)}, u32[]{:S(2)}) collective-permute-start(f32[4,2,16,128]{3,2,1,0:T(8,128)S(1)} %get-tuple-element.38), channel_id=1, source_target_pairs={{32,0},{64,32},{96,64},{128,96},{160,128},{192,160},{224,192},{256... | collective-permute-start | bytes 196616 | tf_op jit(solution)/shard_map/ppermute | solution.py:279
  4.5 20.7 %copy-start = (f32[4,16,16,128]{3,2,1,0:T(8,128)S(1)}, f32[4,16,16,128]{3,2,1,0:T(8,128)}, u32[]{:S(2)}) copy-start(f32[4,16,16,128]{3,2,1,0:T(8,128)} %gas_ref.3) | copy-start | bytes 1572868
  7.4 41.1 %all-to-all-start = ((f32[128,1,1408]{2,1,0:T(1,128)}), f32[128,1,1408]{2,1,0:T(1,128)S(1)}, u32[]{:S(2)}, u32[]{:S(2)}) async-start(f32[128,1,1408]{2,1,0:T(1,128)} %bitcast.29), calls=%async_computation | async-start | bytes 1441792 | tf_op jit(solution)/shard_map/all_to_all | solution.py:342
  25.2 14.0 %copy-start.1 = (f32[128,128]{1,0:T(8,128)S(1)}, f32[128,128]{1,0:T(8,128)}, u32[]{:S(2)}) copy-start(f32[128,128]{1,0:T(8,128)} %param.12) | copy-start | bytes 196612
  25.8 6.0 %collective-permute-start.2 = (f32[20,2,128]{2,1,0:T(2,128)S(1)}, f32[20,2,128]{2,1,0:T(2,128)S(1)}, u32[]{:S(2)}, u32[]{:S(2)}) collective-permute-start(f32[20,2,128]{2,1,0:T(2,128)S(1)} %get-tuple-element.17), channel_id=1, source_target_pairs={{0,1},{1,2},{2,3},{4,5},{5,6},{6,7},{8,9},{9,10},{10,11},{12,13},{... | collective-permute-start | bytes 61448 | tf_op jit(solution)/shard_map/ppermute | solution.py:275
  29.2 5.7 %collective-permute-start.3 = (f32[20,2,128]{2,1,0:T(2,128)S(1)}, f32[20,2,128]{2,1,0:T(2,128)S(1)}, u32[]{:S(2)}, u32[]{:S(2)}) collective-permute-start(f32[20,2,128]{2,1,0:T(2,128)S(1)} %get-tuple-element.18), channel_id=1, source_target_pairs={{1,0},{2,1},{3,2},{5,4},{6,5},{7,6},{9,8},{10,9},{11,10},{13,12},{... | collective-permute-start | bytes 61448 | tf_op jit(solution)/shard_map/ppermute | solution.py:275
  34.9 10.4 %collective-permute-start.4 = (f32[240,128]{1,0:T(8,128)S(1)}, f32[240,128]{1,0:T(8,128)S(1)}, u32[]{:S(2)}, u32[]{:S(2)}) collective-permute-start(f32[240,128]{1,0:T(8,128)S(1)} %get-tuple-element.45), channel_id=1, source_target_pairs={{0,4},{4,8},{8,12},{12,16},{16,20},{20,24},{24,28},{1,5},{5,9},{9,... | collective-permute-start | bytes 368648 | tf_op jit(solution)/shard_map/ppermute | solution.py:275
  37.9 9.3 %collective-permute-start.5 = (f32[240,128]{1,0:T(8,128)S(1)}, f32[240,128]{1,0:T(8,128)S(1)}, u32[]{:S(2)}, u32[]{:S(2)}) collective-permute-start(f32[240,128]{1,0:T(8,128)S(1)} %get-tuple-element.44), channel_id=1, source_target_pairs={{4,0},{8,4},{12,8},{16,12},{20,16},{24,20},{28,24},{5,1},{9,5},{13... | collective-permute-start | bytes 368648 | tf_op jit(solution)/shard_map/ppermute | solution.py:275
  55.7 5.8 %collective-permute-start.6 = (f32[2,144,128]{2,1,0:T(8,128)S(1)}, f32[2,144,128]{2,1,0:T(8,128)S(1)}, u32[]{:S(2)}, u32[]{:S(2)}) collective-permute-start(f32[2,144,128]{2,1,0:T(8,128)S(1)} %bitcast.28), channel_id=1, source_target_pairs={{0,32},{32,64},{64,96},{96,128},{128,160},{160,192},{192,224},{224... | collective-permute-start | bytes 442376 | tf_op jit(solution)/shard_map/ppermute | solution.py:279
  57.2 4.2 %collective-permute-start.7 = (f32[2,144,128]{2,1,0:T(8,128)S(1)}, f32[2,144,128]{2,1,0:T(8,128)S(1)}, u32[]{:S(2)}, u32[]{:S(2)}) collective-permute-start(f32[2,144,128]{2,1,0:T(8,128)S(1)} %bitcast.27), channel_id=1, source_target_pairs={{32,0},{64,32},{96,64},{128,96},{160,128},{192,160},{224,192},{256... | collective-permute-start | bytes 442376 | tf_op jit(solution)/shard_map/ppermute | solution.py:279
  61.5 6.5 %collective-permute-start.8 = (f32[16,2,128]{2,1,0:T(2,128)S(1)}, f32[16,2,128]{2,1,0:T(2,128)S(1)}, u32[]{:S(2)}, u32[]{:S(2)}) collective-permute-start(f32[16,2,128]{2,1,0:T(2,128)S(1)} %pad_maximum_fusion.7), channel_id=1, source_target_pairs={{0,1},{1,2},{2,3},{4,5},{5,6},{6,7},{8,9},{9,10},{10,11},{12,13},{... | collective-permute-start | bytes 49160 | tf_op jit(solution)/shard_map/ppermute | solution.py:275
  65.0 5.6 %collective-permute-start.9 = (f32[16,2,128]{2,1,0:T(2,128)S(1)}, f32[16,2,128]{2,1,0:T(2,128)S(1)}, u32[]{:S(2)}, u32[]{:S(2)}) collective-permute-start(f32[16,2,128]{2,1,0:T(2,128)S(1)} %pad_maximum_fusion.8), channel_id=1, source_target_pairs={{1,0},{2,1},{3,2},{5,4},{6,5},{7,6},{9,8},{10,9},{11,10},{13,12},{... | collective-permute-start | bytes 49160 | tf_op jit(solution)/shard_map/ppermute | solution.py:275
  71.0 5.1 %collective-permute-start.10 = (f32[4,16,2,128]{3,2,1,0:T(2,128)S(1)}, f32[4,16,2,128]{3,2,1,0:T(2,128)S(1)}, u32[]{:S(2)}, u32[]{:S(2)}) collective-permute-start(f32[4,16,2,128]{3,2,1,0:T(2,128)S(1)} %get-tuple-element.24), channel_id=1, source_target_pairs={{0,4},{4,8},{8,12},{12,16},{16,20},{20,24},{24,28},{1,5},{5,9},{9,... | collective-permute-start | bytes 196616 | tf_op jit(solution)/shard_map/ppermute | solution.py:275
  74.2 6.2 %collective-permute-start.11 = (f32[4,16,2,128]{3,2,1,0:T(2,128)S(1)}, f32[4,16,2,128]{3,2,1,0:T(2,128)S(1)}, u32[]{:S(2)}, u32[]{:S(2)}) collective-permute-start(f32[4,16,2,128]{3,2,1,0:T(2,128)S(1)} %get-tuple-element.25), channel_id=1, source_target_pairs={{4,0},{8,4},{12,8},{16,12},{20,16},{24,20},{28,24},{5,1},{9,5},{13... | collective-permute-start | bytes 196616 | tf_op jit(solution)/shard_map/ppermute | solution.py:275

commit v6 on v5

--- a/solution.py
+++ b/solution.py
@@ -77,24 +77,48 @@
         hi_ref[x] = flat[cells_z - 2 : cells_z]
 
 
+SIDE = 8
+
+
+def yface_kernel(gas_ref, xl_ref, xh_ref, zl_ref, zh_ref, lo_ref, hi_ref):
+    cells_x, cells_y = gas_ref.shape[1], gas_ref.shape[2]
+    planes = cells_x + 4
+    each = planes // (SIDE // 2)
+    for ref, at in ((lo_ref, 0), (hi_ref, cells_y - 2)):
+        for k in range(4):
+            ref[k * planes : k * planes + 2] = xl_ref[k, :, at : at + 2, :]
+            ref[k * planes + 2 : k * planes + 2 + cells_x] = gas_ref[k, :, at : at + 2, :]
+            ref[k * planes + 2 + cells_x : (k + 1) * planes] = xh_ref[k, :, at : at + 2, :]
+        total = None
+        for m in range(SIDE):
+            z_ref, first = (zl_ref, m) if m < SIDE // 2 else (zh_ref, m - SIDE // 2)
+            rows = z_ref[first * each : (first + 1) * each].reshape(2 * each, LANES)
+            rows = pltpu.roll(rows, (4 * m - 2 - at) % LANES, 1)
+            y = iota(rows.shape, 1) % YS
+            total = jnp.where((y >= 4 * m) & (y < 4 * m + 2), rows, 0.0 if total is None else total)
+        ref[4 * planes : 4 * planes + each] = total.reshape(each, 2, LANES)
+
+
 def turn_kernel(gas_ref, xl_ref, xh_ref, zl_ref, zh_ref, yl_ref, yh_ref, out_ref, buf):
     planes, cells_y, cells_z = out_ref.shape[0], gas_ref.shape[2], gas_ref.shape[3]
+    each = planes // (SIDE // 2)
     buf[...] = jnp.zeros_like(buf)
     fill_rows(buf, gas_ref, xl_ref, xh_ref)
-    y = iota((2, LANES), 1) % YS
     for x in range(planes):
         for k in range(4):
-            row = (k * planes + x) * 2
-            buf[x, k * YS : k * YS + 2, :] = yl_ref[row : row + 2]
-            buf[x, k * YS + 2 + cells_y : k * YS + 4 + cells_y, :] = yh_ref[row : row + 2]
-        for part, z_ref in enumerate((zl_ref, zh_ref)):
-            row = (4 + part) * planes * 2 + x * 2
-            below = pltpu.roll(yl_ref[row : row + 2], LANES - cells_y, 1)
-            above = pltpu.roll(yh_ref[row : row + 2], cells_y, 1)
-            at = ZO - 2 + part * (cells_z + 2)
-            out_ref[x, at : at + 2, :] = jnp.where(
-                y < 2, below, jnp.where(y < 2 + cells_y, z_ref[x], jnp.where(y < 4 + cells_y, above, 0.0))
-            )
+            buf[x, k * YS : k * YS + 2, :] = yl_ref[k * planes + x]
+            buf[x, k * YS + 2 + cells_y : k * YS + 4 + cells_y, :] = yh_ref[k * planes + x]
+    below, above = (ref[4 * planes : 4 * planes + each].reshape(2 * each, LANES) for ref in (yl_ref, yh_ref))
+    y = iota((2 * each, LANES), 1) % YS
+    for m in range(SIDE):
+        z_ref, first = (zl_ref, m) if m < SIDE // 2 else (zh_ref, m - SIDE // 2)
+        inner = z_ref[first * each : (first + 1) * each].reshape(2 * each, LANES)
+        low = pltpu.roll(below, -4 * m % LANES, 1)
+        high = pltpu.roll(above, (2 + cells_y - 4 * m) % LANES, 1)
+        rows = jnp.where(y < 2, low, jnp.where(y < 2 + cells_y, inner, jnp.where(y < 4 + cells_y, high, 0.0)))
+        at = ZO - 2 if m < SIDE // 2 else ZO + cells_z
+        for x in range(each):
+            out_ref[first * each + x, at : at + 2, :] = rows[2 * x : 2 * x + 2]
     for x in range(planes):
         out_ref[x, ZO : ZO + cells_z, :] = buf[x].T
 
@@ -265,6 +289,19 @@
             out_ref[k, x] = flat[k * YS + 2 : k * YS + 2 + cells_y]
             ylo_ref[k, x] = flat[k * YS : k * YS + 2]
             yhi_ref[k, x] = flat[k * YS + 2 + cells_y : k * YS + 4 + cells_y]
+
+
+def last_kernel(rows_ref, below_ref, above_ref, out_hbm, buf, sems):
+    cells_y = rows_ref.shape[2]
+    copies = []
+    for k in range(4):
+        buf[k] = rows_ref[k]
+        buf[k, :, 0:2, :] += below_ref[k]
+        buf[k, :, cells_y - 2 : cells_y, :] += above_ref[k]
+        copies.append(pltpu.make_async_copy(buf.at[k], out_hbm.at[k], sems.at[k]))
+        copies[-1].start()
+    for copy in copies:
+        copy.wait()
 
 
 def shift_pair(to_low, to_high, axis, ring=False):
@@ -347,14 +384,12 @@
     z_lo, z_hi = call(edge_kernel, [arr(planes, 2, LANES)] * 2, rows_buf)(gas_state, x_low, x_high)
     z_low, z_high = shift_pair(z_lo, z_hi, "gz")
 
-    def y_face(lo):
-        parts = [part[:, :, lo : lo + 2] for part in (x_low, gas_state, x_high)]
-        face = jnp.concatenate(parts, axis=1).reshape(8 * planes, nz)
-        return jnp.concatenate([face, z_low.reshape(2 * planes, LANES), z_high.reshape(2 * planes, LANES)], axis=0)
-
-    y_low, y_high = shift_pair(y_face(0), y_face(ny - 2), "gy")
+    around = (gas_state, x_low, x_high, z_low, z_high)
+    pairs = 4 * planes + planes // (SIDE // 2)
+    y_lo, y_hi = call(yface_kernel, [arr(pairs, 2, nz)] * 2)(*around)
+    y_low, y_high = shift_pair(y_lo, y_hi, "gy")
     padded = call(turn_kernel, arr(planes, ZR, LANES), rows_buf)(
-        gas_state, x_low, x_high, z_low, z_high, y_low, y_high
+        *around, y_low, y_high
     )
 
     weight = shell_weight.reshape(LANES, 4, 4, 8).transpose(2, 1, 3, 0).reshape(LANES, LANES)
@@ -378,9 +413,12 @@
         [pltpu.VMEM((nx, nz, LANES), F32)],
     )(total, base, from_low, from_high, z_below, z_above)
     y_below, y_above = shift_pair(y_lo, y_hi, "gy")
-    gas_next = jnp.concatenate(
-        [rows_out[:, :, :2] + y_below, rows_out[:, :, 2 : ny - 2], rows_out[:, :, ny - 2 :] + y_above], axis=2
-    )
+    gas_next = call(
+        last_kernel,
+        arr(4, nx, ny, nz),
+        [pltpu.VMEM((4, nx, ny, nz), F32), pltpu.SemaphoreType.DMA((4,))],
+        out_specs=pl.BlockSpec(memory_space=pl.ANY),
+    )(rows_out, y_below, y_above)
     return parcels_next, gas_next
 
 

time: 81.8 us -> 81.9 us (level)
  other arithmetic: 1.15 us -> 0.07 us
  Pallas kernels: 12 us -> 13 us
    concatenate x4 -> x0, other arithmetic: 0.99 us -> none  [the longest x1 0.9 us: per_device(): jnp.concatenate([rows_out[:, :, :2] + y_below, rows_out[:, :, 2:ny - 2],...]
    pallas_call x1 -> x3, Pallas kernels: 0.51 us -> 1.43 us  [the longest x1 0.85 us: per_device(): call(last_kernel, arr(4, nx, ny, nz), [pltpu.VMEM((4, nx, ny, nz), F32),...]
    all_to_all x1, waiting for transfers between devices: 0.75 us -> 1.66 us  [per_device(): lax.all_to_all(send.reshape(blocks, ROWS * LANES), ('gx', 'gy'), split_ax...]
  transfers between devices with their start and end apart: 13 -> 13, of which waited for: 8 -> 8; matrix products, arithmetic and copies ran while one was open for 0% -> 0% of each run, Pallas kernels for 5% -> 6%
where the time goes in v6:
time: 81.9 us; the launch traced here: 81.4 us
  starting transfers between devices  44.3 us (54%)
  waiting for transfers between devices  22 us (27%)
  Pallas kernels  13 us (16%)
  local copies, waits for them, and re-layouts  1 us (1%)
  between operations  0.9 us (1%)
    ppermute x8, starting transfers between devices, shift_pair(): return (lax.ppermute(to_high, axis, up), lax.ppermute(to_low, axis, down))  20.5 us
    all_to_all x1, starting transfers between devices, per_device(): lax.all_to_all(send.reshape(blocks, ROWS * LANES), ('gx', 'gy'), split_ax...  17.9 us
    ppermute x8, waiting for transfers between devices, shift_pair(): return (lax.ppermute(to_high, axis, up), lax.ppermute(to_low, axis, down))  17.6 us
    pallas_call x1, Pallas kernels, parcels(): call(parcel_kernel, [arr(5, 2 * blocks, LANES), arr(nx * ZR, LANES), arr(...  7.29 us
    ppermute x2, starting transfers between devices, shift_pair(): lax.ppermute(to_low, axis, down)  4.43 us
    pallas_call x1, Pallas kernels, per_device(): call(pack_kernel, arr(blocks * ROWS, LANES), [pltpu.VMEM((1, blocks), jnp...  2.86 us
    ppermute x2, waiting for transfers between devices, shift_pair(): lax.ppermute(to_high, axis, up)  2.81 us
    all_to_all x1, waiting for transfers between devices, per_device(): lax.all_to_all(send.reshape(blocks, ROWS * LANES), ('gx', 'gy'), split_ax...  1.66 us
  transfers between devices with their start and end apart: 13, of which 8 were waited for; matrix products, arithmetic and copies ran while one was open for 0% of the time, Pallas kernels for 6%

profile of v6, /device:TPU:2, one launch (start us, length us, event | category | flops | bytes accessed | tf_op | source)
XLA Modules:
  0.0 81.4 jit_solution(16959162255670246476)
XLA Ops:
  0.6 0.9 %fusion.1 = (f32[4,2,16,128]{3,2,1,0:T(8,128)S(1)}, f32[4,2,16,128]{3,2,1,0:T(8,128)S(1)}) fusion(f32[4,16,16,128]{3,2,1,0:T(8,128)} %gas_ref.5), kind=kLoop, calls=%fused_computation.11 | loop fusion | bytes 262144 | tf_op jit(solution)/shard_map/slice | solution.py:359
  1.5 2.9 %collective-permute-start.1 = (f32[4,2,16,128]{3,2,1,0:T(8,128)S(1)}, f32[4,2,16,128]{3,2,1,0:T(8,128)S(1)}, u32[]{:S(2)}, u32[]{:S(2)}) collective-permute-start(f32[4,2,16,128]{3,2,1,0:T(8,128)S(1)} %get-tuple-element.38), channel_id=1, source_target_pairs={{32,0},{64,32},{96,64},{128,96},{160,128},{192,160},{224,192},{256... | collective-permute-start | bytes 196616 | tf_op jit(solution)/shard_map/ppermute | solution.py:316
  4.5 2.9 %shard_map.86 = f32[1408,128]{1,0:T(8,128)} custom-call(s32[1,128]{1,0:T(1,128)} %bitcast.26, s32[1,128]{1,0:T(1,128)} %bitcast.27, s32[1,128]{1,0:T(1,128)} %bitcast.28, f32[3,128,128]{2,1,0:T(8,128)} %bitcast.25, f32[128,2,128]{2,1,0:T(2,128)} %prop_hbm.1), custom_call_target="tpu_custom_call" | custom-call | tf_op jit(solution)/shard_map/pallas_call | solution.py:360
  7.4 17.9 %all-to-all-start = ((f32[128,1,1408]{2,1,0:T(1,128)}), f32[128,1,1408]{2,1,0:T(1,128)S(1)}, u32[]{:S(2)}, u32[]{:S(2)}) async-start(f32[128,1,1408]{2,1,0:T(1,128)} %bitcast.23), calls=%async_computation | async-start | bytes 1441792 | tf_op jit(solution)/shard_map/all_to_all | solution.py:379
  25.9 3.4 %collective-permute-start.2 = (f32[20,2,128]{2,1,0:T(2,128)S(1)}, f32[20,2,128]{2,1,0:T(2,128)S(1)}, u32[]{:S(2)}, u32[]{:S(2)}) collective-permute-start(f32[20,2,128]{2,1,0:T(2,128)S(1)} %get-tuple-element.19), channel_id=1, source_target_pairs={{0,1},{1,2},{2,3},{4,5},{5,6},{6,7},{8,9},{9,10},{10,11},{12,13},{... | collective-permute-start | bytes 61448 | tf_op jit(solution)/shard_map/ppermute | solution.py:312
  29.3 2.4 %collective-permute-start.3 = (f32[20,2,128]{2,1,0:T(2,128)S(1)}, f32[20,2,128]{2,1,0:T(2,128)S(1)}, u32[]{:S(2)}, u32[]{:S(2)}) collective-permute-start(f32[20,2,128]{2,1,0:T(2,128)S(1)} %get-tuple-element.20), channel_id=1, source_target_pairs={{1,0},{2,1},{3,2},{5,4},{6,5},{7,6},{9,8},{10,9},{11,10},{13,12},{... | collective-permute-start | bytes 61448 | tf_op jit(solution)/shard_map/ppermute | solution.py:312
  31.7 3.2 %collective-permute-done.3.zh_ref = f32[20,2,128]{2,1,0:T(2,128)S(1)} collective-permute-done((f32[20,2,128]{2,1,0:T(2,128)S(1)}, f32[20,2,128]{2,1,0:T(2,128)S(1)}, u32[]{:S(2)}, u32[]{:S(2)}) %collective-permute-start.3) | collective-permute-done | bytes 20512 | tf_op jit(solution)/shard_map/ppermute | solution.py:312
  35.1 3.0 %collective-permute-start.4 = (f32[85,2,128]{2,1,0:T(2,128)S(1)}, f32[85,2,128]{2,1,0:T(2,128)S(1)}, u32[]{:S(2)}, u32[]{:S(2)}) collective-permute-start(f32[85,2,128]{2,1,0:T(2,128)S(1)} %get-tuple-element.21), channel_id=1, source_target_pairs={{0,4},{4,8},{8,12},{12,16},{16,20},{20,24},{24,28},{1,5},{5,9},{9,... | collective-permute-start | bytes 261128 | tf_op jit(solution)/shard_map/ppermute | solution.py:312
  38.1 1.3 %collective-permute-start.5 = (f32[85,2,128]{2,1,0:T(2,128)S(1)}, f32[85,2,128]{2,1,0:T(2,128)S(1)}, u32[]{:S(2)}, u32[]{:S(2)}) collective-permute-start(f32[85,2,128]{2,1,0:T(2,128)S(1)} %get-tuple-element.22), channel_id=1, source_target_pairs={{4,0},{8,4},{12,8},{16,12},{20,16},{24,20},{28,24},{5,1},{9,5},{13... | collective-permute-start | bytes 261128 | tf_op jit(solution)/shard_map/ppermute | solution.py:312
  39.5 4.9 %collective-permute-done.4.yl_ref = f32[85,2,128]{2,1,0:T(2,128)S(1)} collective-permute-done((f32[85,2,128]{2,1,0:T(2,128)S(1)}, f32[85,2,128]{2,1,0:T(2,128)S(1)}, u32[]{:S(2)}, u32[]{:S(2)}) %collective-permute-start.4) | collective-permute-done | bytes 87072 | tf_op jit(solution)/shard_map/ppermute | solution.py:312
  44.4 2.0 %collective-permute-done.5.yh_ref = f32[85,2,128]{2,1,0:T(2,128)S(1)} collective-permute-done((f32[85,2,128]{2,1,0:T(2,128)S(1)}, f32[85,2,128]{2,1,0:T(2,128)S(1)}, u32[]{:S(2)}, u32[]{:S(2)}) %collective-permute-start.5) | collective-permute-done | bytes 87072 | tf_op jit(solution)/shard_map/ppermute | solution.py:312
  47.0 1.7 %all-to-all-done = f32[128,1,1408]{2,1,0:T(1,128)S(1)} async-done(((f32[128,1,1408]{2,1,0:T(1,128)}), f32[128,1,1408]{2,1,0:T(1,128)S(1)}, u32[]{:S(2)}, u32[]{:S(2)}) %all-to-all-start) | async-done | bytes 720928 | tf_op jit(solution)/shard_map/all_to_all | solution.py:379
  48.6 7.3 %shard_map.90 = (f32[5,256,128]{2,1,0:T(8,128)}, f32[2304,128]{1,0:T(8,128)S(1)}, f32[288,128]{1,0:T(8,128)S(1)}, f32[288,128]{1,0:T(8,128)S(1)}) custom-call(f32[1408,128]{1,0:T(8,128)S(1)} %bitcast.16, f32[2880,128]{1,0:T(8,128)S(1)} %bitcast.15, f32[128,128]{1,0:T(8,128)S(1)} %bitcast.20), custom_call_target="tpu_custom_call" | custom-call | tf_op jit(solution)/shard_map/pallas_call | solution.py:338
  55.9 1.5 %collective-permute-start.6 = (f32[2,144,128]{2,1,0:T(8,128)S(1)}, f32[2,144,128]{2,1,0:T(8,128)S(1)}, u32[]{:S(2)}, u32[]{:S(2)}) collective-permute-start(f32[2,144,128]{2,1,0:T(8,128)S(1)} %bitcast.22), channel_id=1, source_target_pairs={{0,32},{32,64},{64,96},{96,128},{128,160},{160,192},{192,224},{224... | collective-permute-start | bytes 442376 | tf_op jit(solution)/shard_map/ppermute | solution.py:316
  57.4 1.5 %collective-permute-start.7 = (f32[2,144,128]{2,1,0:T(8,128)S(1)}, f32[2,144,128]{2,1,0:T(8,128)S(1)}, u32[]{:S(2)}, u32[]{:S(2)}) collective-permute-start(f32[2,144,128]{2,1,0:T(8,128)S(1)} %bitcast.21), channel_id=1, source_target_pairs={{32,0},{64,32},{96,64},{128,96},{160,128},{192,160},{224,192},{256... | collective-permute-start | bytes 442376 | tf_op jit(solution)/shard_map/ppermute | solution.py:316
  58.9 2.8 %collective-permute-done.6 = f32[2,144,128]{2,1,0:T(8,128)S(1)} collective-permute-done((f32[2,144,128]{2,1,0:T(8,128)S(1)}, f32[2,144,128]{2,1,0:T(8,128)S(1)}, u32[]{:S(2)}, u32[]{:S(2)}) %collective-permute-start.6) | collective-permute-done | bytes 147488 | tf_op jit(solution)/shard_map/ppermute | solution.py:316
  61.8 3.4 %collective-permute-start.8 = (f32[16,2,128]{2,1,0:T(2,128)S(1)}, f32[16,2,128]{2,1,0:T(2,128)S(1)}, u32[]{:S(2)}, u32[]{:S(2)}) collective-permute-start(f32[16,2,128]{2,1,0:T(2,128)S(1)} %pad_maximum_fusion), channel_id=1, source_target_pairs={{0,1},{1,2},{2,3},{4,5},{5,6},{6,7},{8,9},{9,10},{10,11},{12,13},{... | collective-permute-start | bytes 49160 | tf_op jit(solution)/shard_map/ppermute | solution.py:312
  65.2 2.5 %collective-permute-start.9 = (f32[16,2,128]{2,1,0:T(2,128)S(1)}, f32[16,2,128]{2,1,0:T(2,128)S(1)}, u32[]{:S(2)}, u32[]{:S(2)}) collective-permute-start(f32[16,2,128]{2,1,0:T(2,128)S(1)} %pad_maximum_fusion.1), channel_id=1, source_target_pairs={{1,0},{2,1},{3,2},{5,4},{6,5},{7,6},{9,8},{10,9},{11,10},{13,12},{... | collective-permute-start | bytes 49160 | tf_op jit(solution)/shard_map/ppermute | solution.py:312
  67.7 0.6 shard_map.91.base_ref
  68.3 2.5 %collective-permute-done.9.zh_ref = f32[16,2,128]{2,1,0:T(2,128)S(1)} collective-permute-done((f32[16,2,128]{2,1,0:T(2,128)S(1)}, f32[16,2,128]{2,1,0:T(2,128)S(1)}, u32[]{:S(2)}, u32[]{:S(2)}) %collective-permute-start.9) | collective-permute-done | bytes 16416 | tf_op jit(solution)/shard_map/ppermute | solution.py:312
  71.2 3.2 %collective-permute-start.10 = (f32[4,16,2,128]{3,2,1,0:T(2,128)S(1)}, f32[4,16,2,128]{3,2,1,0:T(2,128)S(1)}, u32[]{:S(2)}, u32[]{:S(2)}) collective-permute-start(f32[4,16,2,128]{3,2,1,0:T(2,128)S(1)} %get-tuple-element.28), channel_id=1, source_target_pairs={{0,4},{4,8},{8,12},{12,16},{16,20},{20,24},{24,28},{1,5},{5,9},{9,... | collective-permute-start | bytes 196616 | tf_op jit(solution)/shard_map/ppermute | solution.py:312
  74.4 1.3 %collective-permute-start.11 = (f32[4,16,2,128]{3,2,1,0:T(2,128)S(1)}, f32[4,16,2,128]{3,2,1,0:T(2,128)S(1)}, u32[]{:S(2)}, u32[]{:S(2)}) collective-permute-start(f32[4,16,2,128]{3,2,1,0:T(2,128)S(1)} %get-tuple-element.29), channel_id=1, source_target_pairs={{4,0},{8,4},{12,8},{16,12},{20,16},{24,20},{28,24},{5,1},{9,5},{13... | collective-permute-start | bytes 196616 | tf_op jit(solution)/shard_map/ppermute | solution.py:312
  76.3 4.3 %collective-permute-done.11.above_ref = f32[4,16,2,128]{3,2,1,0:T(2,128)S(1)} collective-permute-done((f32[4,16,2,128]{3,2,1,0:T(2,128)S(1)}, f32[4,16,2,128]{3,2,1,0:T(2,128)S(1)}, u32[]{:S(2)}, u32[]{:S(2)}) %collective-permute-start.11) | collective-permute-done | bytes 65568 | tf_op jit(solution)/shard_map/ppermute | solution.py:312
  80.5 0.8 %shard_map.93 = f32[4,16,16,128]{3,2,1,0:T(8,128)} custom-call(f32[4,16,16,128]{3,2,1,0:T(8,128)S(1)} %get-tuple-element.27.rows_ref, f32[4,16,2,128]{3,2,1,0:T(2,128)S(1)} %collective-permute-done.10.below_ref, f32[4,16,2,128]{3,2,1,0:T(2,128)S(1)} %collective-permute-done.11.above_ref), custom_call_target="tpu_custom_call" | custom-call | tf_op jit(solution)/shard_map/pallas_call | solution.py:416
  (25 shorter events, 2.2 us)
Async XLA Ops:
  1.5 5.8 %collective-permute-start = (f32[4,2,16,128]{3,2,1,0:T(8,128)S(1)}, f32[4,2,16,128]{3,2,1,0:T(8,128)S(1)}, u32[]{:S(2)}, u32[]{:S(2)}) collective-permute-start(f32[4,2,16,128]{3,2,1,0:T(8,128)S(1)} %get-tuple-element.39), channel_id=1, source_target_pairs={{0,32},{32,64},{64,96},{96,128},{128,160},{160,192},{192,224},{224... | collective-permute-start | bytes 196616 | tf_op jit(solution)/shard_map/ppermute | solution.py:316
  1.5 5.8 %collective-permute-start.1 = (f32[4,2,16,128]{3,2,1,0:T(8,128)S(1)}, f32[4,2,16,128]{3,2,1,0:T(8,128)S(1)}, u32[]{:S(2)}, u32[]{:S(2)}) collective-permute-start(f32[4,2,16,128]{3,2,1,0:T(8,128)S(1)} %get-tuple-element.38), channel_id=1, source_target_pairs={{32,0},{64,32},{96,64},{128,96},{160,128},{192,160},{224,192},{256... | collective-permute-start | bytes 196616 | tf_op jit(solution)/shard_map/ppermute | solution.py:316
  4.5 20.9 %copy-start = (f32[4,16,16,128]{3,2,1,0:T(8,128)S(1)}, f32[4,16,16,128]{3,2,1,0:T(8,128)}, u32[]{:S(2)}) copy-start(f32[4,16,16,128]{3,2,1,0:T(8,128)} %gas_ref.5) | copy-start | bytes 1572868
  7.4 32.0 %copy-start.1 = (f32[128,128]{1,0:T(8,128)S(1)}, f32[128,128]{1,0:T(8,128)}, u32[]{:S(2)}) copy-start(f32[128,128]{1,0:T(8,128)} %param.12) | copy-start | bytes 196612
  7.4 41.2 %all-to-all-start = ((f32[128,1,1408]{2,1,0:T(1,128)}), f32[128,1,1408]{2,1,0:T(1,128)S(1)}, u32[]{:S(2)}, u32[]{:S(2)}) async-start(f32[128,1,1408]{2,1,0:T(1,128)} %bitcast.23), calls=%async_computation | async-start | bytes 1441792 | tf_op jit(solution)/shard_map/all_to_all | solution.py:379
  25.9 5.9 %collective-permute-start.2 = (f32[20,2,128]{2,1,0:T(2,128)S(1)}, f32[20,2,128]{2,1,0:T(2,128)S(1)}, u32[]{:S(2)}, u32[]{:S(2)}) collective-permute-start(f32[20,2,128]{2,1,0:T(2,128)S(1)} %get-tuple-element.19), channel_id=1, source_target_pairs={{0,1},{1,2},{2,3},{4,5},{5,6},{6,7},{8,9},{9,10},{10,11},{12,13},{... | collective-permute-start | bytes 61448 | tf_op jit(solution)/shard_map/ppermute | solution.py:312
  29.3 5.7 %collective-permute-start.3 = (f32[20,2,128]{2,1,0:T(2,128)S(1)}, f32[20,2,128]{2,1,0:T(2,128)S(1)}, u32[]{:S(2)}, u32[]{:S(2)}) collective-permute-start(f32[20,2,128]{2,1,0:T(2,128)S(1)} %get-tuple-element.20), channel_id=1, source_target_pairs={{1,0},{2,1},{3,2},{5,4},{6,5},{7,6},{9,8},{10,9},{11,10},{13,12},{... | collective-permute-start | bytes 61448 | tf_op jit(solution)/shard_map/ppermute | solution.py:312
  35.1 9.4 %collective-permute-start.4 = (f32[85,2,128]{2,1,0:T(2,128)S(1)}, f32[85,2,128]{2,1,0:T(2,128)S(1)}, u32[]{:S(2)}, u32[]{:S(2)}) collective-permute-start(f32[85,2,128]{2,1,0:T(2,128)S(1)} %get-tuple-element.21), channel_id=1, source_target_pairs={{0,4},{4,8},{8,12},{12,16},{16,20},{20,24},{24,28},{1,5},{5,9},{9,... | collective-permute-start | bytes 261128 | tf_op jit(solution)/shard_map/ppermute | solution.py:312
  38.1 8.4 %collective-permute-start.5 = (f32[85,2,128]{2,1,0:T(2,128)S(1)}, f32[85,2,128]{2,1,0:T(2,128)S(1)}, u32[]{:S(2)}, u32[]{:S(2)}) collective-permute-start(f32[85,2,128]{2,1,0:T(2,128)S(1)} %get-tuple-element.22), channel_id=1, source_target_pairs={{4,0},{8,4},{12,8},{16,12},{20,16},{24,20},{28,24},{5,1},{9,5},{13... | collective-permute-start | bytes 261128 | tf_op jit(solution)/shard_map/ppermute | solution.py:312
  55.9 5.8 %collective-permute-start.6 = (f32[2,144,128]{2,1,0:T(8,128)S(1)}, f32[2,144,128]{2,1,0:T(8,128)S(1)}, u32[]{:S(2)}, u32[]{:S(2)}) collective-permute-start(f32[2,144,128]{2,1,0:T(8,128)S(1)} %bitcast.22), channel_id=1, source_target_pairs={{0,32},{32,64},{64,96},{96,128},{128,160},{160,192},{192,224},{224... | collective-permute-start | bytes 442376 | tf_op jit(solution)/shard_map/ppermute | solution.py:316
  57.4 4.3 %collective-permute-start.7 = (f32[2,144,128]{2,1,0:T(8,128)S(1)}, f32[2,144,128]{2,1,0:T(8,128)S(1)}, u32[]{:S(2)}, u32[]{:S(2)}) collective-permute-start(f32[2,144,128]{2,1,0:T(8,128)S(1)} %bitcast.21), channel_id=1, source_target_pairs={{32,0},{64,32},{96,64},{128,96},{160,128},{192,160},{224,192},{256... | collective-permute-start | bytes 442376 | tf_op jit(solution)/shard_map/ppermute | solution.py:316
  61.8 6.5 %collective-permute-start.8 = (f32[16,2,128]{2,1,0:T(2,128)S(1)}, f32[16,2,128]{2,1,0:T(2,128)S(1)}, u32[]{:S(2)}, u32[]{:S(2)}) collective-permute-start(f32[16,2,128]{2,1,0:T(2,128)S(1)} %pad_maximum_fusion), channel_id=1, source_target_pairs={{0,1},{1,2},{2,3},{4,5},{5,6},{6,7},{8,9},{9,10},{10,11},{12,13},{... | collective-permute-start | bytes 49160 | tf_op jit(solution)/shard_map/ppermute | solution.py:312
  65.2 5.6 %collective-permute-start.9 = (f32[16,2,128]{2,1,0:T(2,128)S(1)}, f32[16,2,128]{2,1,0:T(2,128)S(1)}, u32[]{:S(2)}, u32[]{:S(2)}) collective-permute-start(f32[16,2,128]{2,1,0:T(2,128)S(1)} %pad_maximum_fusion.1), channel_id=1, source_target_pairs={{1,0},{2,1},{3,2},{5,4},{6,5},{7,6},{9,8},{10,9},{11,10},{13,12},{... | collective-permute-start | bytes 49160 | tf_op jit(solution)/shard_map/ppermute | solution.py:312
  71.2 5.1 %collective-permute-start.10 = (f32[4,16,2,128]{3,2,1,0:T(2,128)S(1)}, f32[4,16,2,128]{3,2,1,0:T(2,128)S(1)}, u32[]{:S(2)}, u32[]{:S(2)}) collective-permute-start(f32[4,16,2,128]{3,2,1,0:T(2,128)S(1)} %get-tuple-element.28), channel_id=1, source_target_pairs={{0,4},{4,8},{8,12},{12,16},{16,20},{20,24},{24,28},{1,5},{5,9},{9,... | collective-permute-start | bytes 196616 | tf_op jit(solution)/shard_map/ppermute | solution.py:312
  74.4 6.2 %collective-permute-start.11 = (f32[4,16,2,128]{3,2,1,0:T(2,128)S(1)}, f32[4,16,2,128]{3,2,1,0:T(2,128)S(1)}, u32[]{:S(2)}, u32[]{:S(2)}) collective-permute-start(f32[4,16,2,128]{3,2,1,0:T(2,128)S(1)} %get-tuple-element.29), channel_id=1, source_target_pairs={{4,0},{8,4},{12,8},{16,12},{20,16},{24,20},{28,24},{5,1},{9,5},{13... | collective-permute-start | bytes 196616 | tf_op jit(solution)/shard_map/ppermute | solution.py:312

commit v7 on v6

--- a/solution.py
+++ b/solution.py
@@ -24,7 +24,10 @@
     return lax.broadcasted_iota(jnp.int32, shape, dim)
 
 
-def pack_kernel(tgt_hbm, off_hbm, cnt_hbm, vel_hbm, prop_hbm, out_ref, tgt_ref, off_ref, cnt_ref, vel_ref, prop_ref, sems):
+def pack_kernel(
+    tgt_hbm, off_hbm, cnt_hbm, vel_hbm, prop_hbm, out_hbm,
+    tgt_ref, off_ref, cnt_ref, vel_ref, prop_ref, out_ref, sems, out_sems,
+):
     n = LANES
     pairs = ((tgt_hbm, tgt_ref), (off_hbm, off_ref), (cnt_hbm, cnt_ref), (vel_hbm, vel_ref), (prop_hbm, prop_ref))
     copies = [pltpu.make_async_copy(src, dst, sems.at[i]) for i, (src, dst) in enumerate(pairs)]
@@ -45,18 +48,32 @@
         column = jnp.sum(pick * val, axis=1, keepdims=True)
         head = jnp.where(lane == place, column, head)
     out_ref[pl.ds(10, n, stride=ROWS), :] = head
-    picks = jnp.concatenate([first, second], axis=0).astype(BF16)
     for copy in copies[3:]:
         copy.wait()
+    parts = []
     for k in range(5):
         x = vel_ref[k] if k < 3 else prop_ref[:, k - 3, :]
-        total = jnp.zeros((2 * n, n), F32)
-        for _ in range(3):
-            part = x.astype(BF16)
-            x = x - part.astype(F32)
-            total = total + jnp.dot(picks, part, preferred_element_type=F32)
-        out_ref[pl.ds(k, n, stride=ROWS), :] = total[:n]
-        out_ref[pl.ds(5 + k, n, stride=ROWS), :] = total[n:]
+        high = x.astype(BF16)
+        x = x - high.astype(F32)
+        middle = x.astype(BF16)
+        parts.append((jnp.concatenate([high, middle], axis=0), (x - middle.astype(F32)).astype(BF16)))
+    half = n // 2
+    leaving = []
+    for h in range(2):
+        lines = slice(h * half, (h + 1) * half)
+        picks = jnp.concatenate([first[lines], second[lines]], axis=0).astype(BF16)
+        picks_twice = jnp.concatenate([picks, picks], axis=1)
+        at = h * half * ROWS
+        for k, (upper, lower) in enumerate(parts):
+            total = jnp.dot(picks_twice, upper, preferred_element_type=F32)
+            total = total + jnp.dot(picks, lower, preferred_element_type=F32)
+            out_ref[pl.ds(at + k, half, stride=ROWS), :] = total[:half]
+            out_ref[pl.ds(at + 5 + k, half, stride=ROWS), :] = total[half:]
+        block = pl.ds(at, half * ROWS)
+        leaving.append(pltpu.make_async_copy(out_ref.at[block], out_hbm.at[block], out_sems.at[h]))
+        leaving[-1].start()
+    for copy in leaving:
+        copy.wait()
 
 
 def fill_rows(buf, gas_ref, xl_ref, xh_ref):
@@ -364,9 +381,12 @@
         + [
             pltpu.VMEM((3, blocks, LANES), F32),
             pltpu.VMEM((blocks, 2, LANES), F32),
+            pltpu.VMEM((blocks * ROWS, LANES), F32),
             pltpu.SemaphoreType.DMA((5,)),
+            pltpu.SemaphoreType.DMA((2,)),
         ],
         in_specs=[pl.BlockSpec(memory_space=pltpu.HBM)] * 5,
+        out_specs=pl.BlockSpec(memory_space=pltpu.HBM),
         vmem=NEARLY_ALL,
     )(
         owner_peer.reshape(1, blocks),

time: 81.9 us -> 81.8 us (level)
  no operation moved by 1% of the time
where the time goes in v7:
time: 81.8 us; the launch traced here: 81.4 us
  starting transfers between devices  44.3 us (54%)
  waiting for transfers between devices  22 us (27%)
  Pallas kernels  13 us (16%)
  local copies, waits for them, and re-layouts  1 us (1%)
  between operations  0.9 us (1%)
    ppermute x8, starting transfers between devices, shift_pair(): return (lax.ppermute(to_high, axis, up), lax.ppermute(to_low, axis, down))  20.5 us
    all_to_all x1, starting transfers between devices, per_device(): lax.all_to_all(send.reshape(blocks, ROWS * LANES), ('gx', 'gy'), split_ax...  17.9 us
    ppermute x8, waiting for transfers between devices, shift_pair(): return (lax.ppermute(to_high, axis, up), lax.ppermute(to_low, axis, down))  17.6 us
    pallas_call x1, Pallas kernels, parcels(): call(parcel_kernel, [arr(5, 2 * blocks, LANES), arr(nx * ZR, LANES), arr(...  7.29 us
    ppermute x2, starting transfers between devices, shift_pair(): lax.ppermute(to_low, axis, down)  4.43 us
    pallas_call x1, Pallas kernels, per_device(): call(pack_kernel, arr(blocks * ROWS, LANES), [pltpu.VMEM((1, blocks), jnp...  2.83 us
    ppermute x2, waiting for transfers between devices, shift_pair(): lax.ppermute(to_high, axis, up)  2.81 us
    all_to_all x1, waiting for transfers between devices, per_device(): lax.all_to_all(send.reshape(blocks, ROWS * LANES), ('gx', 'gy'), split_ax...  1.66 us
  transfers between devices with their start and end apart: 13, of which 8 were waited for; matrix products, arithmetic and copies ran while one was open for 0% of the time, Pallas kernels for 6%

profile of v7, /device:TPU:2, one launch (start us, length us, event | category | flops | bytes accessed | tf_op | source)
XLA Modules:
  0.0 81.4 jit_solution(2897774756702936951)
XLA Ops:
  0.6 0.9 %fusion.1 = (f32[4,2,16,128]{3,2,1,0:T(8,128)S(1)}, f32[4,2,16,128]{3,2,1,0:T(8,128)S(1)}) fusion(f32[4,16,16,128]{3,2,1,0:T(8,128)} %gas_ref.5), kind=kLoop, calls=%fused_computation.11 | loop fusion | bytes 262144 | tf_op jit(solution)/shard_map/slice | solution.py:376
  1.5 2.9 %collective-permute-start.1 = (f32[4,2,16,128]{3,2,1,0:T(8,128)S(1)}, f32[4,2,16,128]{3,2,1,0:T(8,128)S(1)}, u32[]{:S(2)}, u32[]{:S(2)}) collective-permute-start(f32[4,2,16,128]{3,2,1,0:T(8,128)S(1)} %get-tuple-element.38), channel_id=1, source_target_pairs={{32,0},{64,32},{96,64},{128,96},{160,128},{192,160},{224,192},{256... | collective-permute-start | bytes 196616 | tf_op jit(solution)/shard_map/ppermute | solution.py:333
  4.5 2.8 %shard_map.86 = f32[1408,128]{1,0:T(8,128)} custom-call(s32[1,128]{1,0:T(1,128)} %bitcast.26, s32[1,128]{1,0:T(1,128)} %bitcast.27, s32[1,128]{1,0:T(1,128)} %bitcast.28, f32[3,128,128]{2,1,0:T(8,128)} %bitcast.25, f32[128,2,128]{2,1,0:T(2,128)} %prop_hbm.1), custom_call_target="tpu_custom_call" | custom-call | tf_op jit(solution)/shard_map/pallas_call | solution.py:377
  7.4 17.9 %all-to-all-start = ((f32[128,1,1408]{2,1,0:T(1,128)}), f32[128,1,1408]{2,1,0:T(1,128)S(1)}, u32[]{:S(2)}, u32[]{:S(2)}) async-start(f32[128,1,1408]{2,1,0:T(1,128)} %bitcast.23), calls=%async_computation | async-start | bytes 1441792 | tf_op jit(solution)/shard_map/all_to_all | solution.py:399
  25.8 3.4 %collective-permute-start.2 = (f32[20,2,128]{2,1,0:T(2,128)S(1)}, f32[20,2,128]{2,1,0:T(2,128)S(1)}, u32[]{:S(2)}, u32[]{:S(2)}) collective-permute-start(f32[20,2,128]{2,1,0:T(2,128)S(1)} %get-tuple-element.19), channel_id=1, source_target_pairs={{0,1},{1,2},{2,3},{4,5},{5,6},{6,7},{8,9},{9,10},{10,11},{12,13},{... | collective-permute-start | bytes 61448 | tf_op jit(solution)/shard_map/ppermute | solution.py:329
  29.2 2.4 %collective-permute-start.3 = (f32[20,2,128]{2,1,0:T(2,128)S(1)}, f32[20,2,128]{2,1,0:T(2,128)S(1)}, u32[]{:S(2)}, u32[]{:S(2)}) collective-permute-start(f32[20,2,128]{2,1,0:T(2,128)S(1)} %get-tuple-element.20), channel_id=1, source_target_pairs={{1,0},{2,1},{3,2},{5,4},{6,5},{7,6},{9,8},{10,9},{11,10},{13,12},{... | collective-permute-start | bytes 61448 | tf_op jit(solution)/shard_map/ppermute | solution.py:329
  31.7 3.2 %collective-permute-done.3.zh_ref = f32[20,2,128]{2,1,0:T(2,128)S(1)} collective-permute-done((f32[20,2,128]{2,1,0:T(2,128)S(1)}, f32[20,2,128]{2,1,0:T(2,128)S(1)}, u32[]{:S(2)}, u32[]{:S(2)}) %collective-permute-start.3) | collective-permute-done | bytes 20512 | tf_op jit(solution)/shard_map/ppermute | solution.py:329
  35.0 3.0 %collective-permute-start.4 = (f32[85,2,128]{2,1,0:T(2,128)S(1)}, f32[85,2,128]{2,1,0:T(2,128)S(1)}, u32[]{:S(2)}, u32[]{:S(2)}) collective-permute-start(f32[85,2,128]{2,1,0:T(2,128)S(1)} %get-tuple-element.21), channel_id=1, source_target_pairs={{0,4},{4,8},{8,12},{12,16},{16,20},{20,24},{24,28},{1,5},{5,9},{9,... | collective-permute-start | bytes 261128 | tf_op jit(solution)/shard_map/ppermute | solution.py:329
  38.1 1.3 %collective-permute-start.5 = (f32[85,2,128]{2,1,0:T(2,128)S(1)}, f32[85,2,128]{2,1,0:T(2,128)S(1)}, u32[]{:S(2)}, u32[]{:S(2)}) collective-permute-start(f32[85,2,128]{2,1,0:T(2,128)S(1)} %get-tuple-element.22), channel_id=1, source_target_pairs={{4,0},{8,4},{12,8},{16,12},{20,16},{24,20},{28,24},{5,1},{9,5},{13... | collective-permute-start | bytes 261128 | tf_op jit(solution)/shard_map/ppermute | solution.py:329
  39.5 4.9 %collective-permute-done.4.yl_ref = f32[85,2,128]{2,1,0:T(2,128)S(1)} collective-permute-done((f32[85,2,128]{2,1,0:T(2,128)S(1)}, f32[85,2,128]{2,1,0:T(2,128)S(1)}, u32[]{:S(2)}, u32[]{:S(2)}) %collective-permute-start.4) | collective-permute-done | bytes 87072 | tf_op jit(solution)/shard_map/ppermute | solution.py:329
  44.4 2.0 %collective-permute-done.5.yh_ref = f32[85,2,128]{2,1,0:T(2,128)S(1)} collective-permute-done((f32[85,2,128]{2,1,0:T(2,128)S(1)}, f32[85,2,128]{2,1,0:T(2,128)S(1)}, u32[]{:S(2)}, u32[]{:S(2)}) %collective-permute-start.5) | collective-permute-done | bytes 87072 | tf_op jit(solution)/shard_map/ppermute | solution.py:329
  46.9 1.7 %all-to-all-done = f32[128,1,1408]{2,1,0:T(1,128)S(1)} async-done(((f32[128,1,1408]{2,1,0:T(1,128)}), f32[128,1,1408]{2,1,0:T(1,128)S(1)}, u32[]{:S(2)}, u32[]{:S(2)}) %all-to-all-start) | async-done | bytes 720928 | tf_op jit(solution)/shard_map/all_to_all | solution.py:399
  48.6 7.3 %shard_map.90 = (f32[5,256,128]{2,1,0:T(8,128)}, f32[2304,128]{1,0:T(8,128)S(1)}, f32[288,128]{1,0:T(8,128)S(1)}, f32[288,128]{1,0:T(8,128)S(1)}) custom-call(f32[1408,128]{1,0:T(8,128)S(1)} %bitcast.16, f32[2880,128]{1,0:T(8,128)S(1)} %bitcast.15, f32[128,128]{1,0:T(8,128)S(1)} %bitcast.20), custom_call_target="tpu_custom_call" | custom-call | tf_op jit(solution)/shard_map/pallas_call | solution.py:355
  55.9 1.5 %collective-permute-start.6 = (f32[2,144,128]{2,1,0:T(8,128)S(1)}, f32[2,144,128]{2,1,0:T(8,128)S(1)}, u32[]{:S(2)}, u32[]{:S(2)}) collective-permute-start(f32[2,144,128]{2,1,0:T(8,128)S(1)} %bitcast.22), channel_id=1, source_target_pairs={{0,32},{32,64},{64,96},{96,128},{128,160},{160,192},{192,224},{224... | collective-permute-start | bytes 442376 | tf_op jit(solution)/shard_map/ppermute | solution.py:333
  57.4 1.5 %collective-permute-start.7 = (f32[2,144,128]{2,1,0:T(8,128)S(1)}, f32[2,144,128]{2,1,0:T(8,128)S(1)}, u32[]{:S(2)}, u32[]{:S(2)}) collective-permute-start(f32[2,144,128]{2,1,0:T(8,128)S(1)} %bitcast.21), channel_id=1, source_target_pairs={{32,0},{64,32},{96,64},{128,96},{160,128},{192,160},{224,192},{256... | collective-permute-start | bytes 442376 | tf_op jit(solution)/shard_map/ppermute | solution.py:333
  58.9 2.8 %collective-permute-done.6 = f32[2,144,128]{2,1,0:T(8,128)S(1)} collective-permute-done((f32[2,144,128]{2,1,0:T(8,128)S(1)}, f32[2,144,128]{2,1,0:T(8,128)S(1)}, u32[]{:S(2)}, u32[]{:S(2)}) %collective-permute-start.6) | collective-permute-done | bytes 147488 | tf_op jit(solution)/shard_map/ppermute | solution.py:333
  61.8 3.4 %collective-permute-start.8 = (f32[16,2,128]{2,1,0:T(2,128)S(1)}, f32[16,2,128]{2,1,0:T(2,128)S(1)}, u32[]{:S(2)}, u32[]{:S(2)}) collective-permute-start(f32[16,2,128]{2,1,0:T(2,128)S(1)} %pad_maximum_fusion), channel_id=1, source_target_pairs={{0,1},{1,2},{2,3},{4,5},{5,6},{6,7},{8,9},{9,10},{10,11},{12,13},{... | collective-permute-start | bytes 49160 | tf_op jit(solution)/shard_map/ppermute | solution.py:329
  65.2 2.5 %collective-permute-start.9 = (f32[16,2,128]{2,1,0:T(2,128)S(1)}, f32[16,2,128]{2,1,0:T(2,128)S(1)}, u32[]{:S(2)}, u32[]{:S(2)}) collective-permute-start(f32[16,2,128]{2,1,0:T(2,128)S(1)} %pad_maximum_fusion.1), channel_id=1, source_target_pairs={{1,0},{2,1},{3,2},{5,4},{6,5},{7,6},{9,8},{10,9},{11,10},{13,12},{... | collective-permute-start | bytes 49160 | tf_op jit(solution)/shard_map/ppermute | solution.py:329
  67.6 0.6 shard_map.91.base_ref
  68.3 2.5 %collective-permute-done.9.zh_ref = f32[16,2,128]{2,1,0:T(2,128)S(1)} collective-permute-done((f32[16,2,128]{2,1,0:T(2,128)S(1)}, f32[16,2,128]{2,1,0:T(2,128)S(1)}, u32[]{:S(2)}, u32[]{:S(2)}) %collective-permute-start.9) | collective-permute-done | bytes 16416 | tf_op jit(solution)/shard_map/ppermute | solution.py:329
  71.2 3.2 %collective-permute-start.10 = (f32[4,16,2,128]{3,2,1,0:T(2,128)S(1)}, f32[4,16,2,128]{3,2,1,0:T(2,128)S(1)}, u32[]{:S(2)}, u32[]{:S(2)}) collective-permute-start(f32[4,16,2,128]{3,2,1,0:T(2,128)S(1)} %get-tuple-element.28), channel_id=1, source_target_pairs={{0,4},{4,8},{8,12},{12,16},{16,20},{20,24},{24,28},{1,5},{5,9},{9,... | collective-permute-start | bytes 196616 | tf_op jit(solution)/shard_map/ppermute | solution.py:329
  74.3 1.3 %collective-permute-start.11 = (f32[4,16,2,128]{3,2,1,0:T(2,128)S(1)}, f32[4,16,2,128]{3,2,1,0:T(2,128)S(1)}, u32[]{:S(2)}, u32[]{:S(2)}) collective-permute-start(f32[4,16,2,128]{3,2,1,0:T(2,128)S(1)} %get-tuple-element.29), channel_id=1, source_target_pairs={{4,0},{8,4},{12,8},{16,12},{20,16},{24,20},{28,24},{5,1},{9,5},{13... | collective-permute-start | bytes 196616 | tf_op jit(solution)/shard_map/ppermute | solution.py:329
  76.2 4.3 %collective-permute-done.11.above_ref = f32[4,16,2,128]{3,2,1,0:T(2,128)S(1)} collective-permute-done((f32[4,16,2,128]{3,2,1,0:T(2,128)S(1)}, f32[4,16,2,128]{3,2,1,0:T(2,128)S(1)}, u32[]{:S(2)}, u32[]{:S(2)}) %collective-permute-start.11) | collective-permute-done | bytes 65568 | tf_op jit(solution)/shard_map/ppermute | solution.py:329
  80.5 0.8 %shard_map.93 = f32[4,16,16,128]{3,2,1,0:T(8,128)} custom-call(f32[4,16,16,128]{3,2,1,0:T(8,128)S(1)} %get-tuple-element.27.rows_ref, f32[4,16,2,128]{3,2,1,0:T(2,128)S(1)} %collective-permute-done.10.below_ref, f32[4,16,2,128]{3,2,1,0:T(2,128)S(1)} %collective-permute-done.11.above_ref), custom_call_target="tpu_custom_call" | custom-call | tf_op jit(solution)/shard_map/pallas_call | solution.py:436
  (25 shorter events, 2.2 us)
Async XLA Ops:
  1.5 5.8 %collective-permute-start = (f32[4,2,16,128]{3,2,1,0:T(8,128)S(1)}, f32[4,2,16,128]{3,2,1,0:T(8,128)S(1)}, u32[]{:S(2)}, u32[]{:S(2)}) collective-permute-start(f32[4,2,16,128]{3,2,1,0:T(8,128)S(1)} %get-tuple-element.39), channel_id=1, source_target_pairs={{0,32},{32,64},{64,96},{96,128},{128,160},{160,192},{192,224},{224... | collective-permute-start | bytes 196616 | tf_op jit(solution)/shard_map/ppermute | solution.py:333
  1.5 5.8 %collective-permute-start.1 = (f32[4,2,16,128]{3,2,1,0:T(8,128)S(1)}, f32[4,2,16,128]{3,2,1,0:T(8,128)S(1)}, u32[]{:S(2)}, u32[]{:S(2)}) collective-permute-start(f32[4,2,16,128]{3,2,1,0:T(8,128)S(1)} %get-tuple-element.38), channel_id=1, source_target_pairs={{32,0},{64,32},{96,64},{128,96},{160,128},{192,160},{224,192},{256... | collective-permute-start | bytes 196616 | tf_op jit(solution)/shard_map/ppermute | solution.py:333
  4.5 20.9 %copy-start = (f32[4,16,16,128]{3,2,1,0:T(8,128)S(1)}, f32[4,16,16,128]{3,2,1,0:T(8,128)}, u32[]{:S(2)}) copy-start(f32[4,16,16,128]{3,2,1,0:T(8,128)} %gas_ref.5) | copy-start | bytes 1572868
  7.4 32.0 %copy-start.1 = (f32[128,128]{1,0:T(8,128)S(1)}, f32[128,128]{1,0:T(8,128)}, u32[]{:S(2)}) copy-start(f32[128,128]{1,0:T(8,128)} %param.12) | copy-start | bytes 196612
  7.4 41.2 %all-to-all-start = ((f32[128,1,1408]{2,1,0:T(1,128)}), f32[128,1,1408]{2,1,0:T(1,128)S(1)}, u32[]{:S(2)}, u32[]{:S(2)}) async-start(f32[128,1,1408]{2,1,0:T(1,128)} %bitcast.23), calls=%async_computation | async-start | bytes 1441792 | tf_op jit(solution)/shard_map/all_to_all | solution.py:399
  25.8 5.9 %collective-permute-start.2 = (f32[20,2,128]{2,1,0:T(2,128)S(1)}, f32[20,2,128]{2,1,0:T(2,128)S(1)}, u32[]{:S(2)}, u32[]{:S(2)}) collective-permute-start(f32[20,2,128]{2,1,0:T(2,128)S(1)} %get-tuple-element.19), channel_id=1, source_target_pairs={{0,1},{1,2},{2,3},{4,5},{5,6},{6,7},{8,9},{9,10},{10,11},{12,13},{... | collective-permute-start | bytes 61448 | tf_op jit(solution)/shard_map/ppermute | solution.py:329
  29.2 5.7 %collective-permute-start.3 = (f32[20,2,128]{2,1,0:T(2,128)S(1)}, f32[20,2,128]{2,1,0:T(2,128)S(1)}, u32[]{:S(2)}, u32[]{:S(2)}) collective-permute-start(f32[20,2,128]{2,1,0:T(2,128)S(1)} %get-tuple-element.20), channel_id=1, source_target_pairs={{1,0},{2,1},{3,2},{5,4},{6,5},{7,6},{9,8},{10,9},{11,10},{13,12},{... | collective-permute-start | bytes 61448 | tf_op jit(solution)/shard_map/ppermute | solution.py:329
  35.0 9.4 %collective-permute-start.4 = (f32[85,2,128]{2,1,0:T(2,128)S(1)}, f32[85,2,128]{2,1,0:T(2,128)S(1)}, u32[]{:S(2)}, u32[]{:S(2)}) collective-permute-start(f32[85,2,128]{2,1,0:T(2,128)S(1)} %get-tuple-element.21), channel_id=1, source_target_pairs={{0,4},{4,8},{8,12},{12,16},{16,20},{20,24},{24,28},{1,5},{5,9},{9,... | collective-permute-start | bytes 261128 | tf_op jit(solution)/shard_map/ppermute | solution.py:329
  38.1 8.4 %collective-permute-start.5 = (f32[85,2,128]{2,1,0:T(2,128)S(1)}, f32[85,2,128]{2,1,0:T(2,128)S(1)}, u32[]{:S(2)}, u32[]{:S(2)}) collective-permute-start(f32[85,2,128]{2,1,0:T(2,128)S(1)} %get-tuple-element.22), channel_id=1, source_target_pairs={{4,0},{8,4},{12,8},{16,12},{20,16},{24,20},{28,24},{5,1},{9,5},{13... | collective-permute-start | bytes 261128 | tf_op jit(solution)/shard_map/ppermute | solution.py:329
  55.9 5.8 %collective-permute-start.6 = (f32[2,144,128]{2,1,0:T(8,128)S(1)}, f32[2,144,128]{2,1,0:T(8,128)S(1)}, u32[]{:S(2)}, u32[]{:S(2)}) collective-permute-start(f32[2,144,128]{2,1,0:T(8,128)S(1)} %bitcast.22), channel_id=1, source_target_pairs={{0,32},{32,64},{64,96},{96,128},{128,160},{160,192},{192,224},{224... | collective-permute-start | bytes 442376 | tf_op jit(solution)/shard_map/ppermute | solution.py:333
  57.4 4.3 %collective-permute-start.7 = (f32[2,144,128]{2,1,0:T(8,128)S(1)}, f32[2,144,128]{2,1,0:T(8,128)S(1)}, u32[]{:S(2)}, u32[]{:S(2)}) collective-permute-start(f32[2,144,128]{2,1,0:T(8,128)S(1)} %bitcast.21), channel_id=1, source_target_pairs={{32,0},{64,32},{96,64},{128,96},{160,128},{192,160},{224,192},{256... | collective-permute-start | bytes 442376 | tf_op jit(solution)/shard_map/ppermute | solution.py:333
  61.8 6.5 %collective-permute-start.8 = (f32[16,2,128]{2,1,0:T(2,128)S(1)}, f32[16,2,128]{2,1,0:T(2,128)S(1)}, u32[]{:S(2)}, u32[]{:S(2)}) collective-permute-start(f32[16,2,128]{2,1,0:T(2,128)S(1)} %pad_maximum_fusion), channel_id=1, source_target_pairs={{0,1},{1,2},{2,3},{4,5},{5,6},{6,7},{8,9},{9,10},{10,11},{12,13},{... | collective-permute-start | bytes 49160 | tf_op jit(solution)/shard_map/ppermute | solution.py:329
  65.2 5.6 %collective-permute-start.9 = (f32[16,2,128]{2,1,0:T(2,128)S(1)}, f32[16,2,128]{2,1,0:T(2,128)S(1)}, u32[]{:S(2)}, u32[]{:S(2)}) collective-permute-start(f32[16,2,128]{2,1,0:T(2,128)S(1)} %pad_maximum_fusion.1), channel_id=1, source_target_pairs={{1,0},{2,1},{3,2},{5,4},{6,5},{7,6},{9,8},{10,9},{11,10},{13,12},{... | collective-permute-start | bytes 49160 | tf_op jit(solution)/shard_map/ppermute | solution.py:329
  71.2 5.1 %collective-permute-start.10 = (f32[4,16,2,128]{3,2,1,0:T(2,128)S(1)}, f32[4,16,2,128]{3,2,1,0:T(2,128)S(1)}, u32[]{:S(2)}, u32[]{:S(2)}) collective-permute-start(f32[4,16,2,128]{3,2,1,0:T(2,128)S(1)} %get-tuple-element.28), channel_id=1, source_target_pairs={{0,4},{4,8},{8,12},{12,16},{16,20},{20,24},{24,28},{1,5},{5,9},{9,... | collective-permute-start | bytes 196616 | tf_op jit(solution)/shard_map/ppermute | solution.py:329
  74.3 6.2 %collective-permute-start.11 = (f32[4,16,2,128]{3,2,1,0:T(2,128)S(1)}, f32[4,16,2,128]{3,2,1,0:T(2,128)S(1)}, u32[]{:S(2)}, u32[]{:S(2)}) collective-permute-start(f32[4,16,2,128]{3,2,1,0:T(2,128)S(1)} %get-tuple-element.29), channel_id=1, source_target_pairs={{4,0},{8,4},{12,8},{16,12},{20,16},{24,20},{28,24},{5,1},{9,5},{13... | collective-permute-start | bytes 196616 | tf_op jit(solution)/shard_map/ppermute | solution.py:329

commit v8 on v7

--- a/solution.py
+++ b/solution.py
@@ -156,7 +156,7 @@
 def parcel_kernel(
     recv_ref, pad, w_ref,
     pay_hbm, sum_ref, xlo_ref, xhi_ref,
-    code_v, code_s, acc, more, near, force, pay_ref, sem, pay_sem,
+    code_v, code_s, acc, more, near, force, ready, pay_ref, sem, pay_sem,
 ):
     planes = pad.shape[0] // ZR
     n = LANES
@@ -178,12 +178,34 @@
         hi = x.astype(BF16)
         return hi, (x - hi.astype(F32)).astype(BF16)
 
+    lane = iota((YS, n), 1)
+    for s in range(8):
+        rank, q0 = s // 4, (s % 4) * YS
+        row = q0 * ROWS + rank * 5
+
+        def take(k):
+            return recv_ref[pl.ds(row + k, YS, stride=ROWS), :]
+
+        alive = lane.astype(F32) < recv_ref[pl.ds(q0 * ROWS + 10, YS, stride=ROWS), :][:, 2 + rank : 3 + rank]
+        mass = jnp.where(alive, take(3), 0.0)
+        relax = jnp.where(alive, take(4), 1.0)
+        drag = TIME_STEP / relax
+        under = jnp.where(alive, 1.0 / (1.0 + drag), 0.0)
+        mine = slice(s * YS, (s + 1) * YS)
+        slots = pl.ds(2 * q0 + rank, YS, stride=2)
+        for k in range(3):
+            settle = TIME_STEP * SETTLING if k == 2 else 0.0
+            ready[k, mine, :] = (take(k) - settle) * under
+        ready[3, mine, :] = drag * under
+        ready[4, mine, :] = mass * drag
+        pay_ref[3, slots, :] = mass
+        pay_ref[4, slots, :] = jnp.where(alive, relax, 0.0)
+        force[s * n + 3 * YS : (s + 1) * n, :] = mass
     copy.wait()
 
     lane8 = iota((8, n), 1)
     group = (lane8 % YS) // 4
     quad = lane8 % 4
-    lane = iota((YS, n), 1)
 
     def place(s, b):
         c = code_s[s // 4, (s % 4) * YS + b]
@@ -219,28 +241,15 @@
         jnp.concatenate([near_hi, near_lo], axis=1), jnp.concatenate([w_hi, w_hi], axis=0), preferred_element_type=F32
     ) + jnp.dot(near_hi, w_lo, preferred_element_type=F32)
     for s in range(8):
-        rank, q0 = s // 4, (s % 4) * YS
-        row = q0 * ROWS + rank * 5
-
-        def take(k):
-            return recv_ref[pl.ds(row + k, YS, stride=ROWS), :]
-
-        head = recv_ref[pl.ds(q0 * ROWS + 10, YS, stride=ROWS), :]
-        alive = lane.astype(F32) < head[:, 2 + rank : 3 + rank]
-        mass = jnp.where(alive, take(3), 0.0)
-        relax = jnp.where(alive, take(4), 1.0)
-        drag = TIME_STEP / relax
-        under = 1.0 / (1.0 + drag)
-        slots = pl.ds(2 * q0 + rank, YS, stride=2)
+        slots = pl.ds(2 * (s % 4) * YS + s // 4, YS, stride=2)
+        mine = slice(s * YS, (s + 1) * YS)
+        share, push = ready[3, mine, :], ready[4, mine, :]
         for k in range(3):
-            gas = gas_all[s * n + k * YS : s * n + (k + 1) * YS]
-            settle = TIME_STEP * SETTLING if k == 2 else 0.0
-            vel = (take(k) + drag * gas - settle) * under
-            force[s * n + k * YS : s * n + (k + 1) * YS, :] = -(mass * drag * (gas - vel))
-            pay_ref[k, slots, :] = jnp.where(alive, vel, 0.0)
-        pay_ref[3, slots, :] = mass
-        pay_ref[4, slots, :] = jnp.where(alive, relax, 0.0)
-        force[s * n + 3 * YS : (s + 1) * n, :] = mass
+            rows = slice(s * n + k * YS, s * n + (k + 1) * YS)
+            gas = gas_all[rows]
+            vel = ready[k, mine, :] + share * gas
+            force[rows, :] = push * (vel - gas)
+            pay_ref[k, slots, :] = vel
     leave = pltpu.make_async_copy(pay_ref, pay_hbm, pay_sem)
     leave.start()
     across = (((1,), (1,)), ((), ()))
@@ -362,6 +371,7 @@
             pltpu.VMEM((rows, LANES), F32),
             pltpu.VMEM((8 * LANES, LANES), F32),
             pltpu.VMEM((8 * LANES, LANES), F32),
+            pltpu.VMEM((5, 2 * blocks, LANES), F32),
             pltpu.VMEM((5, 2 * blocks, LANES), F32),
             pltpu.SemaphoreType.DMA,
             pltpu.SemaphoreType.DMA,

time: 81.8 us -> 81.6 us (level)
  no operation moved by 1% of the time
where the time goes in v8:
time: 81.6 us; the launch traced here: 81.1 us
  starting transfers between devices  44.3 us (54%)
  waiting for transfers between devices  22 us (27%)
  Pallas kernels  12.8 us (16%)
  local copies, waits for them, and re-layouts  1 us (1%)
  between operations  0.9 us (1%)
    ppermute x8, starting transfers between devices, shift_pair(): return (lax.ppermute(to_high, axis, up), lax.ppermute(to_low, axis, down))  20.5 us
    all_to_all x1, starting transfers between devices, per_device(): lax.all_to_all(send.reshape(blocks, ROWS * LANES), ('gx', 'gy'), split_ax...  17.9 us
    ppermute x8, waiting for transfers between devices, shift_pair(): return (lax.ppermute(to_high, axis, up), lax.ppermute(to_low, axis, down))  17.6 us
    pallas_call x1, Pallas kernels, parcels(): call(parcel_kernel, [arr(5, 2 * blocks, LANES), arr(nx * ZR, LANES), arr(...  7.09 us
    ppermute x2, starting transfers between devices, shift_pair(): lax.ppermute(to_low, axis, down)  4.43 us
    pallas_call x1, Pallas kernels, per_device(): call(pack_kernel, arr(blocks * ROWS, LANES), [pltpu.VMEM((1, blocks), jnp...  2.83 us
    ppermute x2, waiting for transfers between devices, shift_pair(): lax.ppermute(to_high, axis, up)  2.81 us
    all_to_all x1, waiting for transfers between devices, per_device(): lax.all_to_all(send.reshape(blocks, ROWS * LANES), ('gx', 'gy'), split_ax...  1.66 us
  transfers between devices with their start and end apart: 13, of which 8 were waited for; matrix products, arithmetic and copies ran while one was open for 0% of the time, Pallas kernels for 6%

profile of v8, /device:TPU:2, one launch (start us, length us, event | category | flops | bytes accessed | tf_op | source)
XLA Modules:
  0.0 81.1 jit_solution(8430410335810235475)
XLA Ops:
  0.6 0.9 %fusion.1 = (f32[4,2,16,128]{3,2,1,0:T(8,128)S(1)}, f32[4,2,16,128]{3,2,1,0:T(8,128)S(1)}) fusion(f32[4,16,16,128]{3,2,1,0:T(8,128)} %gas_ref.5), kind=kLoop, calls=%fused_computation.11 | loop fusion | bytes 262144 | tf_op jit(solution)/shard_map/slice | solution.py:386
  1.5 2.9 %collective-permute-start.1 = (f32[4,2,16,128]{3,2,1,0:T(8,128)S(1)}, f32[4,2,16,128]{3,2,1,0:T(8,128)S(1)}, u32[]{:S(2)}, u32[]{:S(2)}) collective-permute-start(f32[4,2,16,128]{3,2,1,0:T(8,128)S(1)} %get-tuple-element.38), channel_id=1, source_target_pairs={{32,0},{64,32},{96,64},{128,96},{160,128},{192,160},{224,192},{256... | collective-permute-start | bytes 196616 | tf_op jit(solution)/shard_map/ppermute | solution.py:342
  4.5 2.8 %shard_map.86 = f32[1408,128]{1,0:T(8,128)} custom-call(s32[1,128]{1,0:T(1,128)} %bitcast.26, s32[1,128]{1,0:T(1,128)} %bitcast.27, s32[1,128]{1,0:T(1,128)} %bitcast.28, f32[3,128,128]{2,1,0:T(8,128)} %bitcast.25, f32[128,2,128]{2,1,0:T(2,128)} %prop_hbm.1), custom_call_target="tpu_custom_call" | custom-call | tf_op jit(solution)/shard_map/pallas_call | solution.py:387
  7.4 17.9 %all-to-all-start = ((f32[128,1,1408]{2,1,0:T(1,128)}), f32[128,1,1408]{2,1,0:T(1,128)S(1)}, u32[]{:S(2)}, u32[]{:S(2)}) async-start(f32[128,1,1408]{2,1,0:T(1,128)} %bitcast.23), calls=%async_computation | async-start | bytes 1441792 | tf_op jit(solution)/shard_map/all_to_all | solution.py:409
  25.8 3.4 %collective-permute-start.2 = (f32[20,2,128]{2,1,0:T(2,128)S(1)}, f32[20,2,128]{2,1,0:T(2,128)S(1)}, u32[]{:S(2)}, u32[]{:S(2)}) collective-permute-start(f32[20,2,128]{2,1,0:T(2,128)S(1)} %get-tuple-element.19), channel_id=1, source_target_pairs={{0,1},{1,2},{2,3},{4,5},{5,6},{6,7},{8,9},{9,10},{10,11},{12,13},{... | collective-permute-start | bytes 61448 | tf_op jit(solution)/shard_map/ppermute | solution.py:338
  29.2 2.4 %collective-permute-start.3 = (f32[20,2,128]{2,1,0:T(2,128)S(1)}, f32[20,2,128]{2,1,0:T(2,128)S(1)}, u32[]{:S(2)}, u32[]{:S(2)}) collective-permute-start(f32[20,2,128]{2,1,0:T(2,128)S(1)} %get-tuple-element.20), channel_id=1, source_target_pairs={{1,0},{2,1},{3,2},{5,4},{6,5},{7,6},{9,8},{10,9},{11,10},{13,12},{... | collective-permute-start | bytes 61448 | tf_op jit(solution)/shard_map/ppermute | solution.py:338
  31.7 3.2 %collective-permute-done.3.zh_ref = f32[20,2,128]{2,1,0:T(2,128)S(1)} collective-permute-done((f32[20,2,128]{2,1,0:T(2,128)S(1)}, f32[20,2,128]{2,1,0:T(2,128)S(1)}, u32[]{:S(2)}, u32[]{:S(2)}) %collective-permute-start.3) | collective-permute-done | bytes 20512 | tf_op jit(solution)/shard_map/ppermute | solution.py:338
  35.0 3.0 %collective-permute-start.4 = (f32[85,2,128]{2,1,0:T(2,128)S(1)}, f32[85,2,128]{2,1,0:T(2,128)S(1)}, u32[]{:S(2)}, u32[]{:S(2)}) collective-permute-start(f32[85,2,128]{2,1,0:T(2,128)S(1)} %get-tuple-element.21), channel_id=1, source_target_pairs={{0,4},{4,8},{8,12},{12,16},{16,20},{20,24},{24,28},{1,5},{5,9},{9,... | collective-permute-start | bytes 261128 | tf_op jit(solution)/shard_map/ppermute | solution.py:338
  38.1 1.3 %collective-permute-start.5 = (f32[85,2,128]{2,1,0:T(2,128)S(1)}, f32[85,2,128]{2,1,0:T(2,128)S(1)}, u32[]{:S(2)}, u32[]{:S(2)}) collective-permute-start(f32[85,2,128]{2,1,0:T(2,128)S(1)} %get-tuple-element.22), channel_id=1, source_target_pairs={{4,0},{8,4},{12,8},{16,12},{20,16},{24,20},{28,24},{5,1},{9,5},{13... | collective-permute-start | bytes 261128 | tf_op jit(solution)/shard_map/ppermute | solution.py:338
  39.5 4.9 %collective-permute-done.4.yl_ref = f32[85,2,128]{2,1,0:T(2,128)S(1)} collective-permute-done((f32[85,2,128]{2,1,0:T(2,128)S(1)}, f32[85,2,128]{2,1,0:T(2,128)S(1)}, u32[]{:S(2)}, u32[]{:S(2)}) %collective-permute-start.4) | collective-permute-done | bytes 87072 | tf_op jit(solution)/shard_map/ppermute | solution.py:338
  44.4 2.0 %collective-permute-done.5.yh_ref = f32[85,2,128]{2,1,0:T(2,128)S(1)} collective-permute-done((f32[85,2,128]{2,1,0:T(2,128)S(1)}, f32[85,2,128]{2,1,0:T(2,128)S(1)}, u32[]{:S(2)}, u32[]{:S(2)}) %collective-permute-start.5) | collective-permute-done | bytes 87072 | tf_op jit(solution)/shard_map/ppermute | solution.py:338
  46.9 1.7 %all-to-all-done = f32[128,1,1408]{2,1,0:T(1,128)S(1)} async-done(((f32[128,1,1408]{2,1,0:T(1,128)}), f32[128,1,1408]{2,1,0:T(1,128)S(1)}, u32[]{:S(2)}, u32[]{:S(2)}) %all-to-all-start) | async-done | bytes 720928 | tf_op jit(solution)/shard_map/all_to_all | solution.py:409
  48.6 7.1 %shard_map.90 = (f32[5,256,128]{2,1,0:T(8,128)}, f32[2304,128]{1,0:T(8,128)S(1)}, f32[288,128]{1,0:T(8,128)S(1)}, f32[288,128]{1,0:T(8,128)S(1)}) custom-call(f32[1408,128]{1,0:T(8,128)S(1)} %bitcast.16, f32[2880,128]{1,0:T(8,128)S(1)} %bitcast.15, f32[128,128]{1,0:T(8,128)S(1)} %bitcast.20), custom_call_target="tpu_custom_call" | custom-call | tf_op jit(solution)/shard_map/pallas_call | solution.py:364
  55.7 1.5 %collective-permute-start.6 = (f32[2,144,128]{2,1,0:T(8,128)S(1)}, f32[2,144,128]{2,1,0:T(8,128)S(1)}, u32[]{:S(2)}, u32[]{:S(2)}) collective-permute-start(f32[2,144,128]{2,1,0:T(8,128)S(1)} %bitcast.22), channel_id=1, source_target_pairs={{0,32},{32,64},{64,96},{96,128},{128,160},{160,192},{192,224},{224... | collective-permute-start | bytes 442376 | tf_op jit(solution)/shard_map/ppermute | solution.py:342
  57.2 1.5 %collective-permute-start.7 = (f32[2,144,128]{2,1,0:T(8,128)S(1)}, f32[2,144,128]{2,1,0:T(8,128)S(1)}, u32[]{:S(2)}, u32[]{:S(2)}) collective-permute-start(f32[2,144,128]{2,1,0:T(8,128)S(1)} %bitcast.21), channel_id=1, source_target_pairs={{32,0},{64,32},{96,64},{128,96},{160,128},{192,160},{224,192},{256... | collective-permute-start | bytes 442376 | tf_op jit(solution)/shard_map/ppermute | solution.py:342
  58.7 2.8 %collective-permute-done.6 = f32[2,144,128]{2,1,0:T(8,128)S(1)} collective-permute-done((f32[2,144,128]{2,1,0:T(8,128)S(1)}, f32[2,144,128]{2,1,0:T(8,128)S(1)}, u32[]{:S(2)}, u32[]{:S(2)}) %collective-permute-start.6) | collective-permute-done | bytes 147488 | tf_op jit(solution)/shard_map/ppermute | solution.py:342
  61.6 3.4 %collective-permute-start.8 = (f32[16,2,128]{2,1,0:T(2,128)S(1)}, f32[16,2,128]{2,1,0:T(2,128)S(1)}, u32[]{:S(2)}, u32[]{:S(2)}) collective-permute-start(f32[16,2,128]{2,1,0:T(2,128)S(1)} %pad_maximum_fusion), channel_id=1, source_target_pairs={{0,1},{1,2},{2,3},{4,5},{5,6},{6,7},{8,9},{9,10},{10,11},{12,13},{... | collective-permute-start | bytes 49160 | tf_op jit(solution)/shard_map/ppermute | solution.py:338
  65.0 2.5 %collective-permute-start.9 = (f32[16,2,128]{2,1,0:T(2,128)S(1)}, f32[16,2,128]{2,1,0:T(2,128)S(1)}, u32[]{:S(2)}, u32[]{:S(2)}) collective-permute-start(f32[16,2,128]{2,1,0:T(2,128)S(1)} %pad_maximum_fusion.1), channel_id=1, source_target_pairs={{1,0},{2,1},{3,2},{5,4},{6,5},{7,6},{9,8},{10,9},{11,10},{13,12},{... | collective-permute-start | bytes 49160 | tf_op jit(solution)/shard_map/ppermute | solution.py:338
  67.4 0.6 shard_map.91.base_ref
  68.1 2.5 %collective-permute-done.9.zh_ref = f32[16,2,128]{2,1,0:T(2,128)S(1)} collective-permute-done((f32[16,2,128]{2,1,0:T(2,128)S(1)}, f32[16,2,128]{2,1,0:T(2,128)S(1)}, u32[]{:S(2)}, u32[]{:S(2)}) %collective-permute-start.9) | collective-permute-done | bytes 16416 | tf_op jit(solution)/shard_map/ppermute | solution.py:338
  71.0 3.2 %collective-permute-start.10 = (f32[4,16,2,128]{3,2,1,0:T(2,128)S(1)}, f32[4,16,2,128]{3,2,1,0:T(2,128)S(1)}, u32[]{:S(2)}, u32[]{:S(2)}) collective-permute-start(f32[4,16,2,128]{3,2,1,0:T(2,128)S(1)} %get-tuple-element.28), channel_id=1, source_target_pairs={{0,4},{4,8},{8,12},{12,16},{16,20},{20,24},{24,28},{1,5},{5,9},{9,... | collective-permute-start | bytes 196616 | tf_op jit(solution)/shard_map/ppermute | solution.py:338
  74.1 1.3 %collective-permute-start.11 = (f32[4,16,2,128]{3,2,1,0:T(2,128)S(1)}, f32[4,16,2,128]{3,2,1,0:T(2,128)S(1)}, u32[]{:S(2)}, u32[]{:S(2)}) collective-permute-start(f32[4,16,2,128]{3,2,1,0:T(2,128)S(1)} %get-tuple-element.29), channel_id=1, source_target_pairs={{4,0},{8,4},{12,8},{16,12},{20,16},{24,20},{28,24},{5,1},{9,5},{13... | collective-permute-start | bytes 196616 | tf_op jit(solution)/shard_map/ppermute | solution.py:338
  76.0 4.3 %collective-permute-done.11.above_ref = f32[4,16,2,128]{3,2,1,0:T(2,128)S(1)} collective-permute-done((f32[4,16,2,128]{3,2,1,0:T(2,128)S(1)}, f32[4,16,2,128]{3,2,1,0:T(2,128)S(1)}, u32[]{:S(2)}, u32[]{:S(2)}) %collective-permute-start.11) | collective-permute-done | bytes 65568 | tf_op jit(solution)/shard_map/ppermute | solution.py:338
  80.3 0.8 %shard_map.93 = f32[4,16,16,128]{3,2,1,0:T(8,128)} custom-call(f32[4,16,16,128]{3,2,1,0:T(8,128)S(1)} %get-tuple-element.27.rows_ref, f32[4,16,2,128]{3,2,1,0:T(2,128)S(1)} %collective-permute-done.10.below_ref, f32[4,16,2,128]{3,2,1,0:T(2,128)S(1)} %collective-permute-done.11.above_ref), custom_call_target="tpu_custom_call" | custom-call | tf_op jit(solution)/shard_map/pallas_call | solution.py:446
  (25 shorter events, 2.2 us)
Async XLA Ops:
  1.5 5.8 %collective-permute-start = (f32[4,2,16,128]{3,2,1,0:T(8,128)S(1)}, f32[4,2,16,128]{3,2,1,0:T(8,128)S(1)}, u32[]{:S(2)}, u32[]{:S(2)}) collective-permute-start(f32[4,2,16,128]{3,2,1,0:T(8,128)S(1)} %get-tuple-element.39), channel_id=1, source_target_pairs={{0,32},{32,64},{64,96},{96,128},{128,160},{160,192},{192,224},{224... | collective-permute-start | bytes 196616 | tf_op jit(solution)/shard_map/ppermute | solution.py:342
  1.5 5.8 %collective-permute-start.1 = (f32[4,2,16,128]{3,2,1,0:T(8,128)S(1)}, f32[4,2,16,128]{3,2,1,0:T(8,128)S(1)}, u32[]{:S(2)}, u32[]{:S(2)}) collective-permute-start(f32[4,2,16,128]{3,2,1,0:T(8,128)S(1)} %get-tuple-element.38), channel_id=1, source_target_pairs={{32,0},{64,32},{96,64},{128,96},{160,128},{192,160},{224,192},{256... | collective-permute-start | bytes 196616 | tf_op jit(solution)/shard_map/ppermute | solution.py:342
  4.5 20.9 %copy-start = (f32[4,16,16,128]{3,2,1,0:T(8,128)S(1)}, f32[4,16,16,128]{3,2,1,0:T(8,128)}, u32[]{:S(2)}) copy-start(f32[4,16,16,128]{3,2,1,0:T(8,128)} %gas_ref.5) | copy-start | bytes 1572868
  7.4 32.0 %copy-start.1 = (f32[128,128]{1,0:T(8,128)S(1)}, f32[128,128]{1,0:T(8,128)}, u32[]{:S(2)}) copy-start(f32[128,128]{1,0:T(8,128)} %param.12) | copy-start | bytes 196612
  7.4 41.2 %all-to-all-start = ((f32[128,1,1408]{2,1,0:T(1,128)}), f32[128,1,1408]{2,1,0:T(1,128)S(1)}, u32[]{:S(2)}, u32[]{:S(2)}) async-start(f32[128,1,1408]{2,1,0:T(1,128)} %bitcast.23), calls=%async_computation | async-start | bytes 1441792 | tf_op jit(solution)/shard_map/all_to_all | solution.py:409
  25.8 5.9 %collective-permute-start.2 = (f32[20,2,128]{2,1,0:T(2,128)S(1)}, f32[20,2,128]{2,1,0:T(2,128)S(1)}, u32[]{:S(2)}, u32[]{:S(2)}) collective-permute-start(f32[20,2,128]{2,1,0:T(2,128)S(1)} %get-tuple-element.19), channel_id=1, source_target_pairs={{0,1},{1,2},{2,3},{4,5},{5,6},{6,7},{8,9},{9,10},{10,11},{12,13},{... | collective-permute-start | bytes 61448 | tf_op jit(solution)/shard_map/ppermute | solution.py:338
  29.2 5.7 %collective-permute-start.3 = (f32[20,2,128]{2,1,0:T(2,128)S(1)}, f32[20,2,128]{2,1,0:T(2,128)S(1)}, u32[]{:S(2)}, u32[]{:S(2)}) collective-permute-start(f32[20,2,128]{2,1,0:T(2,128)S(1)} %get-tuple-element.20), channel_id=1, source_target_pairs={{1,0},{2,1},{3,2},{5,4},{6,5},{7,6},{9,8},{10,9},{11,10},{13,12},{... | collective-permute-start | bytes 61448 | tf_op jit(solution)/shard_map/ppermute | solution.py:338
  35.0 9.4 %collective-permute-start.4 = (f32[85,2,128]{2,1,0:T(2,128)S(1)}, f32[85,2,128]{2,1,0:T(2,128)S(1)}, u32[]{:S(2)}, u32[]{:S(2)}) collective-permute-start(f32[85,2,128]{2,1,0:T(2,128)S(1)} %get-tuple-element.21), channel_id=1, source_target_pairs={{0,4},{4,8},{8,12},{12,16},{16,20},{20,24},{24,28},{1,5},{5,9},{9,... | collective-permute-start | bytes 261128 | tf_op jit(solution)/shard_map/ppermute | solution.py:338
  38.1 8.4 %collective-permute-start.5 = (f32[85,2,128]{2,1,0:T(2,128)S(1)}, f32[85,2,128]{2,1,0:T(2,128)S(1)}, u32[]{:S(2)}, u32[]{:S(2)}) collective-permute-start(f32[85,2,128]{2,1,0:T(2,128)S(1)} %get-tuple-element.22), channel_id=1, source_target_pairs={{4,0},{8,4},{12,8},{16,12},{20,16},{24,20},{28,24},{5,1},{9,5},{13... | collective-permute-start | bytes 261128 | tf_op jit(solution)/shard_map/ppermute | solution.py:338
  55.7 5.8 %collective-permute-start.6 = (f32[2,144,128]{2,1,0:T(8,128)S(1)}, f32[2,144,128]{2,1,0:T(8,128)S(1)}, u32[]{:S(2)}, u32[]{:S(2)}) collective-permute-start(f32[2,144,128]{2,1,0:T(8,128)S(1)} %bitcast.22), channel_id=1, source_target_pairs={{0,32},{32,64},{64,96},{96,128},{128,160},{160,192},{192,224},{224... | collective-permute-start | bytes 442376 | tf_op jit(solution)/shard_map/ppermute | solution.py:342
  57.2 4.3 %collective-permute-start.7 = (f32[2,144,128]{2,1,0:T(8,128)S(1)}, f32[2,144,128]{2,1,0:T(8,128)S(1)}, u32[]{:S(2)}, u32[]{:S(2)}) collective-permute-start(f32[2,144,128]{2,1,0:T(8,128)S(1)} %bitcast.21), channel_id=1, source_target_pairs={{32,0},{64,32},{96,64},{128,96},{160,128},{192,160},{224,192},{256... | collective-permute-start | bytes 442376 | tf_op jit(solution)/shard_map/ppermute | solution.py:342
  61.6 6.5 %collective-permute-start.8 = (f32[16,2,128]{2,1,0:T(2,128)S(1)}, f32[16,2,128]{2,1,0:T(2,128)S(1)}, u32[]{:S(2)}, u32[]{:S(2)}) collective-permute-start(f32[16,2,128]{2,1,0:T(2,128)S(1)} %pad_maximum_fusion), channel_id=1, source_target_pairs={{0,1},{1,2},{2,3},{4,5},{5,6},{6,7},{8,9},{9,10},{10,11},{12,13},{... | collective-permute-start | bytes 49160 | tf_op jit(solution)/shard_map/ppermute | solution.py:338
  65.0 5.6 %collective-permute-start.9 = (f32[16,2,128]{2,1,0:T(2,128)S(1)}, f32[16,2,128]{2,1,0:T(2,128)S(1)}, u32[]{:S(2)}, u32[]{:S(2)}) collective-permute-start(f32[16,2,128]{2,1,0:T(2,128)S(1)} %pad_maximum_fusion.1), channel_id=1, source_target_pairs={{1,0},{2,1},{3,2},{5,4},{6,5},{7,6},{9,8},{10,9},{11,10},{13,12},{... | collective-permute-start | bytes 49160 | tf_op jit(solution)/shard_map/ppermute | solution.py:338
  71.0 5.0 %collective-permute-start.10 = (f32[4,16,2,128]{3,2,1,0:T(2,128)S(1)}, f32[4,16,2,128]{3,2,1,0:T(2,128)S(1)}, u32[]{:S(2)}, u32[]{:S(2)}) collective-permute-start(f32[4,16,2,128]{3,2,1,0:T(2,128)S(1)} %get-tuple-element.28), channel_id=1, source_target_pairs={{0,4},{4,8},{8,12},{12,16},{16,20},{20,24},{24,28},{1,5},{5,9},{9,... | collective-permute-start | bytes 196616 | tf_op jit(solution)/shard_map/ppermute | solution.py:338
  74.1 6.2 %collective-permute-start.11 = (f32[4,16,2,128]{3,2,1,0:T(2,128)S(1)}, f32[4,16,2,128]{3,2,1,0:T(2,128)S(1)}, u32[]{:S(2)}, u32[]{:S(2)}) collective-permute-start(f32[4,16,2,128]{3,2,1,0:T(2,128)S(1)} %get-tuple-element.29), channel_id=1, source_target_pairs={{4,0},{8,4},{12,8},{16,12},{20,16},{24,20},{28,24},{5,1},{9,5},{13... | collective-permute-start | bytes 196616 | tf_op jit(solution)/shard_map/ppermute | solution.py:338
